TPU v7x, 128 devices: a whole 4x4x4 slice. The times are simulated.
128 devices in a mesh: leaf: 32 (over x, y, core), front: 4 (over z).
Axes of the slice: x: 4, y: 4, z: 4, core: 2. Of those that a mesh axis runs over, the one named last changes fastest.
Arguments:
- load_leaf: float32 [128, 196608], P(None, ('leaf', 'front')), may hold values from -6 to 6
- leaf_inverse: float32 [1536, 128, 128], P(('leaf', 'front')), may hold values from -1 to 1
- leaf_coupling: float32 [1536, 8, 128, 128], P(('leaf', 'front')), may hold values from -0.0625 to 0.0625
- leaf_pattern: int32 [1536, 8], P(('leaf', 'front')), may hold values from 0 to 61, all different within a row
- load_sep: float32 [128, 20480], P('front', 'leaf'), may hold values from -6 to 6
- sep_inverse: float32 [160, 128, 128], P('leaf'), may hold values from -1 to 1
- sep_coupling: float32 [6272, 128, 128], P('leaf'), may hold values from -0.09375 to 0.09375
Outputs:
- solution_leaf: float32 [128, 196608], P(None, ('leaf', 'front'))
- solution_sep: float32 [128, 20480], P('front', 'leaf')
Inputs may be any that keep to these rules, and one draw needn't show every extreme that they name: `leaf_pattern`: the 8 entries of a row are different ancestor indices; every index 0 to 61 occurs in some row.
All inputs are finite; a program needn't handle non-finite values.
Results may differ from a plain program's by a relative error of at most 0.00011.
Values sent between devices are 32-bit elements; how exact they have to be, the bound alone decides.
No kernel may reach another device: no remote copies, remote signals or barrier semaphores. Data moves between devices by JAX's collectives and lax.ppermute only.
A program may use at most 128 MiB of HBM per device.

v0:
```python
import jax
import jax.numpy as jnp
from jax import lax
from jax.sharding import PartitionSpec as P


def from_partner_2(shard, axis, bit):
    return lax.ppermute(shard, axis, [(i, i ^ 1 << bit) for i in range(lax.axis_size(axis))])


def offsets_table(level_count):
    table_map = {}
    position = 0
    for upper_level in range(2, level_count + 1):
        for lower_level in range(1, upper_level):
            table_map[upper_level, lower_level] = position
            position = position + 2**upper_level
    return table_map


def from_partner(values, bit_index):
    return from_partner_2(values, "leaf", bit_index)


def halve_blocks(buffer, leaf_id, level_count, block_size):
    columns = buffer.shape[0]
    portions = []
    for level_index in range(1, level_count + 1):
        first_row = (2**level_index - 2) * block_size
        last_row = (2 ** (level_index + 1) - 2) * block_size
        portions.append(buffer[:, first_row:last_row].reshape(columns, 2**level_index, block_size))
    for bit_index in range(level_count):
        my_bit = leaf_id >> bit_index & 1
        kept = []
        outgoing = []
        for level_index in range(bit_index + 1, level_count + 1):
            current = portions[level_index - 1]
            paired = current.reshape(columns, current.shape[1] // 2, 2, block_size)
            even_blocks = paired[:, :, 0]
            odd_blocks = paired[:, :, 1]
            kept.append(jnp.where(my_bit == 1, odd_blocks, even_blocks))
            outgoing.append(jnp.where(my_bit == 1, even_blocks, odd_blocks))
        incoming = from_partner(jnp.concatenate(outgoing, axis=1), bit_index)
        position = 0
        for offset_index, level_index in enumerate(range(bit_index + 1, level_count + 1)):
            count_blocks = kept[offset_index].shape[1]
            portions[level_index - 1] = (
                kept[offset_index] + incoming[:, position : position + count_blocks]
            )
            position = position + count_blocks
    return jnp.concatenate(portions, axis=1)


def expand_blocks(portions, leaf_id, bit_index):
    my_bit = leaf_id >> bit_index & 1
    active = portions[bit_index:]
    incoming = from_partner(jnp.concatenate(active, axis=1), bit_index)
    widened = []
    position = 0
    for current in active:
        count_blocks = current.shape[1]
        theirs = incoming[:, position : position + count_blocks]
        position = position + count_blocks
        lower_first = jnp.stack([current, theirs], axis=2)
        upper_first = jnp.stack([theirs, current], axis=2)
        merged = jnp.where(my_bit == 0, lower_first, upper_first)
        widened.append(merged.reshape(current.shape[0], 2 * count_blocks, current.shape[2]))
    return portions[:bit_index] + widened


def local(
    load_leaf, leaf_inverse, leaf_coupling, leaf_pattern, load_sep, sep_inverse, sep_coupling
):
    highest = lax.Precision.HIGHEST
    all_columns = load_leaf.shape[0]
    leaf_blocks = leaf_pattern.shape[0]
    block_size = leaf_inverse.shape[-1]
    leaf_count = lax.axis_size("leaf")
    level_count = leaf_count.bit_length() - 1
    ancestor_blocks = 2 ** (level_count + 1) - 2
    columns = load_sep.shape[0]
    leaf_id = lax.axis_index("leaf")
    table_map = offsets_table(level_count)
    leaf_solved = jnp.einsum(
        "rbi,bji->rbj",
        load_leaf.reshape(all_columns, leaf_blocks, block_size),
        leaf_inverse,
        precision=highest,
    )
    selector = (
        leaf_pattern[:, :, None] == jnp.arange(ancestor_blocks, dtype=jnp.int32)[None, None, :]
    ).astype(jnp.float32)
    products = jnp.einsum("rbi,bqoi->rbqo", leaf_solved, leaf_coupling, precision=highest)
    gathered_terms = jnp.einsum("rbqo,bqa->rao", products, selector, precision=highest)
    reduced = lax.psum_scatter(
        gathered_terms.reshape(lax.axis_size("front") * columns, ancestor_blocks * block_size),
        "front",
        scatter_dimension=0,
        tiled=True,
    )
    level_updates = halve_blocks(reduced, leaf_id, level_count, block_size)
    sep_rhs = load_sep.reshape(columns, level_count, block_size)
    gathered = []
    own_solved = []
    for upper_level in range(1, level_count + 1):
        span_blocks = 2**upper_level
        group_start = (leaf_id >> upper_level) * span_blocks
        summed = level_updates[:, upper_level - 1]
        for lower_level in range(1, upper_level):
            position = table_map[upper_level, lower_level]
            group_rows = lax.dynamic_slice_in_dim(
                gathered[lower_level - 1], group_start, span_blocks, 1
            )
            summed = summed + jnp.einsum(
                "rmi,moi->ro",
                group_rows,
                sep_coupling[position : position + span_blocks],
                precision=highest,
            )
        solved = jnp.einsum(
            "ri,ji->rj",
            sep_rhs[:, upper_level - 1] - summed,
            sep_inverse[upper_level - 1],
            precision=highest,
        )
        own_solved.append(solved)
        if upper_level < level_count:
            gathered.append(
                lax.all_gather(solved, "leaf", axis=1, tiled=True).reshape(
                    columns, leaf_count, block_size
                )
            )
    own_final = [None] * level_count
    portions = [None] * level_count
    for upper_level in range(level_count, 0, -1):
        residual = own_solved[upper_level - 1]
        if upper_level < level_count:
            buffer = jnp.zeros((columns, leaf_count, block_size), jnp.float32)
            for higher_level in range(upper_level + 1, level_count + 1):
                span_blocks = 2**higher_level
                group_start = (leaf_id >> higher_level) * span_blocks
                position = table_map[higher_level, upper_level]
                spread = jnp.einsum(
                    "ro,moi->rmi",
                    own_final[higher_level - 1],
                    sep_coupling[position : position + span_blocks],
                    precision=highest,
                )
                existing = lax.dynamic_slice_in_dim(buffer, group_start, span_blocks, 1)
                buffer = lax.dynamic_update_slice_in_dim(buffer, existing + spread, group_start, 1)
            residual = residual - lax.psum_scatter(
                buffer.reshape(columns, leaf_count * block_size),
                "leaf",
                scatter_dimension=1,
                tiled=True,
            )
        final = jnp.einsum("ro,oi->ri", residual, sep_inverse[upper_level - 1], precision=highest)
        own_final[upper_level - 1] = final
        portions[upper_level - 1] = final[:, None, :]
        portions = expand_blocks(portions, leaf_id, upper_level - 1)
    solution_sep = jnp.stack(own_final, axis=1).reshape(columns, level_count * block_size)
    ancestors = jnp.concatenate(portions, axis=1).reshape(columns, ancestor_blocks * block_size)
    ancestors = lax.all_gather(ancestors, "front", axis=0, tiled=True).reshape(
        all_columns, ancestor_blocks, block_size
    )
    picked = jnp.einsum("rao,bqa->rbqo", ancestors, selector, precision=highest)
    carried = jnp.einsum("rbqo,bqoi->rbi", picked, leaf_coupling, precision=highest)
    solution_leaf = jnp.einsum(
        "rbo,boi->rbi", leaf_solved - carried, leaf_inverse, precision=highest
    )
    return (solution_leaf.reshape(all_columns, leaf_blocks * block_size), solution_sep)


def solution(mesh):
    return jax.shard_map(
        local,
        mesh=mesh,
        in_specs=(
            P(None, ("leaf", "front")),
            P(("leaf", "front"), None, None),
            P(("leaf", "front"), None, None, None),
            P(("leaf", "front"), None),
            P("front", "leaf"),
            P("leaf", None, None),
            P("leaf", None, None),
        ),
        out_specs=(P(None, ("leaf", "front")), P("front", "leaf")),
        check_vma=False,
    )
```

profile of v0, /device:TPU:1, one launch (start us, length us, event | category | flops | bytes accessed | tf_op | source)
XLA Modules:
  0.0 665.9 jit_solution(17174565691540910829)
XLA Ops:
  10.5 7.6 %convolution_bitcast_fusion = f32[128,12,8,128]{3,0,2,1:T(8,128)S(1)} fusion(f32[12,8,128,128]{3,2,1,0:T(8,128)} %param.9, f32[12,128,128]{2,1,0:T(8,128)S(1)} %fusion.196), kind=kOutput, calls=%fused_computation.7 | convolution fusion | flops 2415919104 | bytes 13369344 | tf_op jit(solution)/shard_map/rbi,bqoi->rbqo/dot_general | solution.py:93
  18.1 11.9 %fusion.9 = f32[128,62,128]{2,1,0:T(8,128)} fusion(f32[128,12,8,128]{3,0,2,1:T(8,128)S(1)} %convolution_bitcast_fusion, s32[12,8]{0,1:T(8,128)S(1)} %copy-done.6), kind=kOutput, calls=%fused_computation.8 | convolution fusion | flops 1170216704 | bytes 10355072 | tf_op jit(solution)/shard_map/rbqo,bqa->rao/dot_general | solution.py:94
  30.0 5.5 copy.218
  35.5 5.6 copy.307
  41.3 49.2 %reduce-scatter.16.cloned.1.call-done = f32[32,7936]{1,0:T(8,128)} async-done(((f32[128,7936]{1,0:T(8,128)}), f32[32,7936]{1,0:T(8,128)}) %reduce-scatter.16.cloned.1.call-update) | async-done | bytes 1015824
  112.6 26.3 %all_gather.15 = f32[32,4096]{1,0:T(8,128)S(1)} all-gather(f32[32,128]{1,0:T(8,128)S(1)} %fusion.102), channel_id=1, replica_groups=mesh['leaf'=32,'front'=4] {'leaf'}, dimensions={1}, use_global_device_ids=true | all-gather | bytes 540672 | tf_op jit(solution)/shard_map/all_gather | solution.py:129
  139.0 2.4 convolution_bitcast_fusion.4
  144.3 3.7 fusion.53
  148.3 23.9 %all_gather.16 = f32[32,4096]{1,0:T(8,128)S(1)} all-gather(f32[32,128]{1,0:T(8,128)S(1)} %fusion.99), channel_id=1, replica_groups=mesh['leaf'=32,'front'=4] {'leaf'}, dimensions={1}, use_global_device_ids=true | all-gather | bytes 540672 | tf_op jit(solution)/shard_map/all_gather | solution.py:129
  172.1 3.7 fusion.56
  177.3 2.3 convolution_bitcast_fusion.3
  182.4 24.0 %all_gather.17 = f32[32,4096]{1,0:T(8,128)S(1)} all-gather(f32[32,128]{1,0:T(8,128)S(1)} %fusion.95), channel_id=1, replica_groups=mesh['leaf'=32,'front'=4] {'leaf'}, dimensions={1}, use_global_device_ids=true | all-gather | bytes 540672 | tf_op jit(solution)/shard_map/all_gather | solution.py:129
  206.4 3.7 fusion.59
  210.9 2.3 convolution_bitcast_fusion.2
  213.3 2.5 collective-permute-start.4
  216.0 24.1 %all_gather.18 = f32[32,4096]{1,0:T(8,128)S(1)} all-gather(f32[32,128]{1,0:T(8,128)S(1)} %fusion.91), channel_id=1, replica_groups=mesh['leaf'=32,'front'=4] {'leaf'}, dimensions={1}, use_global_device_ids=true | all-gather | bytes 540672 | tf_op jit(solution)/shard_map/all_gather | solution.py:129
  240.1 3.7 fusion.62
  244.2 2.8 fusion.34
  249.2 2.8 fusion.16
  252.1 67.4 %reduce-scatter.8.cloned.1.call-done = f32[32,128]{1,0:T(8,128)} async-done(((f32[32,4096]{1,0:T(8,128)}), f32[32,128]{1,0:T(8,128)}) %reduce-scatter.8.cloned.1.call-update) | async-done | bytes 16400 | tf_op jit(solution)/shard_map/reduce_scatter | solution.py:151
  324.0 76.7 %reduce-scatter.10.cloned.1.call-done = f32[32,128]{1,0:T(8,128)} async-done(((f32[32,4096]{1,0:T(8,128)}), f32[32,128]{1,0:T(8,128)}) %reduce-scatter.10.cloned.1.call-update) | async-done | bytes 16400 | tf_op jit(solution)/shard_map/reduce_scatter | solution.py:151
  404.9 2.5 collective-permute-start.7
  407.4 2.8 fusion.46
  411.2 76.5 %reduce-scatter.12.cloned.1.call-done = f32[32,128]{1,0:T(8,128)} async-done(((f32[32,4096]{1,0:T(8,128)}), f32[32,128]{1,0:T(8,128)}) %reduce-scatter.12.cloned.1.call-update) | async-done | bytes 16400 | tf_op jit(solution)/shard_map/reduce_scatter | solution.py:151
  493.9 2.8 fusion.40
  497.8 76.8 %reduce-scatter.14.cloned.1.call-done = f32[32,128]{1,0:T(8,128)} async-done(((f32[32,4096]{1,0:T(8,128)}), f32[32,128]{1,0:T(8,128)}) %reduce-scatter.14.cloned.1.call-update) | async-done | bytes 16400 | tf_op jit(solution)/shard_map/reduce_scatter | solution.py:151
  575.5 2.4 collective-permute-start.9
  581.6 46.0 %all-gather.2.cloned.1.call-done = f32[128,7936]{1,0:T(8,128)} async-done(((f32[32,7936]{1,0:T(8,128)}), f32[128,7936]{1,0:T(8,128)}) %all-gather.2.cloned.1.call-update) | async-done | bytes 4063248 | tf_op jit(solution)/shard_map/all_gather | solution.py:163
  627.6 5.6 copy.274
  633.2 5.4 copy.275
  638.6 5.7 fusion.6
  644.4 11.9 %fusion.31 = f32[128,12,128]{0,2,1:T(8,128)S(1)} fusion(f32[12,8,128,128]{3,2,1,0:T(8,128)S(1)} %bitcast.462, f32[128,12,8,128]{3,1,0,2:T(8,128)S(1)} %fusion.6, f32[12,128,128]{2,1,0:T(8,128)S(1)} %copy-done.2), kind=kOutput, calls=%fused_computation.26 | convolution fusion | flops 2416115712 | bytes 14155776 | tf_op jit(solution)/shard_map/rbqo,bqoi->rbi/dot_general | solution.py:167
  (193 shorter events, 60.1 us)
Async XLA Ops:
  7.2 1.5 copy-start
  7.2 10.9 %copy-start.6 = (s32[12,8]{0,1:T(8,128)S(1)}, s32[12,8]{0,1:T(8,128)}, u32[]{:S(2)}) copy-start(s32[12,8]{0,1:T(8,128)} %param.10) | copy-start | bytes 1156
  7.2 83.3 %reduce-scatter.16.cloned.1.call-start = ((), (), s32[]{:S(2)}) async-start(), calls=%async_computation.10 | async-start | bytes 5079040
  9.6 0.9 copy-start.1
  41.1 278.4 %reduce-scatter.8.cloned.1.call-start = ((), (), s32[]{:S(2)}) async-start(), calls=%async_computation.5 | async-start | bytes 540672 | tf_op jit(solution)/shard_map/reduce_scatter | solution.py:151
  90.5 9.1 %slice-start.2 = ((f32[32,7936]{1,0:T(8,128)}), f32[32,4096]{1,0:T(8,128)S(1)}, s32[]{:S(2)}) async-start(f32[32,7936]{1,0:T(8,128)} %reduce-scatter.16.cloned.1.call-done), calls=%async_computation.13 | async-start | bytes 1048576 | tf_op jit(solution)/shard_map/slice | solution.py:31
  100.2 10.7 %copy-start.5 = (f32[32,4,1,128]{3,0,1,2:T(8,128)S(1)}, f32[32,4,1,128]{3,0,1,2:T(8,128)}, u32[]{:S(2)}) copy-start(f32[32,4,1,128]{3,0,1,2:T(8,128)} %copy.318) | copy-start | bytes 196612
  100.2 10.7 %copy-start.4 = (f32[32,8,1,128]{3,0,1,2:T(8,128)S(1)}, f32[32,8,1,128]{3,0,1,2:T(8,128)}, u32[]{:S(2)}) copy-start(f32[32,8,1,128]{3,0,1,2:T(8,128)} %copy.320) | copy-start | bytes 393220
  100.2 12.2 %copy-start.3 = (f32[5,128,128]{2,1,0:T(8,128)S(1)}, f32[5,128,128]{2,1,0:T(8,128)}, u32[]{:S(2)}) copy-start(f32[5,128,128]{2,1,0:T(8,128)} %param.12) | copy-start | bytes 983044
  108.1 2.0 collective-permute-start
  111.1 37.0 %collective-permute-start.1 = (f32[32,15,128]{2,0,1:T(8,128)S(1)}, f32[32,15,128]{2,0,1:T(8,128)S(1)}, u32[]{:S(2)}, u32[]{:S(2)}) collective-permute-start(f32[32,15,128]{2,0,1:T(8,128)S(1)} %pad_maximum_fusion), channel_id=1, source_target_pairs={{0,8},{4,12},{8,0},{12,4},{16,24},{20,28},{24,16},{28,20},{32,40},... | collective-permute-start | bytes 737288 | tf_op jit(solution)/shard_map/ppermute | solution.py:8
  176.1 6.2 collective-permute-start.2
  210.3 3.0 collective-permute-start.3
  213.3 30.5 %collective-permute-start.4 = (f32[32,1,128]{2,0,1:T(8,128)S(1)}, f32[32,1,128]{2,0,1:T(8,128)S(1)}, u32[]{:S(2)}, u32[]{:S(2)}) collective-permute-start(f32[32,1,128]{2,0,1:T(8,128)S(1)} %select_bitcast_fusion.6), channel_id=1, source_target_pairs={{0,64},{4,68},{8,72},{12,76},{16,80},{20,84},{24,88},{28,92},{32,9... | collective-permute-start | bytes 49160 | tf_op jit(solution)/shard_map/ppermute | solution.py:8
  247.8 152.8 %reduce-scatter.10.cloned.1.call-start = ((), (), s32[]{:S(2)}) async-start(), calls=%async_computation.6 | async-start | bytes 540672 | tf_op jit(solution)/shard_map/reduce_scatter | solution.py:151
  247.9 4.2 collective-permute-start.5
  320.4 3.5 collective-permute-start.6
  323.8 163.9 %reduce-scatter.12.cloned.1.call-start = ((), (), s32[]{:S(2)}) async-start(), calls=%async_computation.7 | async-start | bytes 540672 | tf_op jit(solution)/shard_map/reduce_scatter | solution.py:151
  404.9 6.2 collective-permute-start.7
  411.0 163.5 %reduce-scatter.14.cloned.1.call-start = ((), (), s32[]{:S(2)}) async-start(), calls=%async_computation.8 | async-start | bytes 540672 | tf_op jit(solution)/shard_map/reduce_scatter | solution.py:151
  491.4 6.3 collective-permute-start.8
  497.6 130.0 %all-gather.2.cloned.1.call-start = ((), (), s32[]{:S(2)}) async-start(), calls=%async_computation.9 | async-start | bytes 5079040 | tf_op jit(solution)/shard_map/all_gather | solution.py:163
  575.5 3.9 collective-permute-start.9
  580.9 57.7 %copy-start.7 = (s32[12,8]{0,1:T(8,128)S(1)}, s32[12,8]{0,1:T(8,128)}, u32[]{:S(2)}) copy-start(s32[12,8]{0,1:T(8,128)} %param.10) | copy-start | bytes 1156
  633.2 11.1 %slice-start = ((s8[6291456]{0:T(1024)(128)(4,1)}), s8[2097152]{0:T(1024)(128)(4,1)S(1)}, s32[]{:S(2)}) async-start(s8[6291456]{0:T(1024)(128)(4,1)} %bitcast.461), calls=%async_computation.11 | async-start | bytes 4194304
  638.6 5.8 slice-start.1
  638.6 5.8 copy-start.2
Sparse Core Ops, SparseCore 0:
  41.2 49.2 reduce-scatter.15
  248.0 71.5 reduce-scatter.7
  324.0 76.6 reduce-scatter.9
  411.2 76.5 reduce-scatter.11
  497.7 76.8 reduce-scatter.13
  581.0 46.5 all-gather.1
where the time goes:
time: 675 us; the launch traced here: 666 us
  waiting for transfers between devices  396 us (59%)
  blocking collectives  98.3 us (15%)
  matrix products  91.5 us (14%)
  local copies, waits for them, and re-layouts  46.4 us (7%)
  between operations  15.5 us (2%)
  starting transfers between devices  13.6 us (2%)
    reduce_scatter x4, waiting for transfers between devices, local(): lax.psum_scatter(buffer.reshape(columns, leaf_count * block_size), 'leaf'...  297 us
    all_gather x4, blocking collectives, local(): lax.all_gather(solved, 'leaf', axis=1, tiled=True)  98.3 us
    unnamed x7, waiting for transfers between devices  49.2 us
    all_gather x1, waiting for transfers between devices, local(): lax.all_gather(ancestors, 'front', axis=0, tiled=True)  46 us
    dot_general x10, matrix products, local(): jnp.einsum('rmi,moi->ro', group_rows, sep_coupling[position:position + sp...  26.5 us
    dot_general x10, matrix products, local(): jnp.einsum('ro,moi->rmi', own_final[higher_level - 1], sep_coupling[posit...  20.8 us
    unnamed x46, local copies, waits for them, and re-layouts  18.1 us
  transfers between devices with their start and end apart: 16, of which 10 were waited for; matrix products, arithmetic and copies ran while one was open for 5% of the time, Pallas kernels for 0%

commit v1 on v0

--- a/solution.py
+++ b/solution.py
@@ -20,6 +20,15 @@
 
 def from_partner(values, bit_index):
     return from_partner_2(values, "leaf", bit_index)
+
+
+def sum_to_owner(parts, axis):
+    return lax.all_to_all(parts, axis, 0, 0).sum(axis=0)
+
+
+def copies_of_all(shard, axis):
+    copies = jnp.broadcast_to(shard, (lax.axis_size(axis),) + shard.shape)
+    return lax.all_to_all(copies, axis, 0, 0)
 
 
 def halve_blocks(buffer, leaf_id, level_count, block_size):
@@ -71,7 +80,7 @@
 def local(
     load_leaf, leaf_inverse, leaf_coupling, leaf_pattern, load_sep, sep_inverse, sep_coupling
 ):
-    highest = lax.Precision.HIGHEST
+    highest = lax.Precision.HIGH
     all_columns = load_leaf.shape[0]
     leaf_blocks = leaf_pattern.shape[0]
     block_size = leaf_inverse.shape[-1]
@@ -92,11 +101,9 @@
     ).astype(jnp.float32)
     products = jnp.einsum("rbi,bqoi->rbqo", leaf_solved, leaf_coupling, precision=highest)
     gathered_terms = jnp.einsum("rbqo,bqa->rao", products, selector, precision=highest)
-    reduced = lax.psum_scatter(
-        gathered_terms.reshape(lax.axis_size("front") * columns, ancestor_blocks * block_size),
+    reduced = sum_to_owner(
+        gathered_terms.reshape(lax.axis_size("front"), columns, ancestor_blocks * block_size),
         "front",
-        scatter_dimension=0,
-        tiled=True,
     )
     level_updates = halve_blocks(reduced, leaf_id, level_count, block_size)
     sep_rhs = load_sep.reshape(columns, level_count, block_size)
@@ -126,9 +133,7 @@
         own_solved.append(solved)
         if upper_level < level_count:
             gathered.append(
-                lax.all_gather(solved, "leaf", axis=1, tiled=True).reshape(
-                    columns, leaf_count, block_size
-                )
+                jnp.moveaxis(copies_of_all(solved, "leaf"), 0, 1)
             )
     own_final = [None] * level_count
     portions = [None] * level_count
@@ -148,19 +153,14 @@
                 )
                 existing = lax.dynamic_slice_in_dim(buffer, group_start, span_blocks, 1)
                 buffer = lax.dynamic_update_slice_in_dim(buffer, existing + spread, group_start, 1)
-            residual = residual - lax.psum_scatter(
-                buffer.reshape(columns, leaf_count * block_size),
-                "leaf",
-                scatter_dimension=1,
-                tiled=True,
-            )
+            residual = residual - sum_to_owner(jnp.moveaxis(buffer, 1, 0), "leaf")
         final = jnp.einsum("ro,oi->ri", residual, sep_inverse[upper_level - 1], precision=highest)
         own_final[upper_level - 1] = final
         portions[upper_level - 1] = final[:, None, :]
         portions = expand_blocks(portions, leaf_id, upper_level - 1)
     solution_sep = jnp.stack(own_final, axis=1).reshape(columns, level_count * block_size)
     ancestors = jnp.concatenate(portions, axis=1).reshape(columns, ancestor_blocks * block_size)
-    ancestors = lax.all_gather(ancestors, "front", axis=0, tiled=True).reshape(
+    ancestors = copies_of_all(ancestors, "front").reshape(
         all_columns, ancestor_blocks, block_size
     )
     picked = jnp.einsum("rao,bqa->rbqo", ancestors, selector, precision=highest)

time: 675 us -> 356 us (0.53)
  waiting for transfers between devices: 396 us -> 175 us
  blocking collectives: 98.3 us -> 0 us
  starting transfers between devices: 13.6 us -> 74.9 us
  matrix products: 91.5 us -> 69.7 us
  local copies, waits for them, and re-layouts: 46.4 us -> 25.7 us
  between operations: 15.5 us -> 1.91 us
    reduce_scatter x4 -> x0, waiting for transfers between devices: 297 us -> none  [local(): lax.psum_scatter(buffer.reshape(columns, leaf_count * block_size), 'leaf'...]
    all_to_all x0 -> x10, waiting for transfers between devices: none -> 159 us  [the longest x5 90.4 us: sum_to_owner(): return lax.all_to_all(parts, axis, 0, 0).sum(axis=0)]
    all_gather x4 -> x0, blocking collectives: 98.3 us -> none  [local(): lax.all_gather(solved, 'leaf', axis=1, tiled=True)]
    all_to_all x0 -> x10, starting transfers between devices: none -> 62.3 us  [the longest x5 37.6 us: sum_to_owner(): return lax.all_to_all(parts, axis, 0, 0).sum(axis=0)]
    unnamed x7 -> x0, waiting for transfers between devices: 49.2 us -> none
    all_gather x1 -> x0, waiting for transfers between devices: 46 us -> none  [local(): lax.all_gather(ancestors, 'front', axis=0, tiled=True)]
    unnamed x46 -> x24, local copies, waits for them, and re-layouts: 18.1 us -> 4.83 us
    ppermute x10, waiting for transfers between devices: 3.45 us -> 15.9 us  [from_partner_2(): lax.ppermute(shard, axis, [(i, i ^ 1 << bit) for i in range(lax.axis_size...]
  transfers between devices with their start and end apart: 16 -> 20, of which waited for: 10 -> 14; matrix products, arithmetic and copies ran while one was open for 5% -> 9% of each run, Pallas kernels for 0% -> 0%
where the time goes in v1:
time: 356 us; the launch traced here: 351 us
  waiting for transfers between devices  175 us (49%)
  starting transfers between devices  74.9 us (21%)
  matrix products  69.7 us (20%)
  local copies, waits for them, and re-layouts  25.7 us (7%)
  other arithmetic  4.24 us (1%)
    all_to_all x5, waiting for transfers between devices, sum_to_owner(): return lax.all_to_all(parts, axis, 0, 0).sum(axis=0)  90.4 us
    all_to_all x5, waiting for transfers between devices, copies_of_all(): return lax.all_to_all(copies, axis, 0, 0)  68.2 us
    all_to_all x5, starting transfers between devices, sum_to_owner(): return lax.all_to_all(parts, axis, 0, 0).sum(axis=0)  37.6 us
    all_to_all x5, starting transfers between devices, copies_of_all(): return lax.all_to_all(copies, axis, 0, 0)  24.7 us
    dot_general x10, matrix products, local(): jnp.einsum('ro,moi->rmi', own_final[higher_level - 1], sep_coupling[posit...  21.5 us
    dot_general x10, matrix products, local(): jnp.einsum('rmi,moi->ro', group_rows, sep_coupling[position:position + sp...  20.3 us
    ppermute x10, waiting for transfers between devices, from_partner_2(): lax.ppermute(shard, axis, [(i, i ^ 1 << bit) for i in range(lax.axis_size...  15.9 us
    ppermute x10, starting transfers between devices, from_partner_2(): lax.ppermute(shard, axis, [(i, i ^ 1 << bit) for i in range(lax.axis_size...  12.6 us
  transfers between devices with their start and end apart: 20, of which 14 were waited for; matrix products, arithmetic and copies ran while one was open for 9% of the time, Pallas kernels for 0%

profile of v1, /device:TPU:1, one launch (start us, length us, event | category | flops | bytes accessed | tf_op | source)
XLA Modules:
  0.0 351.0 jit_solution(17462578818381100519)
XLA Ops:
  3.5 5.1 %convolution_bitcast_fusion.1 = f32[128,12,8,128]{3,0,2,1:T(8,128)S(1)} fusion(f32[12,8,128,128]{3,2,1,0:T(8,128)} %param.9, f32[12,128,128]{2,1,0:T(8,128)S(1)} %fusion.199), kind=kOutput, calls=%fused_computation.5 | convolution fusion | flops 1207959552 | bytes 13369344 | tf_op jit(solution)/shard_map/rbi,bqoi->rbqo/dot_general | solution.py:102
  8.6 7.7 %fusion.4 = f32[128,62,128]{2,1,0:T(8,128)} fusion(f32[128,12,8,128]{3,0,2,1:T(8,128)S(1)} %convolution_bitcast_fusion.1, s32[12,8]{0,1:T(8,128)S(1)} %copy-done.4), kind=kOutput, calls=%fused_computation.6 | convolution fusion | flops 585111360 | bytes 10355072 | tf_op jit(solution)/shard_map/rbqo,bqa->rao/dot_general | solution.py:103
  16.4 5.3 %reshape.833 = f32[4,32,7936]{2,1,0:T(8,128)} reshape(f32[128,62,128]{2,1,0:T(8,128)} %fusion.4) | data formatting | bytes 8126464 | tf_op jit(solution)/shard_map/reshape | solution.py:105
  21.6 5.9 %all-to-all-start = ((f32[4,32,7936]{2,1,0:T(8,128)}), f32[4,32,7936]{2,1,0:T(8,128)}, u32[]{:S(2)}, u32[]{:S(2)}) async-start(f32[4,32,7936]{2,1,0:T(8,128)} %reshape.833), calls=%async_computation | async-start | bytes 8126464 | tf_op jit(solution)/shard_map/all_to_all | solution.py:26
  27.5 47.5 %all-to-all-done = f32[4,32,7936]{2,1,0:T(8,128)} async-done(((f32[4,32,7936]{2,1,0:T(8,128)}), f32[4,32,7936]{2,1,0:T(8,128)}, u32[]{:S(2)}, u32[]{:S(2)}) %all-to-all-start) | async-done | bytes 4063264 | tf_op jit(solution)/shard_map/all_to_all | solution.py:26
  85.6 4.9 %collective-permute-done.1 = f32[32,15,128]{2,0,1:T(8,128)S(1)} collective-permute-done((f32[32,15,128]{2,0,1:T(8,128)S(1)}, f32[32,15,128]{2,0,1:T(8,128)S(1)}, u32[]{:S(2)}, u32[]{:S(2)}) %collective-permute-start.1) | collective-permute-done | bytes 245792 | tf_op jit(solution)/shard_map/ppermute | solution.py:8
  90.7 3.0 collective-permute-start.2
  94.7 6.4 %all-to-all-start.1 = ((f32[32,32,128]{2,1,0:T(8,128)}), f32[32,32,128]{2,1,0:T(8,128)S(1)}, u32[]{:S(2)}, u32[]{:S(2)}) async-start(f32[32,32,128]{2,1,0:T(8,128)} %broadcast_in_dim.10), calls=%async_computation.1 | async-start | bytes 1048576 | tf_op jit(solution)/shard_map/all_to_all | solution.py:31
  101.2 11.5 %all-to-all-done.1 = f32[32,32,128]{2,1,0:T(8,128)S(1)} async-done(((f32[32,32,128]{2,1,0:T(8,128)}), f32[32,32,128]{2,1,0:T(8,128)S(1)}, u32[]{:S(2)}, u32[]{:S(2)}) %all-to-all-start.1) | async-done | bytes 524320 | tf_op jit(solution)/shard_map/all_to_all | solution.py:31
  115.0 3.7 %all-to-all-start.2 = ((f32[32,32,128]{2,1,0:T(8,128)}), f32[32,32,128]{2,1,0:T(8,128)S(1)}, u32[]{:S(2)}, u32[]{:S(2)}) async-start(f32[32,32,128]{2,1,0:T(8,128)} %broadcast_in_dim.11), calls=%async_computation.2 | async-start | bytes 1048576 | tf_op jit(solution)/shard_map/all_to_all | solution.py:31
  120.1 7.4 %collective-permute-done.3 = f32[32,3,128]{2,0,1:T(8,128)S(1)} collective-permute-done((f32[32,3,128]{2,0,1:T(8,128)S(1)}, f32[32,3,128]{2,0,1:T(8,128)S(1)}, u32[]{:S(2)}, u32[]{:S(2)}) %collective-permute-start.3) | collective-permute-done | bytes 49184 | tf_op jit(solution)/shard_map/ppermute | solution.py:8
  132.8 6.1 %all-to-all-start.3 = ((f32[32,32,128]{2,1,0:T(8,128)}), f32[32,32,128]{2,1,0:T(8,128)S(1)}, u32[]{:S(2)}, u32[]{:S(2)}) async-start(f32[32,32,128]{2,1,0:T(8,128)} %broadcast_in_dim.24), calls=%async_computation.3 | async-start | bytes 1048576 | tf_op jit(solution)/shard_map/all_to_all | solution.py:31
  145.6 5.0 %all-to-all-done.3 = f32[32,32,128]{2,1,0:T(8,128)S(1)} async-done(((f32[32,32,128]{2,1,0:T(8,128)}), f32[32,32,128]{2,1,0:T(8,128)S(1)}, u32[]{:S(2)}, u32[]{:S(2)}) %all-to-all-start.3) | async-done | bytes 524320 | tf_op jit(solution)/shard_map/all_to_all | solution.py:31
  153.6 3.7 %all-to-all-start.4 = ((f32[32,32,128]{2,1,0:T(8,128)}), f32[32,32,128]{2,1,0:T(8,128)S(1)}, u32[]{:S(2)}, u32[]{:S(2)}) async-start(f32[32,32,128]{2,1,0:T(8,128)} %broadcast_in_dim.25), calls=%async_computation.4 | async-start | bytes 1048576 | tf_op jit(solution)/shard_map/all_to_all | solution.py:31
  165.4 3.5 all-to-all-done.4
  171.9 3.1 fusion.29
  176.1 4.9 %all-to-all-start.5 = ((f32[32,32,128]{2,1,0:T(8,128)}), f32[32,32,128]{2,1,0:T(8,128)S(1)}, u32[]{:S(2)}, u32[]{:S(2)}) async-start(f32[32,32,128]{2,1,0:T(8,128)} %fusion.29), calls=%async_computation.5 | async-start | bytes 1048576 | tf_op jit(solution)/shard_map/all_to_all | solution.py:26
  181.0 3.0 fusion.11
  184.1 8.6 %all-to-all-done.5 = f32[32,32,128]{2,1,0:T(8,128)S(1)} async-done(((f32[32,32,128]{2,1,0:T(8,128)}), f32[32,32,128]{2,1,0:T(8,128)S(1)}, u32[]{:S(2)}, u32[]{:S(2)}) %all-to-all-start.5) | async-done | bytes 524320 | tf_op jit(solution)/shard_map/all_to_all | solution.py:26
  195.3 16.7 %all-to-all-start.6 = ((f32[32,32,128]{2,1,0:T(8,128)}), f32[32,32,128]{2,1,0:T(8,128)S(1)}, u32[]{:S(2)}, u32[]{:S(2)}) async-start(f32[32,32,128]{2,1,0:T(8,128)} %bitcast.86), calls=%async_computation.6 | async-start | bytes 1048576 | tf_op jit(solution)/shard_map/all_to_all | solution.py:26
  212.1 11.4 %all-to-all-done.6 = f32[32,32,128]{2,1,0:T(8,128)S(1)} async-done(((f32[32,32,128]{2,1,0:T(8,128)}), f32[32,32,128]{2,1,0:T(8,128)S(1)}, u32[]{:S(2)}, u32[]{:S(2)}) %all-to-all-start.6) | async-done | bytes 524320 | tf_op jit(solution)/shard_map/all_to_all | solution.py:26
  227.3 3.0 fusion.41
  230.3 5.4 %all-to-all-start.7 = ((f32[32,32,128]{2,1,0:T(8,128)}), f32[32,32,128]{2,1,0:T(8,128)S(1)}, u32[]{:S(2)}, u32[]{:S(2)}) async-start(f32[32,32,128]{2,1,0:T(8,128)} %fusion.41), calls=%async_computation.7 | async-start | bytes 1048576 | tf_op jit(solution)/shard_map/all_to_all | solution.py:26
  235.8 11.5 %all-to-all-done.7 = f32[32,32,128]{2,1,0:T(8,128)S(1)} async-done(((f32[32,32,128]{2,1,0:T(8,128)}), f32[32,32,128]{2,1,0:T(8,128)S(1)}, u32[]{:S(2)}, u32[]{:S(2)}) %all-to-all-start.7) | async-done | bytes 524320 | tf_op jit(solution)/shard_map/all_to_all | solution.py:26
  251.8 3.0 fusion.35
  254.9 4.7 %all-to-all-start.8 = ((f32[32,32,128]{2,1,0:T(8,128)}), f32[32,32,128]{2,1,0:T(8,128)S(1)}, u32[]{:S(2)}, u32[]{:S(2)}) async-start(f32[32,32,128]{2,1,0:T(8,128)} %fusion.35), calls=%async_computation.8 | async-start | bytes 1048576 | tf_op jit(solution)/shard_map/all_to_all | solution.py:26
  259.8 11.4 %all-to-all-done.8 = f32[32,32,128]{2,1,0:T(8,128)S(1)} async-done(((f32[32,32,128]{2,1,0:T(8,128)}), f32[32,32,128]{2,1,0:T(8,128)S(1)}, u32[]{:S(2)}, u32[]{:S(2)}) %all-to-all-start.8) | async-done | bytes 524320 | tf_op jit(solution)/shard_map/all_to_all | solution.py:26
  279.4 4.9 %all-to-all-start.9 = ((f32[4,32,7936]{2,1,0:T(8,128)}), f32[4,32,7936]{2,1,0:T(8,128)}, u32[]{:S(2)}, u32[]{:S(2)}) async-start(f32[4,32,7936]{2,1,0:T(8,128)} %broadcast_in_dim.26), calls=%async_computation.9 | async-start | bytes 8126464 | tf_op jit(solution)/shard_map/all_to_all | solution.py:31
  284.9 46.8 %all-to-all-done.9 = f32[4,32,7936]{2,1,0:T(8,128)} async-done(((f32[4,32,7936]{2,1,0:T(8,128)}), f32[4,32,7936]{2,1,0:T(8,128)}, u32[]{:S(2)}, u32[]{:S(2)}) %all-to-all-start.9) | async-done | bytes 4063264 | tf_op jit(solution)/shard_map/all_to_all | solution.py:31
  331.7 5.2 %reshape.865 = f32[128,62,128,1]{2,1,0,3:T(8,128)} reshape(f32[4,32,7936]{2,1,0:T(8,128)} %all-to-all-done.9) | data formatting | bytes 8126464 | tf_op jit(solution)/shard_map/reshape | solution.py:163
  337.0 4.8 %convolution_bitcast_fusion = f32[128,12,8,128]{3,1,0,2:T(8,128)S(1)} fusion(f32[128,62,128,1]{2,1,0,3:T(8,128)} %reshape.865, s32[12,8]{0,1:T(8,128)S(1)} %copy-done.4), kind=kOutput, calls=%fused_computation.4 | convolution fusion | flops 585111360 | bytes 10355072 | tf_op jit(solution)/shard_map/rao,bqa->rbqo/dot_general | solution.py:166
  341.8 7.1 %fusion.26 = f32[128,12,128]{0,2,1:T(8,128)S(1)} fusion(f32[12,8,128,128]{3,2,1,0:T(8,128)S(1)} %bitcast.435, f32[128,12,8,128]{3,1,0,2:T(8,128)S(1)} %convolution_bitcast_fusion, f32[12,128,128]{2,1,0:T(8,128)S(1)} %copy-done.2), kind=kOutput, calls=%fused_computation.24 | convolution fusion | flops 1208156160 | bytes 14155776 | tf_op jit(solution)/shard_map/rbqo,bqoi->rbi/dot_general | solution.py:167
  (175 shorter events, 66.9 us)
Async XLA Ops:
  0.6 1.5 copy-start
  0.6 8.0 %copy-start.4 = (s32[12,8]{0,1:T(8,128)S(1)}, s32[12,8]{0,1:T(8,128)}, u32[]{:S(2)}) copy-start(s32[12,8]{0,1:T(8,128)} %param.10) | copy-start | bytes 1156
  2.6 0.9 copy-start.1
  21.6 53.3 %all-to-all-start = ((f32[4,32,7936]{2,1,0:T(8,128)}), f32[4,32,7936]{2,1,0:T(8,128)}, u32[]{:S(2)}, u32[]{:S(2)}) async-start(f32[4,32,7936]{2,1,0:T(8,128)} %reshape.833), calls=%async_computation | async-start | bytes 8126464 | tf_op jit(solution)/shard_map/all_to_all | solution.py:26
  27.5 66.2 %copy-start.3 = (f32[5,128,128]{2,1,0:T(8,128)S(1)}, f32[5,128,128]{2,1,0:T(8,128)}, u32[]{:S(2)}) copy-start(f32[5,128,128]{2,1,0:T(8,128)} %param.12) | copy-start | bytes 983044
  79.6 3.1 collective-permute-start
  83.0 7.5 %collective-permute-start.1 = (f32[32,15,128]{2,0,1:T(8,128)S(1)}, f32[32,15,128]{2,0,1:T(8,128)S(1)}, u32[]{:S(2)}, u32[]{:S(2)}) collective-permute-start(f32[32,15,128]{2,0,1:T(8,128)S(1)} %pad_maximum_fusion), channel_id=1, source_target_pairs={{0,8},{4,12},{8,0},{12,4},{16,24},{20,28},{24,16},{28,20},{32,40},... | collective-permute-start | bytes 737288 | tf_op jit(solution)/shard_map/ppermute | solution.py:8
  90.7 10.5 %collective-permute-start.2 = (f32[32,7,128]{2,0,1:T(8,128)S(1)}, f32[32,7,128]{2,0,1:T(8,128)S(1)}, u32[]{:S(2)}, u32[]{:S(2)}) collective-permute-start(f32[32,7,128]{2,0,1:T(8,128)S(1)} %pad_maximum_fusion.2), channel_id=1, source_target_pairs={{0,16},{4,20},{8,24},{12,28},{16,0},{20,4},{24,8},{28,12},{32,48},... | collective-permute-start | bytes 344072 | tf_op jit(solution)/shard_map/ppermute | solution.py:8
  94.7 18.1 %all-to-all-start.1 = ((f32[32,32,128]{2,1,0:T(8,128)}), f32[32,32,128]{2,1,0:T(8,128)S(1)}, u32[]{:S(2)}, u32[]{:S(2)}) async-start(f32[32,32,128]{2,1,0:T(8,128)} %broadcast_in_dim.10), calls=%async_computation.1 | async-start | bytes 1048576 | tf_op jit(solution)/shard_map/all_to_all | solution.py:31
  115.0 15.4 %all-to-all-start.2 = ((f32[32,32,128]{2,1,0:T(8,128)}), f32[32,32,128]{2,1,0:T(8,128)S(1)}, u32[]{:S(2)}, u32[]{:S(2)}) async-start(f32[32,32,128]{2,1,0:T(8,128)} %broadcast_in_dim.11), calls=%async_computation.2 | async-start | bytes 1048576 | tf_op jit(solution)/shard_map/all_to_all | solution.py:31
  118.7 8.9 %collective-permute-start.3 = (f32[32,3,128]{2,0,1:T(8,128)S(1)}, f32[32,3,128]{2,0,1:T(8,128)S(1)}, u32[]{:S(2)}, u32[]{:S(2)}) collective-permute-start(f32[32,3,128]{2,0,1:T(8,128)S(1)} %pad_maximum_fusion.4), channel_id=1, source_target_pairs={{0,32},{4,36},{8,40},{12,44},{16,48},{20,52},{24,56},{28,60},{32,0... | collective-permute-start | bytes 147464 | tf_op jit(solution)/shard_map/ppermute | solution.py:8
  132.8 17.8 %all-to-all-start.3 = ((f32[32,32,128]{2,1,0:T(8,128)}), f32[32,32,128]{2,1,0:T(8,128)S(1)}, u32[]{:S(2)}, u32[]{:S(2)}) async-start(f32[32,32,128]{2,1,0:T(8,128)} %broadcast_in_dim.24), calls=%async_computation.3 | async-start | bytes 1048576 | tf_op jit(solution)/shard_map/all_to_all | solution.py:31
  138.9 32.7 %collective-permute-start.4 = (f32[32,1,128]{2,0,1:T(8,128)S(1)}, f32[32,1,128]{2,0,1:T(8,128)S(1)}, u32[]{:S(2)}, u32[]{:S(2)}) collective-permute-start(f32[32,1,128]{2,0,1:T(8,128)S(1)} %select_bitcast_fusion.6), channel_id=1, source_target_pairs={{0,64},{4,68},{8,72},{12,76},{16,80},{20,84},{24,88},{28,92},{32,9... | collective-permute-start | bytes 49160 | tf_op jit(solution)/shard_map/ppermute | solution.py:8
  153.6 15.3 %all-to-all-start.4 = ((f32[32,32,128]{2,1,0:T(8,128)}), f32[32,32,128]{2,1,0:T(8,128)S(1)}, u32[]{:S(2)}, u32[]{:S(2)}) async-start(f32[32,32,128]{2,1,0:T(8,128)} %broadcast_in_dim.25), calls=%async_computation.4 | async-start | bytes 1048576 | tf_op jit(solution)/shard_map/all_to_all | solution.py:31
  175.0 9.1 %collective-permute-start.5 = (f32[32,1,128]{2,0,1:T(8,128)S(1)}, f32[32,1,128]{2,0,1:T(8,128)S(1)}, u32[]{:S(2)}, u32[]{:S(2)}) collective-permute-start(f32[32,1,128]{2,0,1:T(8,128)S(1)} %bitcast.451), channel_id=1, source_target_pairs={{0,64},{4,68},{8,72},{12,76},{16,80},{20,84},{24,88},{28,92},{32,9... | collective-permute-start | bytes 49160 | tf_op jit(solution)/shard_map/ppermute | solution.py:8
  176.1 16.5 %all-to-all-start.5 = ((f32[32,32,128]{2,1,0:T(8,128)}), f32[32,32,128]{2,1,0:T(8,128)S(1)}, u32[]{:S(2)}, u32[]{:S(2)}) async-start(f32[32,32,128]{2,1,0:T(8,128)} %fusion.29), calls=%async_computation.5 | async-start | bytes 1048576 | tf_op jit(solution)/shard_map/all_to_all | solution.py:26
  192.8 19.2 %collective-permute-start.6 = (f32[32,3,128]{2,0,1:T(8,128)S(1)}, f32[32,3,128]{2,0,1:T(8,128)S(1)}, u32[]{:S(2)}, u32[]{:S(2)}) collective-permute-start(f32[32,3,128]{2,0,1:T(8,128)S(1)} %pad_maximum_fusion.5), channel_id=1, source_target_pairs={{0,32},{4,36},{8,40},{12,44},{16,48},{20,52},{24,56},{28,60},{32,0... | collective-permute-start | bytes 147464 | tf_op jit(solution)/shard_map/ppermute | solution.py:8
  195.3 28.2 %all-to-all-start.6 = ((f32[32,32,128]{2,1,0:T(8,128)}), f32[32,32,128]{2,1,0:T(8,128)S(1)}, u32[]{:S(2)}, u32[]{:S(2)}) async-start(f32[32,32,128]{2,1,0:T(8,128)} %bitcast.86), calls=%async_computation.6 | async-start | bytes 1048576 | tf_op jit(solution)/shard_map/all_to_all | solution.py:26
  226.7 9.0 %collective-permute-start.7 = (f32[32,7,128]{2,0,1:T(8,128)S(1)}, f32[32,7,128]{2,0,1:T(8,128)S(1)}, u32[]{:S(2)}, u32[]{:S(2)}) collective-permute-start(f32[32,7,128]{2,0,1:T(8,128)S(1)} %pad_maximum_fusion.3), channel_id=1, source_target_pairs={{0,16},{4,20},{8,24},{12,28},{16,0},{20,4},{24,8},{28,12},{32,48},... | collective-permute-start | bytes 344072 | tf_op jit(solution)/shard_map/ppermute | solution.py:8
  230.3 17.0 %all-to-all-start.7 = ((f32[32,32,128]{2,1,0:T(8,128)}), f32[32,32,128]{2,1,0:T(8,128)S(1)}, u32[]{:S(2)}, u32[]{:S(2)}) async-start(f32[32,32,128]{2,1,0:T(8,128)} %fusion.41), calls=%async_computation.7 | async-start | bytes 1048576 | tf_op jit(solution)/shard_map/all_to_all | solution.py:26
  251.7 7.9 %collective-permute-start.8 = (f32[32,15,128]{2,0,1:T(8,128)S(1)}, f32[32,15,128]{2,0,1:T(8,128)S(1)}, u32[]{:S(2)}, u32[]{:S(2)}) collective-permute-start(f32[32,15,128]{2,0,1:T(8,128)S(1)} %pad_maximum_fusion.1), channel_id=1, source_target_pairs={{0,8},{4,12},{8,0},{12,4},{16,24},{20,28},{24,16},{28,20},{32,40},... | collective-permute-start | bytes 737288 | tf_op jit(solution)/shard_map/ppermute | solution.py:8
  254.9 16.4 %all-to-all-start.8 = ((f32[32,32,128]{2,1,0:T(8,128)}), f32[32,32,128]{2,1,0:T(8,128)S(1)}, u32[]{:S(2)}, u32[]{:S(2)}) async-start(f32[32,32,128]{2,1,0:T(8,128)} %fusion.35), calls=%async_computation.8 | async-start | bytes 1048576 | tf_op jit(solution)/shard_map/all_to_all | solution.py:26
  274.6 2.1 collective-permute-start.9
  279.4 52.3 %all-to-all-start.9 = ((f32[4,32,7936]{2,1,0:T(8,128)}), f32[4,32,7936]{2,1,0:T(8,128)}, u32[]{:S(2)}, u32[]{:S(2)}) async-start(f32[4,32,7936]{2,1,0:T(8,128)} %broadcast_in_dim.26), calls=%async_computation.9 | async-start | bytes 8126464 | tf_op jit(solution)/shard_map/all_to_all | solution.py:31
  284.9 56.8 %slice-start = ((s8[6291456]{0:T(1024)(128)(4,1)}), s8[2097152]{0:T(1024)(128)(4,1)S(1)}, s32[]{:S(2)}) async-start(s8[6291456]{0:T(1024)(128)(4,1)} %bitcast.434), calls=%async_computation.10 | async-start | bytes 4194304
  336.9 4.8 %slice-start.1 = ((s8[6291456]{0:T(1024)(128)(4,1)}), s8[4194304]{0:T(1024)(128)(4,1)S(1)}, s32[]{:S(2)}) async-start(s8[6291456]{0:T(1024)(128)(4,1)} %bitcast.434), calls=%async_computation.11 | async-start | bytes 8388608
  337.0 4.8 %copy-start.2 = (f32[12,128,128]{2,1,0:T(8,128)S(1)}, f32[12,128,128]{2,1,0:T(8,128)}, u32[]{:S(2)}) copy-start(f32[12,128,128]{2,1,0:T(8,128)} %copy-done.1) | copy-start | bytes 2359300

commit v2 on v1

v2 whole, which is shorter than its diff:
```python
import jax
import jax.numpy as jnp
from jax import lax
from jax.experimental import pallas as pl
from jax.experimental.pallas import tpu as pltpu
from jax.sharding import PartitionSpec as P

F32 = jnp.float32
BF16 = jnp.bfloat16
BLK = 128
COLS = 32
VMEM_BYTES = 48 * 1024 * 1024
RUNS = {(2, 1): 0, (3, 1): 4, (3, 2): 12, (4, 1): 20, (4, 2): 36, (4, 3): 52}
RUNS |= {(5, 1): 68, (5, 2): 100, (5, 3): 132, (5, 4): 164}
CHUNK = 8


def split(value):
    high = value.astype(BF16)
    low = (value - high.astype(F32)).astype(BF16)
    return high, low


def stacked(value):
    return jnp.concatenate(split(value), axis=0)


def beside(value):
    return jnp.concatenate(split(value), axis=1)


def dot_nt(left, right):
    return lax.dot_general(left, right, (((1,), (1,)), ((), ())), preferred_element_type=F32)


def dot_nn(left, right):
    return lax.dot_general(left, right, (((1,), (0,)), ((), ())), preferred_element_type=F32)


def fold(terms):
    rows = terms.shape[0] // 2
    return (terms[:rows, :BLK] + terms[:rows, BLK:]) + (terms[rows:, :BLK] + terms[rows:, BLK:])


def times_transposed(value, matrix):
    return fold(dot_nt(stacked(value), stacked(matrix)))


def times(value, matrix):
    return fold(dot_nn(stacked(value), beside(matrix)))


def sum_times_transposed(lefts, matrices):
    total = None
    for k in range(0, len(lefts), 2):
        left = jnp.concatenate([lefts[k], lefts[k + 1]], axis=1)
        right = jnp.concatenate([stacked(matrices[k]), stacked(matrices[k + 1])], axis=1)
        part = dot_nt(left, right)
        total = part if total is None else total + part
    return total


def wide_left(value):
    both = stacked(value)
    return jnp.concatenate([both, both], axis=1)


def two_times(left, first, second):
    right = jnp.concatenate([stacked(first), stacked(second)], axis=1)
    out = dot_nn(left, right)
    rows = out.shape[0] // 2
    out = out[:rows] + out[rows:]
    return out[:, :BLK], out[:, BLK:]


def call(body, name, coords, inputs, outs, in_any=(), scratch=(), flops=0):
    specs = [
        pl.BlockSpec(memory_space=pl.ANY if k in in_any else pltpu.VMEM)
        for k in range(len(inputs))
    ]
    return pl.pallas_call(
        body,
        name=name,
        out_shape=[jax.ShapeDtypeStruct(shape, F32) for shape in outs],
        grid_spec=pltpu.PrefetchScalarGridSpec(
            num_scalar_prefetch=1,
            grid=(1,),
            in_specs=specs,
            out_specs=[pl.BlockSpec(memory_space=pltpu.VMEM) for _ in outs],
            scratch_shapes=list(scratch),
        ),
        compiler_params=pltpu.CompilerParams(vmem_limit_bytes=VMEM_BYTES),
        cost_estimate=pl.CostEstimate(flops=flops, bytes_accessed=1 << 20, transcendentals=0),
    )(coords, *inputs)


def fetch(source, first, count, target, sems):
    for k in range(0, count, CHUNK):
        size = min(CHUNK, count - k)
        pltpu.make_async_copy(
            source.at[pl.ds(first + k, size)], target.at[pl.ds(k, size)], sems.at[k // CHUNK]
        ).start()


def fetched(source, first, count, target, sems):
    for k in range(0, count, CHUNK):
        size = min(CHUNK, count - k)
        pltpu.make_async_copy(
            source.at[pl.ds(first + k, size)], target.at[pl.ds(k, size)], sems.at[k // CHUNK]
        ).wait()


def matrices(count):
    return [pltpu.VMEM((count, BLK, BLK), F32), pltpu.SemaphoreType.DMA((-(-count // CHUNK),))]


def leaf_forward_kernel(
    coords, pattern, load, inverse, coupling, load_sep, solved, mine13, theirs13, mine45, theirs45, sums
):
    block = pl.program_id(0)
    core, y_at, x_at, front = coords[0], coords[1], coords[2], coords[3]

    @pl.when(block == 0)
    def _():
        sums[...] = jnp.zeros_like(sums)
        rows = pl.ds(pl.multiple_of(front * COLS, COLS), COLS)
        slots = (
            core,
            2 + (y_at & 1) * 2 + core,
            6 + y_at,
            10 + (x_at & 1) * 4 + y_at,
            18 + x_at * 4 + y_at,
        )
        for level, slot in enumerate(slots):
            sums[slot, rows, :] = -load_sep[:, level * BLK : (level + 1) * BLK]

    here = times_transposed(load[...], inverse[0])
    solved[...] = here
    left = beside(here)
    for q in range(8):
        matrix = stacked(coupling[0, q])
        out = dot_nt(left, jnp.concatenate([matrix, matrix], axis=1))
        index = pattern[block * 8 + q]
        slot = jnp.where(index < 6, index, 6 + ((index - 6) >> 1))
        slot = jnp.where((index >= 6) & ((index & 1) != core), slot + 34, slot)
        sums[slot] += out[:, :BLK] + out[:, BLK:]

    @pl.when(block == pl.num_programs(0) - 1)
    def _():
        mine13[...] = sums[0:10]
        theirs13[0:6] = sums[0:6]
        theirs13[6:10] = sums[40:44]
        mine45[...] = sums[10:34]
        theirs45[...] = sums[44:68]


def leaf_forward(coords, pattern, load_leaf, leaf_inverse, leaf_coupling, load_sep):
    blocks = leaf_inverse.shape[0]
    whole = lambda *shape: pl.BlockSpec(shape, lambda b, *_: (0,) * len(shape))
    outs = [(BLK, blocks * BLK), (10, BLK, BLK), (10, BLK, BLK), (24, BLK, BLK), (24, BLK, BLK)]
    return pl.pallas_call(
        leaf_forward_kernel,
        name="leaf_forward",
        out_shape=[jax.ShapeDtypeStruct(shape, F32) for shape in outs],
        grid_spec=pltpu.PrefetchScalarGridSpec(
            num_scalar_prefetch=2,
            grid=(blocks,),
            in_specs=[
                pl.BlockSpec((BLK, BLK), lambda b, *_: (0, b)),
                pl.BlockSpec((1, BLK, BLK), lambda b, *_: (b, 0, 0)),
                pl.BlockSpec((1, 8, BLK, BLK), lambda b, *_: (b, 0, 0, 0)),
                whole(COLS, 5 * BLK),
            ],
            out_specs=[pl.BlockSpec((BLK, BLK), lambda b, *_: (0, b))]
            + [whole(*shape) for shape in outs[1:]],
            scratch_shapes=[pltpu.VMEM((68, BLK, BLK), F32)],
        ),
        compiler_params=pltpu.CompilerParams(vmem_limit_bytes=VMEM_BYTES),
    )(coords, pattern, load_leaf, leaf_inverse, leaf_coupling, load_sep)


def front_parts_kernel(coords, mine, received, own, part1, part2, part3):
    for j, out in enumerate((own, part1, part2, part3)):
        rows = pl.ds(pl.multiple_of((coords[3] ^ j) * COLS, COLS), COLS)
        out[...] = mine[:, rows, :] + received[:, rows, :]


def front_parts(coords, mine, received):
    shape = (mine.shape[0], COLS, BLK)
    return call(front_parts_kernel, "front_parts", coords, [mine, received], [shape] * 4)


def level12_message_kernel(coords, own, part1, part2, part3, keep, message):
    total = (own[...] + part1[...]) + (part2[...] + part3[...])
    y_at = coords[1]
    keep[0:6] = total[0:6]
    message[0:6] = total[0:6]

    def level3(j):
        row = pl.ds(6 + (y_at ^ j), 1)
        return (own[row] + part1[row]) + (part2[row] + part3[row])

    keep[6:7] = level3(0)
    keep[7:8] = level3(3)
    message[6:7] = level3(1)
    message[7:8] = level3(2)


def level12_kernel(
    coords, keep, received, own6, core6, y6, diagonal6, solved, message, left1, level1
):
    core, y_bit = coords[0], coords[1] & 1
    members = []
    for dy in range(2):
        for dc in range(2):
            members.append(((y_bit ^ dy) * 2 + (core ^ dc), dy, core ^ dc))
    mats = (own6, core6, y6, diagonal6)
    for (index, dy, at), mat in zip(members, mats):
        source = received if dy else keep
        here = times_transposed(-source[at], mat[0])
        solved[index] = here
        left1[index] = stacked(here)
    for (index, dy, at), mat in zip(members, mats):
        acc = sum_times_transposed([left1[m] for m in range(4)], [mat[2 + m] for m in range(4)])
        rhs = -(keep[2 + index] + received[2 + index]) - fold(acc)
        solved[4 + index] = times_transposed(rhs, mat[1])
    message[0:8] = solved[0:8]
    solved[8] = keep[6] + received[6]
    message[8] = keep[7] + received[7]


def level3_kernel(
    coords, solved, received, inverse, coupling, y3, y12, y12p, mats, sems, left
):
    fetch(coupling, RUNS[3, 1], 16, mats, sems)
    core, half = coords[0], coords[1] >> 1
    for level in range(2):
        for k in range(4):
            for source, part in ((solved, half), (received, 1 - half)):
                at = level * 8 + part * 4 + k
                y12[at] = source[level * 4 + k]
                left[at] = stacked(source[level * 4 + k])
    for level in range(2):
        for y in range(4):
            y12p[level * 4 + y] = y12[level * 8 + y * 2 + core]
    fetched(coupling, RUNS[3, 1], 16, mats, sems)
    acc = sum_times_transposed([left[m] for m in range(16)], [mats[m] for m in range(16)])
    rhs = -(solved[8] + received[8]) - fold(acc)
    y3[...] = times_transposed(rhs, inverse[2])


def level4_operand_kernel(coords, y3, own, part1, part2, part3, operand, sums5):
    for p in range(8):
        operand[p, 0] = y3[...]
        operand[p, 1] = (own[p] + part1[p]) + (part2[p] + part3[p])
    sums5[...] = (own[8:24] + part1[8:24]) + (part2[8:24] + part3[8:24])


def level4_before_kernel(coords, y12, r8, c8, coupling, acc, mats, sems, left):
    fetch(coupling, RUNS[4, 1], 32, mats, sems)
    core, x_bit = coords[0], coords[2] & 1
    for level in range(2):
        for m in range(8):
            left[level * 16 + x_bit * 8 + m] = stacked(y12[level * 8 + m])
        for y in range(4):
            at = level * 16 + (1 - x_bit) * 8 + y * 2
            left[at + core] = stacked(r8[level * 4 + y])
            left[at + 1 - core] = stacked(c8[level * 4 + y])
    fetched(coupling, RUNS[4, 1], 32, mats, sems)
    acc[...] = sum_times_transposed([left[m] for m in range(32)], [mats[m] for m in range(32)])


def level4_kernel(coords, acc, mine, other, sums5, inverse, coupling, y4, operand, mats, sems, left):
    fetch(coupling, RUNS[4, 3], 16, mats, sems)
    core = coords[0]
    total = mine[0, 1]
    for p in range(1, 8):
        total = total + mine[p, 1]
    for p in range(8):
        left[p * 2 + core] = stacked(mine[p, 0])
        left[p * 2 + 1 - core] = stacked(other[p, 0])
    fetched(coupling, RUNS[4, 3], 16, mats, sems)
    terms = acc[...] + sum_times_transposed(
        [left[m] for m in range(16)], [mats[m] for m in range(16)]
    )
    here = times_transposed(-total - fold(terms), inverse[3])
    y4[...] = here
    for p in range(16):
        operand[p, 0] = here
        operand[p, 1] = sums5[p]


def level5_before_kernel(
    coords, y12, r8, c8, r24, c24, r16, c16, y3m, y3o, z3m, z3o, coupling, acc, mats, sems, left
):
    fetch(coupling, RUNS[5, 1], 96, mats, sems)
    core, x_at = coords[0], coords[2]
    for level in range(2):
        for m in range(8):
            left[level * 32 + x_at * 8 + m] = stacked(y12[level * 8 + m])
        for j, same, other in ((1, r8, c8), (3, r24, c24), (2, r16, c16)):
            for y in range(4):
                at = level * 32 + (x_at ^ j) * 8 + y * 2
                left[at + core] = stacked(same[level * 4 + y])
                left[at + 1 - core] = stacked(other[level * 4 + y])
    for half, same, other in ((x_at >> 1, y3m, y3o), (1 - (x_at >> 1), z3m, z3o)):
        for p in range(8):
            at = 64 + half * 16 + p * 2
            left[at + core] = stacked(same[p, 0])
            left[at + 1 - core] = stacked(other[p, 0])
    fetched(coupling, RUNS[5, 1], 96, mats, sems)

    def step(i, total):
        at = i * CHUNK
        return total + sum_times_transposed(
            [left[at + m] for m in range(CHUNK)], [mats[at + m] for m in range(CHUNK)]
        )

    acc[...] = lax.fori_loop(0, 96 // CHUNK, step, jnp.zeros((2 * COLS, 2 * BLK), F32))


def level5_kernel(coords, acc, mine, other, inverse, coupling, x5, operand, mats, sems, left):
    fetch(coupling, RUNS[5, 4], 32, mats, sems)
    core = coords[0]
    total = mine[0, 1]
    for p in range(1, 16):
        total = total + mine[p, 1]
    for p in range(16):
        left[p * 2 + core] = stacked(mine[p, 0])
        left[p * 2 + 1 - core] = stacked(other[p, 0])
    fetched(coupling, RUNS[5, 4], 32, mats, sems)
    terms = acc[...] + sum_times_transposed(
        [left[m] for m in range(32)], [mats[m] for m in range(32)]
    )
    solved = times_transposed(-total - fold(terms), inverse[4])
    here = times(solved, inverse[4])
    x5[...] = here
    wide = wide_left(here)
    for p in range(16):
        operand[p, 0], operand[p, 1] = two_times(wide, mats[2 * p], mats[2 * p + 1])
        operand[p, 2] = here


def level5_back_kernel(coords, x5, coupling, mine, theirs, mats, sems):
    fetch(coupling, RUNS[5, 1], 96, mats, sems)
    core = coords[0]
    wide = wide_left(x5[...])
    fetched(coupling, RUNS[5, 1], 96, mats, sems)

    def step(i, _):
        for k in range(CHUNK // 2):
            pair = i * (CHUNK // 2) + k
            at = pair * 2
            mine[pair], theirs[pair] = two_times(wide, mats[at + core], mats[at + 1 - core])
        return 0

    lax.fori_loop(0, 96 // CHUNK, step, 0)


def halves_kernel(coords, mine, received, keep, send):
    half = coords[2] >> 1
    for level in range(3):
        for out, part in ((keep, half), (send, 1 - half)):
            rows = pl.ds(level * 16 + part * 8, 8)
            out[level * 8 : level * 8 + 8] = mine[rows] + received[rows]


def level4_sum_kernel(coords, parts, own, other, x5p):
    core = coords[0]
    for out, at in ((own, core), (other, 1 - core)):
        total = parts[0, at]
        for p in range(1, 16):
            total = total + parts[p, at]
        out[...] = total
    for p in range(16):
        x5p[p] = parts[p, 2]


def level4_back_kernel(coords, y4, own, received, inverse, coupling, x4, mine, theirs, mats, sems):
    fetch(coupling, RUNS[4, 1], 48, mats, sems)
    core = coords[0]
    here = times(y4[...] - (own[...] + received[...]), inverse[3])
    x4[...] = here
    wide = wide_left(here)
    fetched(coupling, RUNS[4, 1], 48, mats, sems)
    for pair in range(24):
        mine[pair], theirs[pair] = two_times(wide, mats[2 * pair + core], mats[2 * pair + 1 - core])


def level3_operand_kernel(coords, x4, mine, received, keep, top, operand):
    for p in range(8):
        for level in range(3):
            at = level * 8 + p
            operand[p, level] = (mine[at] + received[at]) + (keep[at] + top[at])
        operand[p, 3] = x4[...]


def level3_back_kernel(
    coords, parts, y3, inverse, coupling, x3, x4p, keep, message, mats, sems, spread
):
    fetch(coupling, RUNS[3, 1], 16, mats, sems)
    core, y_at = coords[0], coords[1]
    sums = []
    for level in range(3):
        total = parts[0, level]
        for p in range(1, 8):
            total = total + parts[p, level]
        sums.append(total)
    for p in range(8):
        x4p[p] = parts[p, 3]
    here = times(y3[...] - sums[2], inverse[2])
    x3[...] = here
    wide = wide_left(here)
    fetched(coupling, RUNS[3, 1], 16, mats, sems)
    for pair in range(8):
        spread[2 * pair], spread[2 * pair + 1] = two_times(wide, mats[2 * pair], mats[2 * pair + 1])
    for level in range(2):
        spread[level * 8 + y_at * 2 + core] += sums[level]
    half = y_at >> 1
    for level in range(2):
        for out, part in ((keep, half), (message, 1 - half)):
            out[level * 4 : level * 4 + 4] = spread[pl.ds(level * 8 + part * 4, 4)]
    message[8] = here


def level3_sum_kernel(coords, keep, received, x3, message):
    message[0:8] = keep[...] + received[0:8]
    message[8] = x3[...]
    message[9] = received[8]


def level12_back_kernel(
    coords, m0, m1, m2, m3, solved, own6, core6, y6, diagonal6, own1, own2, x123, left, terms, here2
):
    core, y_at = coords[0], coords[1]
    y_bit = y_at & 1
    terms[...] = (m0[0:8] + m1[0:8]) + (m2[0:8] + m3[0:8])
    for message, dy, dc in ((m0, 0, 0), (m1, 0, 1), (m2, 1, 0), (m3, 1, 1)):
        x123[6 + (y_at ^ dy) * 2 + (core ^ dc)] = message[8]
        x123[6 + (y_at ^ dy ^ 3) * 2 + (core ^ dc)] = message[9]
    members = [
        ((y_bit ^ dy) * 2 + (core ^ dc), dy, core ^ dc) for dy in range(2) for dc in range(2)
    ]
    mats = (own6, core6, y6, diagonal6)
    for k, ((index, dy, at), mat) in enumerate(zip(members, mats)):
        here = times(solved[4 + index] - terms[4 + index], mat[1])
        x123[2 + index] = here
        if k == 0:
            own2[...] = here
        wide = wide_left(here)
        for m in range(0, 4, 2):
            first, second = two_times(wide, mat[2 + m], mat[3 + m])
            terms[m] += first
            terms[m + 1] += second
    for k in range(2):
        index, dy, at = members[k]
        here = times(solved[index] - terms[index], mats[k][0])
        x123[at] = here
        if k == 0:
            own1[...] = here


def leaf_backward_kernel(
    coords, pattern, low0, low1, low2, low3, x4m, x4o, x5m, x5o, solved, inverse, coupling, out, blocks
):
    block = pl.program_id(0)
    core, front = coords[0], coords[3]

    @pl.when(block == 0)
    def _():
        def place(index, j, value):
            high, low = split(value)
            at = pl.multiple_of((front ^ j) * COLS, COLS)
            blocks[index, pl.ds(at, COLS), :] = high
            blocks[index, pl.ds(BLK + at, COLS), :] = low

        for j, low in enumerate((low0, low1, low2, low3)):
            for a in range(14):
                place(a, j, low[a])
            for p in range(8):
                place(14 + 2 * p + core, j, x4m[j, p])
                place(15 + 2 * p - core, j, x4o[j, p])
            for p in range(16):
                place(30 + 2 * p + core, j, x5m[j, p])
                place(31 + 2 * p - core, j, x5o[j, p])

    total = None
    for q in range(0, 8, 2):
        left = jnp.concatenate([blocks[pattern[block * 8 + q + k]] for k in range(2)], axis=1)
        right = jnp.concatenate([beside(coupling[0, q + k]) for k in range(2)], axis=0)
        part = dot_nn(left, right)
        total = part if total is None else total + part
    out[...] = times(solved[...] - fold(total), inverse[0])


def leaf_backward(coords, pattern, lows, x4m, x4o, x5m, x5o, solved, leaf_inverse, leaf_coupling):
    blocks = leaf_inverse.shape[0]
    whole = lambda array: pl.BlockSpec(array.shape, lambda b, *_: (0,) * array.ndim)
    gathered = [*lows, x4m, x4o, x5m, x5o]
    return pl.pallas_call(
        leaf_backward_kernel,
        name="leaf_backward",
        out_shape=jax.ShapeDtypeStruct((BLK, blocks * BLK), F32),
        grid_spec=pltpu.PrefetchScalarGridSpec(
            num_scalar_prefetch=2,
            grid=(blocks,),
            in_specs=[whole(array) for array in gathered]
            + [
                pl.BlockSpec((BLK, BLK), lambda b, *_: (0, b)),
                pl.BlockSpec((1, BLK, BLK), lambda b, *_: (b, 0, 0)),
                pl.BlockSpec((1, 8, BLK, BLK), lambda b, *_: (b, 0, 0, 0)),
            ],
            out_specs=pl.BlockSpec((BLK, BLK), lambda b, *_: (0, b)),
            scratch_shapes=[pltpu.VMEM((62, 2 * BLK, BLK), BF16)],
        ),
        compiler_params=pltpu.CompilerParams(vmem_limit_bytes=VMEM_BYTES),
    )(coords, pattern, *gathered, solved, leaf_inverse, leaf_coupling)


def across(value, mask):
    return lax.ppermute(value, "leaf", [(i, i ^ mask) for i in range(32)])


def across_front(value, mask):
    return lax.ppermute(value, "front", [(i, i ^ mask) for i in range(4)])


def swap8(value):
    groups = [[s + c + 2 * p for p in range(8)] for s in (0, 16) for c in (0, 1)]
    return lax.all_to_all(value, "leaf", 0, 0, axis_index_groups=groups)


def swap16(value):
    groups = [[c + 2 * p for p in range(16)] for c in (0, 1)]
    return lax.all_to_all(value, "leaf", 0, 0, axis_index_groups=groups)


def local(
    load_leaf, leaf_inverse, leaf_coupling, leaf_pattern, load_sep, sep_inverse, sep_coupling
):
    leaf_at = lax.axis_index("leaf")
    coords = jnp.stack([leaf_at & 1, (leaf_at >> 1) & 3, leaf_at >> 3, lax.axis_index("front")])
    coords = coords.astype(jnp.int32)
    pattern = leaf_pattern.reshape(-1)
    one = (COLS, BLK)
    left = lambda count: pltpu.VMEM((count, 2 * COLS, BLK), BF16)

    own6 = jnp.concatenate([sep_inverse[0:2], sep_coupling[0:4]], axis=0)
    y6 = across(own6, 2)
    core6 = across(own6, 1)
    diagonal6 = across(y6, 1)
    group = [own6, core6, y6, diagonal6]

    solved_leaf, mine13, theirs13, mine45, theirs45 = leaf_forward(
        coords, pattern, load_leaf, leaf_inverse, leaf_coupling, load_sep
    )
    parts13 = front_parts(coords, mine13, across(theirs13, 1))
    parts13 = [parts13[0]] + [across_front(parts13[j], j) for j in (1, 2, 3)]
    keep, message = call(
        level12_message_kernel, "level12_message", coords, parts13, [(8, *one), (8, *one)]
    )
    solved12, message = call(
        level12_kernel,
        "level12",
        coords,
        [keep, across(message, 2), *group],
        [(9, *one), (9, *one)],
        scratch=[left(4), pltpu.VMEM((8, 128), F32)],
    )
    y3, y12, y12p = call(
        level3_kernel,
        "level3",
        coords,
        [solved12, across(message, 6), sep_inverse, sep_coupling],
        [one, (16, *one), (8, *one)],
        in_any=(3,),
        scratch=[*matrices(16), left(16)],
    )
    parts45 = front_parts(coords, mine45, across(theirs45, 1))
    parts45 = [parts45[0]] + [across_front(parts45[j], j) for j in (1, 2, 3)]
    operand, sums5 = call(
        level4_operand_kernel, "level4_operand", coords, [y3, *parts45], [(8, 2, *one), (16, *one)]
    )
    y3m = swap8(operand)
    r8 = across(y12p, 8)
    c8 = across(r8, 1)
    y3o = across(y3m, 1)
    (acc4,) = call(
        level4_before_kernel,
        "level4_before",
        coords,
        [y12, r8, c8, sep_coupling],
        [(2 * COLS, 2 * BLK)],
        in_any=(3,),
        scratch=[*matrices(32), left(32)],
    )
    y4, operand = call(
        level4_kernel,
        "level4",
        coords,
        [acc4, y3m, y3o, sums5, sep_inverse, sep_coupling],
        [one, (16, 2, *one)],
        in_any=(5,),
        scratch=[*matrices(16), left(16)],
    )
    y4m = swap16(operand)
    r24 = across(y12p, 24)
    r16 = across(r8, 24)
    c24 = across(r24, 1)
    c16 = across(r16, 1)
    z3m = across(y3m, 24)
    z3o = across(z3m, 1)
    y4o = across(y4m, 1)
    (acc5,) = call(
        level5_before_kernel,
        "level5_before",
        coords,
        [y12, r8, c8, r24, c24, r16, c16, y3m, y3o, z3m, z3o, sep_coupling],
        [(2 * COLS, 2 * BLK)],
        in_any=(11,),
        scratch=[*matrices(96), left(96)],
    )
    x5, operand = call(
        level5_kernel,
        "level5",
        coords,
        [acc5, y4m, y4o, sep_inverse, sep_coupling],
        [one, (16, 3, *one)],
        in_any=(4,),
        scratch=[*matrices(32), left(32)],
    )
    parts4 = swap16(operand)
    mine, theirs = call(
        level5_back_kernel,
        "level5_back",
        coords,
        [x5, sep_coupling],
        [(48, *one), (48, *one)],
        in_any=(1,),
        scratch=matrices(96),
    )
    keep_top, send_top = call(
        halves_kernel, "halves", coords, [mine, across(theirs, 1)], [(24, *one), (24, *one)]
    )
    top = across(send_top, 24)
    own, other, x5p = call(
        level4_sum_kernel, "level4_sum", coords, [parts4], [one, one, (16, *one)]
    )
    x4, mine, theirs = call(
        level4_back_kernel,
        "level4_back",
        coords,
        [y4, own, across(other, 1), sep_inverse, sep_coupling],
        [one, (24, *one), (24, *one)],
        in_any=(4,),
        scratch=matrices(48),
    )
    (operand,) = call(
        level3_operand_kernel,
        "level3_operand",
        coords,
        [x4, mine, across(theirs, 1), keep_top, top],
        [(8, 4, *one)],
    )
    parts3 = swap8(operand)
    x3, x4p, keep, message = call(
        level3_back_kernel,
        "level3_back",
        coords,
        [parts3, y3, sep_inverse, sep_coupling],
        [one, (8, *one), (8, *one), (9, *one)],
        in_any=(3,),
        scratch=[*matrices(16), pltpu.VMEM((16, *one), F32)],
    )
    (message,) = call(
        level3_sum_kernel, "level3_sum", coords, [keep, across(message, 6), x3], [(10, *one)]
    )
    x1, x2, x123 = call(
        level12_back_kernel,
        "level12_back",
        coords,
        [message, across(message, 1), across(message, 2), across(message, 3), solved12, *group],
        [one, one, (14, *one)],
        scratch=[left(4), pltpu.VMEM((8, *one), F32), pltpu.VMEM((8, 128), F32)],
    )
    lows = [x123] + [across_front(x123, j) for j in (1, 2, 3)]
    x4m = jnp.stack([x4p] + [across_front(x4p, j) for j in (1, 2, 3)])
    x5m = jnp.stack([x5p] + [across_front(x5p, j) for j in (1, 2, 3)])
    solution_leaf = leaf_backward(
        coords,
        pattern,
        lows,
        x4m,
        across(x4m, 1),
        x5m,
        across(x5m, 1),
        solved_leaf,
        leaf_inverse,
        leaf_coupling,
    )
    solution_sep = jnp.concatenate([x1, x2, x3, x4, x5], axis=1)
    return solution_leaf, solution_sep


def solution(mesh):
    return jax.shard_map(
        local,
        mesh=mesh,
        in_specs=(
            P(None, ("leaf", "front")),
            P(("leaf", "front"), None, None),
            P(("leaf", "front"), None, None, None),
            P(("leaf", "front"), None),
            P("front", "leaf"),
            P("leaf", None, None),
            P("leaf", None, None),
        ),
        out_specs=(P(None, ("leaf", "front")), P("front", "leaf")),
        check_vma=False,
    )
```

time: 356 us -> 231 us (0.65)
  waiting for transfers between devices: 175 us -> 66.7 us
  matrix products: 69.7 us -> 0 us
  Pallas kernels: 0 us -> 66.5 us
  local copies, waits for them, and re-layouts: 25.7 us -> 5.75 us
  blocking collectives: 0 us -> 16.1 us
    all_to_all x10 -> x3, waiting for transfers between devices: 159 us -> 16.9 us  [the longest x2 9.12 us: swap8(): return lax.all_to_all(value, 'leaf', 0, 0, axis_index_groups=groups)]
    dot_general x36 -> x0, matrix products: 69.7 us -> none  [the longest x10 21.5 us: local(): jnp.einsum('ro,moi->rmi', own_final[higher_level - 1], sep_coupling[posit...]
    pallas_call x0 -> x20, Pallas kernels: none -> 66.5 us  [the longest x18 40.9 us: call(): pl.pallas_call(body, name=name, out_shape=[jax.ShapeDtypeStruct(shape, F3...]
    all_to_all x10 -> x3, starting transfers between devices: 62.3 us -> 14 us  [the longest x2 8.61 us: swap8(): return lax.all_to_all(value, 'leaf', 0, 0, axis_index_groups=groups)]
    ppermute x10 -> x42, starting transfers between devices: 12.6 us -> 57.7 us  [the longest x27 37.8 us: across(): return lax.ppermute(value, 'leaf', [(i, i ^ mask) for i in range(32)])]
    ppermute x10 -> x42, waiting for transfers between devices: 15.9 us -> 49.8 us  [the longest x27 30.6 us: across(): return lax.ppermute(value, 'leaf', [(i, i ^ mask) for i in range(32)])]
    all_to_all x0 -> x1, blocking collectives: none -> 16.1 us  [swap16(): return lax.all_to_all(value, 'leaf', 0, 0, axis_index_groups=groups)]
    reshape x5 -> x1, local copies, waits for them, and re-layouts: 12.1 us -> 0.08 us  [local(): pattern = leaf_pattern.reshape(-1)]
  transfers between devices with their start and end apart: 20 -> 45, of which waited for: 14 -> 21; matrix products, arithmetic and copies ran while one was open for 9% -> 1% of each run, Pallas kernels for 0% -> 12%
where the time goes in v2:
time: 231 us; the launch traced here: 229 us
  starting transfers between devices  71.6 us (31%)
  waiting for transfers between devices  66.7 us (29%)
  Pallas kernels  66.5 us (29%)
  blocking collectives  16.1 us (7%)
  local copies, waits for them, and re-layouts  5.75 us (2%)
    pallas_call x18, Pallas kernels, call(): pl.pallas_call(body, name=name, out_shape=[jax.ShapeDtypeStruct(shape, F3...  40.9 us
    ppermute x27, starting transfers between devices, across(): return lax.ppermute(value, 'leaf', [(i, i ^ mask) for i in range(32)])  37.8 us
    ppermute x27, waiting for transfers between devices, across(): return lax.ppermute(value, 'leaf', [(i, i ^ mask) for i in range(32)])  30.6 us
    ppermute x15, starting transfers between devices, across_front(): return lax.ppermute(value, 'front', [(i, i ^ mask) for i in range(4)])  19.9 us
    ppermute x15, waiting for transfers between devices, across_front(): return lax.ppermute(value, 'front', [(i, i ^ mask) for i in range(4)])  19.1 us
    all_to_all x1, blocking collectives, swap16(): return lax.all_to_all(value, 'leaf', 0, 0, axis_index_groups=groups)  16.1 us
    pallas_call x1, Pallas kernels, leaf_forward(): pl.pallas_call(leaf_forward_kernel, name='leaf_forward', out_shape=[jax.S...  13.3 us
    pallas_call x1, Pallas kernels, leaf_backward(): pl.pallas_call(leaf_backward_kernel, name='leaf_backward', out_shape=jax....  12.3 us
  transfers between devices with their start and end apart: 45, of which 21 were waited for; matrix products, arithmetic and copies ran while one was open for 1% of the time, Pallas kernels for 12%

profile of v2, /device:TPU:1, one launch (start us, length us, event | category | flops | bytes accessed | tf_op | source)
XLA Modules:
  0.0 229.1 jit_solution(16690796424198689139)
XLA Ops:
  4.7 13.3 %leaf_forward.1 = (f32[128,1536]{1,0:T(8,128)S(1)}, f32[10,128,128]{2,1,0:T(8,128)S(1)}, f32[10,128,128]{2,1,0:T(8,128)S(1)}, f32[24,128,128]{2,1,0:T(8,128)S(1)}, f32[24,128,128]{2,1,0:T(8,128)}) custom-call(s32[4]{0:T(128)S(1)} %pad_add_fusion.coords, s32[96]{0:T(128)S(1)} %reshape.7.pattern, f32[128,1536]{1,0:T(8,128)S(1)} %copy-done.3, ...), custom_call_target="tpu_custom_call" | custom-call | tf_op jit(solution)/shard_map/leaf_forward/pallas_call | solution.py:161
  25.7 3.3 %collective-permute-start.2 = (f32[10,32,128]{2,1,0:T(8,128)S(1)}, f32[10,32,128]{2,1,0:T(8,128)S(1)}, u32[]{:S(2)}, u32[]{:S(2)}) collective-permute-start(f32[10,32,128]{2,1,0:T(8,128)S(1)} %get-tuple-element.49), channel_id=1, source_target_pairs={{0,2},{1,3},{2,0},{3,1},{4,6},{5,7},{6,4},{7,5},{8,10},{9,11},{10,... | collective-permute-start | bytes 491528 | tf_op jit(solution)/shard_map/ppermute | solution.py:525
  29.5 4.0 %collective-permute-start.3 = (f32[10,32,128]{2,1,0:T(8,128)S(1)}, f32[10,32,128]{2,1,0:T(8,128)S(1)}, u32[]{:S(2)}, u32[]{:S(2)}) collective-permute-start(f32[10,32,128]{2,1,0:T(8,128)S(1)} %get-tuple-element.50), channel_id=1, source_target_pairs={{0,3},{1,2},{2,1},{3,0},{4,7},{5,6},{6,5},{7,4},{8,11},{9,10},{10,... | collective-permute-start | bytes 491528 | tf_op jit(solution)/shard_map/ppermute | solution.py:525
  37.0 3.6 %collective-permute-done.3.part3 = f32[10,32,128]{2,1,0:T(8,128)S(1)} collective-permute-done((f32[10,32,128]{2,1,0:T(8,128)S(1)}, f32[10,32,128]{2,1,0:T(8,128)S(1)}, u32[]{:S(2)}, u32[]{:S(2)}) %collective-permute-start.3) | collective-permute-done | bytes 163872 | tf_op jit(solution)/shard_map/ppermute | solution.py:525
  42.6 2.8 %collective-permute-done.4.received = f32[8,32,128]{2,1,0:T(8,128)S(1)} collective-permute-done((f32[8,32,128]{2,1,0:T(8,128)S(1)}, f32[8,32,128]{2,1,0:T(8,128)S(1)}, u32[]{:S(2)}, u32[]{:S(2)}) %collective-permute-start.4) | collective-permute-done | bytes 131104 | tf_op jit(solution)/shard_map/ppermute | solution.py:521
  47.4 2.8 %collective-permute-start.8 = (f32[9,32,128]{2,1,0:T(8,128)S(1)}, f32[9,32,128]{2,1,0:T(8,128)S(1)}, u32[]{:S(2)}, u32[]{:S(2)}) collective-permute-start(f32[9,32,128]{2,1,0:T(8,128)S(1)} %get-tuple-element.54), channel_id=1, source_target_pairs={{0,24},{4,28},{8,16},{12,20},{16,8},{20,12},{24,0},{28,4},{32,56},... | collective-permute-start | bytes 442376 | tf_op jit(solution)/shard_map/ppermute | solution.py:521
  50.2 2.8 %collective-permute-done.8.received = f32[9,32,128]{2,1,0:T(8,128)S(1)} collective-permute-done((f32[9,32,128]{2,1,0:T(8,128)S(1)}, f32[9,32,128]{2,1,0:T(8,128)S(1)}, u32[]{:S(2)}, u32[]{:S(2)}) %collective-permute-start.8) | collective-permute-done | bytes 147488 | tf_op jit(solution)/shard_map/ppermute | solution.py:521
  55.4 5.1 %collective-permute-done.14.part3 = f32[24,32,128]{2,1,0:T(8,128)S(1)} collective-permute-done((f32[24,32,128]{2,1,0:T(8,128)S(1)}, f32[24,32,128]{2,1,0:T(8,128)S(1)}, u32[]{:S(2)}, u32[]{:S(2)}) %collective-permute-start.14) | collective-permute-done | bytes 393248 | tf_op jit(solution)/shard_map/ppermute | solution.py:525
  61.9 5.1 %all-to-all-start = ((f32[8,2,32,128]{3,2,1,0:T(8,128)}), f32[8,2,32,128]{3,2,1,0:T(8,128)S(1)}, u32[]{:S(2)}, u32[]{:S(2)}) async-start(f32[8,2,32,128]{3,2,1,0:T(8,128)} %get-tuple-element.64), calls=%async_computation | async-start | bytes 524288 | tf_op jit(solution)/shard_map/all_to_all | solution.py:530
  68.5 4.6 %all-to-all-done.mine.y3m = f32[8,2,32,128]{3,2,1,0:T(8,128)S(1)} async-done(((f32[8,2,32,128]{3,2,1,0:T(8,128)}), f32[8,2,32,128]{3,2,1,0:T(8,128)S(1)}, u32[]{:S(2)}, u32[]{:S(2)}) %all-to-all-start) | async-done | bytes 262176 | tf_op jit(solution)/shard_map/all_to_all | solution.py:530
  73.1 3.4 %collective-permute-start.15 = (f32[8,2,32,128]{3,2,1,0:T(8,128)S(1)}, f32[8,2,32,128]{3,2,1,0:T(8,128)S(1)}, u32[]{:S(2)}, u32[]{:S(2)}) collective-permute-start(f32[8,2,32,128]{3,2,1,0:T(8,128)S(1)} %all-to-all-done.mine.y3m), channel_id=1, source_target_pairs={{0,4},{4,0},{8,12},{12,8},{16,20},{20,16},{24,28},{28,24},{32,36},... | collective-permute-start | bytes 786440 | tf_op jit(solution)/shard_map/ppermute | solution.py:521
  77.8 2.8 %level4_before.1.acc = f32[64,256]{1,0:T(8,128)S(1)} custom-call(s32[4]{0:T(128)S(1)} %pad_add_fusion.coords, f32[16,32,128]{2,1,0:T(8,128)S(1)} %get-tuple-element.55.y12, f32[8,32,128]{2,1,0:T(8,128)S(1)} %collective-permute-done.9.r8, f32[8,32,128]{2,1,0:T(8,128)S(1)} %collective-permute-done.10.c8, f32[196,128,128]{2,1,0:T(8,128)} %coupling.18), custom_call_target="tpu_custom_call" | custom-call | bytes 1048576 | tf_op jit(solution)/shard_map/level4_before/pallas_call | solution.py:81
  83.9 5.4 %all-to-all-start.1 = ((f32[16,2,32,128]{3,2,1,0:T(8,128)}), f32[16,2,32,128]{3,2,1,0:T(8,128)S(1)}, u32[]{:S(2)}, u32[]{:S(2)}) async-start(f32[16,2,32,128]{3,2,1,0:T(8,128)} %copy-done.8), calls=%async_computation.1 | async-start | bytes 1048576 | tf_op jit(solution)/shard_map/all_to_all | solution.py:535
  91.8 7.8 %all-to-all-done.1.mine = f32[16,2,32,128]{3,2,1,0:T(8,128)S(1)} async-done(((f32[16,2,32,128]{3,2,1,0:T(8,128)}), f32[16,2,32,128]{3,2,1,0:T(8,128)S(1)}, u32[]{:S(2)}, u32[]{:S(2)}) %all-to-all-start.1) | async-done | bytes 524320 | tf_op jit(solution)/shard_map/all_to_all | solution.py:535
  99.6 2.8 %collective-permute-start.22 = (f32[16,2,32,128]{3,2,1,0:T(8,128)S(1)}, f32[16,2,32,128]{3,2,1,0:T(8,128)S(1)}, u32[]{:S(2)}, u32[]{:S(2)}) collective-permute-start(f32[16,2,32,128]{3,2,1,0:T(8,128)S(1)} %all-to-all-done.1.mine), channel_id=1, source_target_pairs={{0,4},{4,0},{8,12},{12,8},{16,20},{20,16},{24,28},{28,24},{32,36},... | collective-permute-start | bytes 1572872 | tf_op jit(solution)/shard_map/ppermute | solution.py:521
  105.7 3.3 %collective-permute-done.16.r24 = f32[8,32,128]{2,1,0:T(8,128)S(1)} collective-permute-done((f32[8,32,128]{2,1,0:T(8,128)}, f32[8,32,128]{2,1,0:T(8,128)S(1)}, u32[]{:S(2)}, u32[]{:S(2)}) %collective-permute-start.16) | collective-permute-done | bytes 131104 | tf_op jit(solution)/shard_map/ppermute | solution.py:521
  113.6 7.9 %level5_before.1.acc = f32[64,256]{1,0:T(8,128)S(1)} custom-call(s32[4]{0:T(128)S(1)} %pad_add_fusion.coords, f32[16,32,128]{2,1,0:T(8,128)S(1)} %get-tuple-element.55.y12, f32[8,32,128]{2,1,0:T(8,128)S(1)} %collective-permute-done.9.r8, f32[8,32,128]{2,1,0:T(8,128)S(1)} %collective-permute-done.10.c8, f32[8,32,128]{2,1,0:T(8,128)S(1)} %collective-permute-done.16.r24, ...), custom_call_target="tpu_custom_call" | custom-call | bytes 1048576 | tf_op jit(solution)/shard_map/level5_before/pallas_call | solution.py:81
  121.5 4.0 %level5.1 = (f32[32,128]{1,0:T(8,128)S(1)}, f32[16,3,32,128]{3,2,1,0:T(8,128)S(1)}) custom-call(s32[4]{0:T(128)S(1)} %pad_add_fusion.coords, f32[64,256]{1,0:T(8,128)S(1)} %level5_before.1.acc, f32[16,2,32,128]{3,2,1,0:T(8,128)S(1)} %all-to-all-done.1.mine, f32[16,2,32,128]{3,2,1,0:T(8,128)S(1)} %collective-permute-done.22.other, ...), custom_call_target="tpu_custom_call" | custom-call | bytes 1048576 | tf_op jit(solution)/shard_map/level5/pallas_call | solution.py:81
  125.5 6.0 %level5_back.1 = (f32[48,32,128]{2,1,0:T(8,128)S(1)}, f32[48,32,128]{2,1,0:T(8,128)S(1)}) custom-call(s32[4]{0:T(128)S(1)} %pad_add_fusion.coords, f32[32,128]{1,0:T(8,128)S(1)} %get-tuple-element.74.x5, f32[196,128,128]{2,1,0:T(8,128)} %coupling.18), custom_call_target="tpu_custom_call" | custom-call | bytes 1048576 | tf_op jit(solution)/shard_map/level5_back/pallas_call | solution.py:81
  131.9 16.1 %all_to_all.20.parts = f32[16,3,32,128]{3,2,1,0:T(8,128)S(1)} all-to-all(f32[16,3,32,128]{3,2,1,0:T(8,128)S(1)} %get-tuple-element.68), channel_id=1, replica_groups={{0,8,16,24,32,40,48,56,64,72,80,88,96,104,112,120},{4,12,20,28,36,44,52..., dimensions={0} | all-to-all | bytes 1572864 | tf_op jit(solution)/shard_map/all_to_all | solution.py:535
  151.1 3.1 %level4_back.1 = (f32[32,128]{1,0:T(8,128)S(1)}, f32[24,32,128]{2,1,0:T(8,128)S(1)}, f32[24,32,128]{2,1,0:T(8,128)S(1)}) custom-call(s32[4]{0:T(128)S(1)} %pad_add_fusion.coords, f32[32,128]{1,0:T(8,128)S(1)} %get-tuple-element.66.y4, f32[32,128]{1,0:T(8,128)S(1)} %get-tuple-element.69.own, f32[32,128]{1,0:T(8,128)S(1)} %collective-permute-done.23.received, ...), custom_call_target="tpu_custom_call" | custom-call | bytes 1048576 | tf_op jit(solution)/shard_map/level4_back/pallas_call | solution.py:81
  158.8 8.4 %collective-permute-done.26.top = f32[24,32,128]{2,1,0:T(8,128)S(1)} collective-permute-done((f32[24,32,128]{2,1,0:T(8,128)S(1)}, f32[24,32,128]{2,1,0:T(8,128)S(1)}, u32[]{:S(2)}, u32[]{:S(2)}) %collective-permute-start.26) | collective-permute-done | bytes 393248 | tf_op jit(solution)/shard_map/ppermute | solution.py:521
  168.6 3.5 %all-to-all-start.3 = ((f32[8,4,32,128]{3,2,1,0:T(8,128)}), f32[8,4,32,128]{3,2,1,0:T(8,128)S(1)}, u32[]{:S(2)}, u32[]{:S(2)}) async-start(f32[8,4,32,128]{3,2,1,0:T(8,128)} %level3_operand.1), calls=%async_computation.3 | async-start | bytes 1048576 | tf_op jit(solution)/shard_map/all_to_all | solution.py:530
  175.3 4.5 %all-to-all-done.3.parts = f32[8,4,32,128]{3,2,1,0:T(8,128)S(1)} async-done(((f32[8,4,32,128]{3,2,1,0:T(8,128)}), f32[8,4,32,128]{3,2,1,0:T(8,128)S(1)}, u32[]{:S(2)}, u32[]{:S(2)}) %all-to-all-start.3) | async-done | bytes 524320 | tf_op jit(solution)/shard_map/all_to_all | solution.py:530
  184.5 3.1 %collective-permute-start.36 = (f32[8,32,128]{2,1,0:T(8,128)S(1)}, f32[8,32,128]{2,1,0:T(8,128)S(1)}, u32[]{:S(2)}, u32[]{:S(2)}) collective-permute-start(f32[8,32,128]{2,1,0:T(8,128)S(1)} %get-tuple-element.83), channel_id=1, source_target_pairs={{0,3},{1,2},{2,1},{3,0},{4,7},{5,6},{6,5},{7,4},{8,11},{9,10},{10,... | collective-permute-start | bytes 393224 | tf_op jit(solution)/shard_map/ppermute | solution.py:525
  188.2 3.6 %collective-permute-start.28 = (f32[10,32,128]{2,1,0:T(8,128)S(1)}, f32[10,32,128]{2,1,0:T(8,128)S(1)}, u32[]{:S(2)}, u32[]{:S(2)}) collective-permute-start(f32[10,32,128]{2,1,0:T(8,128)S(1)} %level3_sum.1.m0), channel_id=1, source_target_pairs={{0,4},{4,0},{8,12},{12,8},{16,20},{20,16},{24,28},{28,24},{32,36},... | collective-permute-start | bytes 491528 | tf_op jit(solution)/shard_map/ppermute | solution.py:521
  194.5 3.1 %collective-permute-done.29.m2 = f32[10,32,128]{2,1,0:T(8,128)S(1)} collective-permute-done((f32[10,32,128]{2,1,0:T(8,128)S(1)}, f32[10,32,128]{2,1,0:T(8,128)S(1)}, u32[]{:S(2)}, u32[]{:S(2)}) %collective-permute-start.29) | collective-permute-done | bytes 163872 | tf_op jit(solution)/shard_map/ppermute | solution.py:521
  197.6 3.7 %collective-permute-done.30.m3 = f32[10,32,128]{2,1,0:T(8,128)S(1)} collective-permute-done((f32[10,32,128]{2,1,0:T(8,128)S(1)}, f32[10,32,128]{2,1,0:T(8,128)S(1)}, u32[]{:S(2)}, u32[]{:S(2)}) %collective-permute-start.30) | collective-permute-done | bytes 163872 | tf_op jit(solution)/shard_map/ppermute | solution.py:521
  204.2 2.8 %collective-permute-start.33 = (f32[14,32,128]{2,1,0:T(8,128)S(1)}, f32[14,32,128]{2,1,0:T(8,128)S(1)}, u32[]{:S(2)}, u32[]{:S(2)}) collective-permute-start(f32[14,32,128]{2,1,0:T(8,128)S(1)} %get-tuple-element.82.low0), channel_id=1, source_target_pairs={{0,3},{1,2},{2,1},{3,0},{4,7},{5,6},{6,5},{7,4},{8,11},{9,10},{10,... | collective-permute-start | bytes 688136 | tf_op jit(solution)/shard_map/ppermute | solution.py:525
  207.0 3.1 %collective-permute-done.31.low1 = f32[14,32,128]{2,1,0:T(8,128)S(1)} collective-permute-done((f32[14,32,128]{2,1,0:T(8,128)S(1)}, f32[14,32,128]{2,1,0:T(8,128)S(1)}, u32[]{:S(2)}, u32[]{:S(2)}) %collective-permute-start.31) | collective-permute-done | bytes 229408 | tf_op jit(solution)/shard_map/ppermute | solution.py:525
  210.1 4.3 %collective-permute-done.32.low2 = f32[14,32,128]{2,1,0:T(8,128)S(1)} collective-permute-done((f32[14,32,128]{2,1,0:T(8,128)S(1)}, f32[14,32,128]{2,1,0:T(8,128)S(1)}, u32[]{:S(2)}, u32[]{:S(2)}) %collective-permute-start.32) | collective-permute-done | bytes 229408 | tf_op jit(solution)/shard_map/ppermute | solution.py:525
  216.8 12.3 %leaf_backward.1 = f32[128,1536]{1,0:T(8,128)} custom-call(s32[4]{0:T(128)S(1)} %pad_add_fusion.coords, s32[96]{0:T(128)S(1)} %reshape.7.pattern, f32[14,32,128]{2,1,0:T(8,128)S(1)} %get-tuple-element.82.low0, f32[14,32,128]{2,1,0:T(8,128)S(1)} %collective-permute-done.31.low1, f32[14,32,128]{2,1,0:T(8,128)S(1)} %collective-permute-done.32.low2, ...), custom_call_target="tpu_custom_call" | custom-call | tf_op jit(solution)/shard_map/leaf_backward/pallas_call | solution.py:500
  (130 shorter events, 65.6 us)
Async XLA Ops:
  18.0 15.5 %collective-permute-start.11 = (f32[24,128,128]{2,1,0:T(8,128)}, f32[24,128,128]{2,1,0:T(8,128)S(1)}, u32[]{:S(2)}, u32[]{:S(2)}) collective-permute-start(f32[24,128,128]{2,1,0:T(8,128)} %get-tuple-element.59), channel_id=1, source_target_pairs={{0,4},{4,0},{8,12},{12,8},{16,20},{20,16},{24,28},{28,24},{32,36},... | collective-permute-start | bytes 4718600 | tf_op jit(solution)/shard_map/ppermute | solution.py:521
  19.5 10.0 %collective-permute-start.6 = (f32[6,128,128]{2,1,0:T(8,128)S(1)}, f32[6,128,128]{2,1,0:T(8,128)S(1)}, u32[]{:S(2)}, u32[]{:S(2)}) collective-permute-start(f32[6,128,128]{2,1,0:T(8,128)S(1)} %pad_maximum_fusion.2.own6), channel_id=1, source_target_pairs={{0,8},{4,12},{8,0},{12,4},{16,24},{20,28},{24,16},{28,20},{32,40},... | collective-permute-start | bytes 1179656 | tf_op jit(solution)/shard_map/ppermute | solution.py:521
  21.0 20.2 %collective-permute-start.5 = (f32[6,128,128]{2,1,0:T(8,128)S(1)}, f32[6,128,128]{2,1,0:T(8,128)S(1)}, u32[]{:S(2)}, u32[]{:S(2)}) collective-permute-start(f32[6,128,128]{2,1,0:T(8,128)S(1)} %pad_maximum_fusion.2.own6), channel_id=1, source_target_pairs={{0,4},{4,0},{8,12},{12,8},{16,20},{20,16},{24,28},{28,24},{32,36},... | collective-permute-start | bytes 1179656 | tf_op jit(solution)/shard_map/ppermute | solution.py:521
  23.9 12.1 %collective-permute-start.1 = (f32[10,32,128]{2,1,0:T(8,128)S(1)}, f32[10,32,128]{2,1,0:T(8,128)S(1)}, u32[]{:S(2)}, u32[]{:S(2)}) collective-permute-start(f32[10,32,128]{2,1,0:T(8,128)S(1)} %get-tuple-element.48), channel_id=1, source_target_pairs={{0,1},{1,0},{2,3},{3,2},{4,5},{5,4},{6,7},{7,6},{8,9},{9,8},{10,11... | collective-permute-start | bytes 491528 | tf_op jit(solution)/shard_map/ppermute | solution.py:525
  25.7 11.1 %collective-permute-start.2 = (f32[10,32,128]{2,1,0:T(8,128)S(1)}, f32[10,32,128]{2,1,0:T(8,128)S(1)}, u32[]{:S(2)}, u32[]{:S(2)}) collective-permute-start(f32[10,32,128]{2,1,0:T(8,128)S(1)} %get-tuple-element.49), channel_id=1, source_target_pairs={{0,2},{1,3},{2,0},{3,1},{4,6},{5,7},{6,4},{7,5},{8,10},{9,11},{10,... | collective-permute-start | bytes 491528 | tf_op jit(solution)/shard_map/ppermute | solution.py:525
  29.5 11.2 %collective-permute-start.3 = (f32[10,32,128]{2,1,0:T(8,128)S(1)}, f32[10,32,128]{2,1,0:T(8,128)S(1)}, u32[]{:S(2)}, u32[]{:S(2)}) collective-permute-start(f32[10,32,128]{2,1,0:T(8,128)S(1)} %get-tuple-element.50), channel_id=1, source_target_pairs={{0,3},{1,2},{2,1},{3,0},{4,7},{5,6},{6,5},{7,4},{8,11},{9,10},{10,... | collective-permute-start | bytes 491528 | tf_op jit(solution)/shard_map/ppermute | solution.py:525
  33.5 9.2 %collective-permute-start.7 = (f32[6,128,128]{2,1,0:T(8,128)S(1)}, f32[6,128,128]{2,1,0:T(8,128)S(1)}, u32[]{:S(2)}, u32[]{:S(2)}) collective-permute-start(f32[6,128,128]{2,1,0:T(8,128)S(1)} %collective-permute-done.6.y6), channel_id=1, source_target_pairs={{0,4},{4,0},{8,12},{12,8},{16,20},{20,16},{24,28},{28,24},{32,36},... | collective-permute-start | bytes 1179656 | tf_op jit(solution)/shard_map/ppermute | solution.py:521
  36.0 19.4 %collective-permute-start.12 = (f32[24,32,128]{2,1,0:T(8,128)S(1)}, f32[24,32,128]{2,1,0:T(8,128)S(1)}, u32[]{:S(2)}, u32[]{:S(2)}) collective-permute-start(f32[24,32,128]{2,1,0:T(8,128)S(1)} %get-tuple-element.61), channel_id=1, source_target_pairs={{0,1},{1,0},{2,3},{3,2},{4,5},{5,4},{6,7},{7,6},{8,9},{9,8},{10,11... | collective-permute-start | bytes 1179656 | tf_op jit(solution)/shard_map/ppermute | solution.py:525
  36.7 18.7 %collective-permute-start.13 = (f32[24,32,128]{2,1,0:T(8,128)S(1)}, f32[24,32,128]{2,1,0:T(8,128)S(1)}, u32[]{:S(2)}, u32[]{:S(2)}) collective-permute-start(f32[24,32,128]{2,1,0:T(8,128)S(1)} %get-tuple-element.62), channel_id=1, source_target_pairs={{0,2},{1,3},{2,0},{3,1},{4,6},{5,7},{6,4},{7,5},{8,10},{9,11},{10,... | collective-permute-start | bytes 1179656 | tf_op jit(solution)/shard_map/ppermute | solution.py:525
  40.7 19.8 %collective-permute-start.14 = (f32[24,32,128]{2,1,0:T(8,128)S(1)}, f32[24,32,128]{2,1,0:T(8,128)S(1)}, u32[]{:S(2)}, u32[]{:S(2)}) collective-permute-start(f32[24,32,128]{2,1,0:T(8,128)S(1)} %get-tuple-element.63), channel_id=1, source_target_pairs={{0,3},{1,2},{2,1},{3,0},{4,7},{5,6},{6,5},{7,4},{8,11},{9,10},{10,... | collective-permute-start | bytes 1179656 | tf_op jit(solution)/shard_map/ppermute | solution.py:525
  61.9 11.2 %all-to-all-start = ((f32[8,2,32,128]{3,2,1,0:T(8,128)}), f32[8,2,32,128]{3,2,1,0:T(8,128)S(1)}, u32[]{:S(2)}, u32[]{:S(2)}) async-start(f32[8,2,32,128]{3,2,1,0:T(8,128)} %get-tuple-element.64), calls=%async_computation | async-start | bytes 524288 | tf_op jit(solution)/shard_map/all_to_all | solution.py:530
  67.0 9.5 %collective-permute-start.9 = (f32[8,32,128]{2,1,0:T(8,128)S(1)}, f32[8,32,128]{2,1,0:T(8,128)S(1)}, u32[]{:S(2)}, u32[]{:S(2)}) collective-permute-start(f32[8,32,128]{2,1,0:T(8,128)S(1)} %get-tuple-element.56), channel_id=1, source_target_pairs={{0,32},{4,36},{8,40},{12,44},{16,48},{20,52},{24,56},{28,60},{32,0... | collective-permute-start | bytes 393224 | tf_op jit(solution)/shard_map/ppermute | solution.py:521
  73.1 7.6 %collective-permute-start.15 = (f32[8,2,32,128]{3,2,1,0:T(8,128)S(1)}, f32[8,2,32,128]{3,2,1,0:T(8,128)S(1)}, u32[]{:S(2)}, u32[]{:S(2)}) collective-permute-start(f32[8,2,32,128]{3,2,1,0:T(8,128)S(1)} %all-to-all-done.mine.y3m), channel_id=1, source_target_pairs={{0,4},{4,0},{8,12},{12,8},{16,20},{20,16},{24,28},{28,24},{32,36},... | collective-permute-start | bytes 786440 | tf_op jit(solution)/shard_map/ppermute | solution.py:521
  83.9 15.7 %all-to-all-start.1 = ((f32[16,2,32,128]{3,2,1,0:T(8,128)}), f32[16,2,32,128]{3,2,1,0:T(8,128)S(1)}, u32[]{:S(2)}, u32[]{:S(2)}) async-start(f32[16,2,32,128]{3,2,1,0:T(8,128)} %copy-done.8), calls=%async_computation.1 | async-start | bytes 1048576 | tf_op jit(solution)/shard_map/all_to_all | solution.py:535
  89.2 15.9 %collective-permute-start.20 = (f32[8,2,32,128]{3,2,1,0:T(8,128)S(1)}, f32[8,2,32,128]{3,2,1,0:T(8,128)}, u32[]{:S(2)}, u32[]{:S(2)}) collective-permute-start(f32[8,2,32,128]{3,2,1,0:T(8,128)S(1)} %all-to-all-done.mine.y3m), channel_id=1, source_target_pairs={{0,96},{4,100},{8,104},{12,108},{16,112},{20,116},{24,120},{28,124... | collective-permute-start | bytes 786440 | tf_op jit(solution)/shard_map/ppermute | solution.py:521
  99.6 21.9 %collective-permute-start.22 = (f32[16,2,32,128]{3,2,1,0:T(8,128)S(1)}, f32[16,2,32,128]{3,2,1,0:T(8,128)S(1)}, u32[]{:S(2)}, u32[]{:S(2)}) collective-permute-start(f32[16,2,32,128]{3,2,1,0:T(8,128)S(1)} %all-to-all-done.1.mine), channel_id=1, source_target_pairs={{0,4},{4,0},{8,12},{12,8},{16,20},{20,16},{24,28},{28,24},{32,36},... | collective-permute-start | bytes 1572872 | tf_op jit(solution)/shard_map/ppermute | solution.py:521
  102.5 9.3 %collective-permute-start.18 = (f32[8,32,128]{2,1,0:T(8,128)S(1)}, f32[8,32,128]{2,1,0:T(8,128)S(1)}, u32[]{:S(2)}, u32[]{:S(2)}) collective-permute-start(f32[8,32,128]{2,1,0:T(8,128)S(1)} %collective-permute-done.9.r8), channel_id=1, source_target_pairs={{0,96},{4,100},{8,104},{12,108},{16,112},{20,116},{24,120},{28,124... | collective-permute-start | bytes 393224 | tf_op jit(solution)/shard_map/ppermute | solution.py:521
  105.1 8.5 %collective-permute-start.21 = (f32[8,2,32,128]{3,2,1,0:T(8,128)}, f32[8,2,32,128]{3,2,1,0:T(8,128)S(1)}, u32[]{:S(2)}, u32[]{:S(2)}) collective-permute-start(f32[8,2,32,128]{3,2,1,0:T(8,128)} %collective-permute-done.20.z3m), channel_id=1, source_target_pairs={{0,4},{4,0},{8,12},{12,8},{16,20},{20,16},{24,28},{28,24},{32,36},... | collective-permute-start | bytes 786440 | tf_op jit(solution)/shard_map/ppermute | solution.py:521
  131.5 23.1 %collective-permute-start.25 = (f32[48,32,128]{2,1,0:T(8,128)S(1)}, f32[48,32,128]{2,1,0:T(8,128)S(1)}, u32[]{:S(2)}, u32[]{:S(2)}) collective-permute-start(f32[48,32,128]{2,1,0:T(8,128)S(1)} %get-tuple-element.76), channel_id=1, source_target_pairs={{0,4},{4,0},{8,12},{12,8},{16,20},{20,16},{24,28},{28,24},{32,36},... | collective-permute-start | bytes 2359304 | tf_op jit(solution)/shard_map/ppermute | solution.py:521
  155.3 11.9 %collective-permute-start.26 = (f32[24,32,128]{2,1,0:T(8,128)S(1)}, f32[24,32,128]{2,1,0:T(8,128)S(1)}, u32[]{:S(2)}, u32[]{:S(2)}) collective-permute-start(f32[24,32,128]{2,1,0:T(8,128)S(1)} %get-tuple-element.78), channel_id=1, source_target_pairs={{0,96},{4,100},{8,104},{12,108},{16,112},{20,116},{24,120},{28,124... | collective-permute-start | bytes 1179656 | tf_op jit(solution)/shard_map/ppermute | solution.py:521
  156.1 16.0 %collective-permute-start.39 = (f32[16,32,128]{2,1,0:T(8,128)S(1)}, f32[16,32,128]{2,1,0:T(8,128)S(1)}, u32[]{:S(2)}, u32[]{:S(2)}) collective-permute-start(f32[16,32,128]{2,1,0:T(8,128)S(1)} %get-tuple-element.84), channel_id=1, source_target_pairs={{0,2},{1,3},{2,0},{3,1},{4,6},{5,7},{6,4},{7,5},{8,10},{9,11},{10,... | collective-permute-start | bytes 786440 | tf_op jit(solution)/shard_map/ppermute | solution.py:525
  156.1 16.0 %collective-permute-start.40 = (f32[16,32,128]{2,1,0:T(8,128)S(1)}, f32[16,32,128]{2,1,0:T(8,128)S(1)}, u32[]{:S(2)}, u32[]{:S(2)}) collective-permute-start(f32[16,32,128]{2,1,0:T(8,128)S(1)} %get-tuple-element.84), channel_id=1, source_target_pairs={{0,3},{1,2},{2,1},{3,0},{4,7},{5,6},{6,5},{7,4},{8,11},{9,10},{10,... | collective-permute-start | bytes 786440 | tf_op jit(solution)/shard_map/ppermute | solution.py:525
  156.8 15.3 %collective-permute-start.38 = (f32[16,32,128]{2,1,0:T(8,128)S(1)}, f32[16,32,128]{2,1,0:T(8,128)S(1)}, u32[]{:S(2)}, u32[]{:S(2)}) collective-permute-start(f32[16,32,128]{2,1,0:T(8,128)S(1)} %get-tuple-element.84), channel_id=1, source_target_pairs={{0,1},{1,0},{2,3},{3,2},{4,5},{5,4},{6,7},{7,6},{8,9},{9,8},{10,11... | collective-permute-start | bytes 786440 | tf_op jit(solution)/shard_map/ppermute | solution.py:525
  168.6 11.2 %all-to-all-start.3 = ((f32[8,4,32,128]{3,2,1,0:T(8,128)}), f32[8,4,32,128]{3,2,1,0:T(8,128)S(1)}, u32[]{:S(2)}, u32[]{:S(2)}) async-start(f32[8,4,32,128]{3,2,1,0:T(8,128)} %level3_operand.1), calls=%async_computation.3 | async-start | bytes 1048576 | tf_op jit(solution)/shard_map/all_to_all | solution.py:530
  174.3 32.8 %collective-permute-start.41 = (f32[4,16,32,128]{3,2,1,0:T(8,128)S(1)}, f32[4,16,32,128]{3,2,1,0:T(8,128)}, u32[]{:S(2)}, u32[]{:S(2)}) collective-permute-start(f32[4,16,32,128]{3,2,1,0:T(8,128)S(1)} %pad_maximum_fusion.x5m), channel_id=1, source_target_pairs={{0,4},{4,0},{8,12},{12,8},{16,20},{20,16},{24,28},{28,24},{32,36},... | collective-permute-start | bytes 3145736 | tf_op jit(solution)/shard_map/ppermute | solution.py:521
  183.8 8.0 %collective-permute-start.34 = (f32[8,32,128]{2,1,0:T(8,128)S(1)}, f32[8,32,128]{2,1,0:T(8,128)S(1)}, u32[]{:S(2)}, u32[]{:S(2)}) collective-permute-start(f32[8,32,128]{2,1,0:T(8,128)S(1)} %get-tuple-element.83), channel_id=1, source_target_pairs={{0,1},{1,0},{2,3},{3,2},{4,5},{5,4},{6,7},{7,6},{8,9},{9,8},{10,11... | collective-permute-start | bytes 393224 | tf_op jit(solution)/shard_map/ppermute | solution.py:525
  183.8 8.0 %collective-permute-start.35 = (f32[8,32,128]{2,1,0:T(8,128)S(1)}, f32[8,32,128]{2,1,0:T(8,128)S(1)}, u32[]{:S(2)}, u32[]{:S(2)}) collective-permute-start(f32[8,32,128]{2,1,0:T(8,128)S(1)} %get-tuple-element.83), channel_id=1, source_target_pairs={{0,2},{1,3},{2,0},{3,1},{4,6},{5,7},{6,4},{7,5},{8,10},{9,11},{10,... | collective-permute-start | bytes 393224 | tf_op jit(solution)/shard_map/ppermute | solution.py:525
  184.5 9.0 %collective-permute-start.36 = (f32[8,32,128]{2,1,0:T(8,128)S(1)}, f32[8,32,128]{2,1,0:T(8,128)S(1)}, u32[]{:S(2)}, u32[]{:S(2)}) collective-permute-start(f32[8,32,128]{2,1,0:T(8,128)S(1)} %get-tuple-element.83), channel_id=1, source_target_pairs={{0,3},{1,2},{2,1},{3,0},{4,7},{5,6},{6,5},{7,4},{8,11},{9,10},{10,... | collective-permute-start | bytes 393224 | tf_op jit(solution)/shard_map/ppermute | solution.py:525
  191.8 9.4 %collective-permute-start.30 = (f32[10,32,128]{2,1,0:T(8,128)S(1)}, f32[10,32,128]{2,1,0:T(8,128)S(1)}, u32[]{:S(2)}, u32[]{:S(2)}) collective-permute-start(f32[10,32,128]{2,1,0:T(8,128)S(1)} %level3_sum.1.m0), channel_id=1, source_target_pairs={{0,12},{4,8},{8,4},{12,0},{16,28},{20,24},{24,20},{28,16},{32,44},... | collective-permute-start | bytes 491528 | tf_op jit(solution)/shard_map/ppermute | solution.py:521
  193.6 23.2 %collective-permute-start.37 = (f32[4,8,32,128]{3,2,1,0:T(8,128)S(1)}, f32[4,8,32,128]{3,2,1,0:T(8,128)S(1)}, u32[]{:S(2)}, u32[]{:S(2)}) collective-permute-start(f32[4,8,32,128]{3,2,1,0:T(8,128)S(1)} %pad_maximum_fusion.1.x4m), channel_id=1, source_target_pairs={{0,4},{4,0},{8,12},{12,8},{16,20},{20,16},{24,28},{28,24},{32,36},... | collective-permute-start | bytes 1572872 | tf_op jit(solution)/shard_map/ppermute | solution.py:521
  203.1 11.3 %collective-permute-start.32 = (f32[14,32,128]{2,1,0:T(8,128)S(1)}, f32[14,32,128]{2,1,0:T(8,128)S(1)}, u32[]{:S(2)}, u32[]{:S(2)}) collective-permute-start(f32[14,32,128]{2,1,0:T(8,128)S(1)} %get-tuple-element.82.low0), channel_id=1, source_target_pairs={{0,2},{1,3},{2,0},{3,1},{4,6},{5,7},{6,4},{7,5},{8,10},{9,11},{10,... | collective-permute-start | bytes 688136 | tf_op jit(solution)/shard_map/ppermute | solution.py:525
  204.2 12.6 %collective-permute-start.33 = (f32[14,32,128]{2,1,0:T(8,128)S(1)}, f32[14,32,128]{2,1,0:T(8,128)S(1)}, u32[]{:S(2)}, u32[]{:S(2)}) collective-permute-start(f32[14,32,128]{2,1,0:T(8,128)S(1)} %get-tuple-element.82.low0), channel_id=1, source_target_pairs={{0,3},{1,2},{2,1},{3,0},{4,7},{5,6},{6,5},{7,4},{8,11},{9,10},{10,... | collective-permute-start | bytes 688136 | tf_op jit(solution)/shard_map/ppermute | solution.py:525
  (33 other events, 247.5 us)

commit v3 on v2

v3 whole, which is shorter than its diff:
```python
import jax
import jax.numpy as jnp
from jax import lax
from jax.experimental import pallas as pl
from jax.experimental.pallas import tpu as pltpu
from jax.sharding import PartitionSpec as P

F32 = jnp.float32
BF16 = jnp.bfloat16
BLK = 128
COLS = 32
VMEM_BYTES = 32 * 1024 * 1024
LARGE_VMEM_BYTES = 48 * 1024 * 1024
RUNS = {(2, 1): 0, (3, 1): 4, (3, 2): 12, (4, 1): 20, (4, 2): 36, (4, 3): 52}
RUNS |= {(5, 1): 68, (5, 2): 100, (5, 3): 132, (5, 4): 164}
CHUNK = 8


def split(value):
    high = value.astype(BF16)
    low = (value - high.astype(F32)).astype(BF16)
    return high, low


def stacked(value):
    return jnp.concatenate(split(value), axis=0)


def beside(value):
    return jnp.concatenate(split(value), axis=1)


def dot_nt(left, right):
    return lax.dot_general(left, right, (((1,), (1,)), ((), ())), preferred_element_type=F32)


def dot_nn(left, right):
    return lax.dot_general(left, right, (((1,), (0,)), ((), ())), preferred_element_type=F32)


def fold(terms):
    rows = terms.shape[0] // 2
    return (terms[:rows, :BLK] + terms[:rows, BLK:]) + (terms[rows:, :BLK] + terms[rows:, BLK:])


def times_transposed(value, matrix):
    return fold(dot_nt(stacked(value), stacked(matrix)))


def times(value, matrix):
    return fold(dot_nn(stacked(value), beside(matrix)))


def sum_times_transposed(lefts, matrices):
    total = None
    for k in range(0, len(lefts), 2):
        left = jnp.concatenate([lefts[k], lefts[k + 1]], axis=1)
        right = jnp.concatenate([stacked(matrices[k]), stacked(matrices[k + 1])], axis=1)
        part = dot_nt(left, right)
        total = part if total is None else total + part
    return total


def wide_left(value):
    both = stacked(value)
    return jnp.concatenate([both, both], axis=1)


def two_times(left, first, second):
    right = jnp.concatenate([stacked(first), stacked(second)], axis=1)
    out = dot_nn(left, right)
    rows = out.shape[0] // 2
    out = out[:rows] + out[rows:]
    return out[:, :BLK], out[:, BLK:]


def cost(us):
    return pl.CostEstimate(
        flops=int(us * 1e8), bytes_accessed=int(us * 3e5), transcendentals=0
    )


def call(
    body, name, coords, inputs, outs, us=1.0, in_hbm=(), after=(), through=(), scratch=(), limit=VMEM_BYTES
):
    count, results = len(inputs), len(outs)
    extra = len(after) + len(through)

    def kernel(coords_ref, *refs):
        refs = list(refs)
        del refs[count + extra + results : count + extra + results + len(through)]
        del refs[count : count + extra]
        body(coords_ref, *refs)

    anywhere = pl.BlockSpec(memory_space=pl.ANY)
    hbm = pl.BlockSpec(memory_space=pltpu.HBM)
    vmem = pl.BlockSpec(memory_space=pltpu.VMEM)
    specs = [hbm if k in in_hbm else vmem for k in range(count)] + [anywhere] * extra
    first = 1 + count + len(after)
    return pl.pallas_call(
        kernel,
        name=name,
        out_shape=[jax.ShapeDtypeStruct(shape, F32) for shape in outs]
        + [jax.ShapeDtypeStruct(array.shape, array.dtype) for array in through],
        grid_spec=pltpu.PrefetchScalarGridSpec(
            num_scalar_prefetch=1,
            grid=(1,),
            in_specs=specs,
            out_specs=[vmem] * results + [anywhere] * len(through),
            scratch_shapes=list(scratch),
        ),
        input_output_aliases={first + k: results + k for k in range(len(through))},
        compiler_params=pltpu.CompilerParams(vmem_limit_bytes=limit),
        cost_estimate=cost(us),
    )(coords, *inputs, *after, *through)


def fetch(source, first, count, target, sems):
    for k in range(0, count, CHUNK):
        pltpu.make_async_copy(
            source.at[pl.ds(first + k, CHUNK)], target.at[pl.ds(k, CHUNK)], sems.at[k // CHUNK]
        ).start()


def fetched(source, first, target, sems, k):
    pltpu.make_async_copy(
        source.at[pl.ds(first + k * CHUNK, CHUNK)], target.at[pl.ds(k * CHUNK, CHUNK)], sems.at[k]
    ).wait()


def matrices(count):
    return [pltpu.VMEM((count, BLK, BLK), F32), pltpu.SemaphoreType.DMA((count // CHUNK,))]


PER_COPY = 2


def leaf_copies(load, inverse, coupling, loads, inverses, couplings, sems, blocks):
    copies = [
        pltpu.make_async_copy(load, loads, sems.at[0]),
        pltpu.make_async_copy(inverse, inverses, sems.at[1]),
    ]
    for k in range(blocks // PER_COPY):
        part = pl.ds(k * PER_COPY, PER_COPY)
        copies.append(
            pltpu.make_async_copy(coupling.at[part], couplings.at[part], sems.at[2 + k])
        )
    return copies


def leaf_forward_kernel(
    coords, pattern, load, inverse, coupling, load_sep,
    mine13, theirs13, mine45, theirs45,
    loads, inverses, couplings, load_seps, solved, sums, columns, sems, sep_sem,
):
    blocks = couplings.shape[0]
    core, y_at, x_at, front = coords[0], coords[1], coords[2], coords[3]
    copies = leaf_copies(load, inverse, coupling, loads, inverses, couplings, sems, blocks)
    sep_copy = pltpu.make_async_copy(load_sep, load_seps, sep_sem)
    sep_copy.start()
    for copy in copies:
        copy.start()
    sums[...] = jnp.zeros_like(sums)
    columns[...] = jnp.zeros_like(columns)
    rows = pl.ds(pl.multiple_of(front * COLS, COLS), COLS)
    slots = (
        core,
        2 + (y_at & 1) * 2 + core,
        6 + y_at,
        10 + (x_at & 1) * 4 + y_at,
        18 + x_at * 4 + y_at,
    )
    sep_copy.wait()
    for level, slot in enumerate(slots):
        columns[rows, :] = -load_seps[:, level * BLK : (level + 1) * BLK]
        sums[slot] = columns[...].T
    copies[0].wait()
    copies[1].wait()
    for b in range(blocks):
        turned = fold(
            dot_nt(stacked(inverses[b]), stacked(loads[:, b * BLK : (b + 1) * BLK]))
        )
        solved[b] = beside(turned)

    for k in range(blocks // PER_COPY):
        copies[2 + k].wait()
        for b in range(k * PER_COPY, (k + 1) * PER_COPY):
            right = jnp.concatenate([solved[b], solved[b]], axis=0)
            left = jnp.concatenate([beside(couplings[b, q]) for q in range(8)], axis=0)
            out = dot_nn(left, right)
            out = out[:, :BLK] + out[:, BLK:]
            for q in range(8):
                index = pattern[b, q]
                slot = jnp.where(index < 6, index, 6 + ((index - 6) >> 1))
                slot = jnp.where((index >= 6) & ((index & 1) != core), slot + 34, slot)
                sums[slot] += out[q * BLK : (q + 1) * BLK]

    mine13[...] = sums[0:10]
    theirs13[0:6] = sums[0:6]
    theirs13[6:10] = sums[40:44]
    mine45[...] = sums[10:34]
    theirs45[...] = sums[44:68]


def leaf_forward(coords, pattern, load_leaf, leaf_inverse, leaf_coupling, load_sep):
    blocks = leaf_inverse.shape[0]
    outs = [(10, BLK, BLK), (10, BLK, BLK), (24, BLK, BLK), (24, BLK, BLK)]
    vmem = pl.BlockSpec(memory_space=pltpu.VMEM)
    return pl.pallas_call(
        leaf_forward_kernel,
        name="leaf_forward",
        out_shape=[jax.ShapeDtypeStruct(shape, F32) for shape in outs],
        grid_spec=pltpu.PrefetchScalarGridSpec(
            num_scalar_prefetch=2,
            grid=(1,),
            in_specs=[pl.BlockSpec(memory_space=pltpu.HBM)] * 4,
            out_specs=[vmem] * 4,
            scratch_shapes=[
                pltpu.VMEM(load_leaf.shape, F32),
                pltpu.VMEM(leaf_inverse.shape, F32),
                pltpu.VMEM(leaf_coupling.shape, F32),
                pltpu.VMEM(load_sep.shape, F32),
                pltpu.VMEM((blocks, BLK, 2 * BLK), BF16),
                pltpu.VMEM((68, BLK, BLK), F32),
                pltpu.VMEM((BLK, BLK), F32),
                pltpu.SemaphoreType.DMA((2 + blocks // PER_COPY,)),
                pltpu.SemaphoreType.DMA,
            ],
        ),
        compiler_params=pltpu.CompilerParams(vmem_limit_bytes=LARGE_VMEM_BYTES),
        cost_estimate=cost(6),
    )(coords, pattern, load_leaf, leaf_inverse, leaf_coupling, load_sep)


def front_parts(coords, mine, received, cuts, through=(), after=()):
    def kernel(coords_ref, mine_ref, received_ref, *refs):
        outs, rows_of = refs[:-1], refs[-1]
        for k in range(mine.shape[0]):
            rows_of[k] = (mine_ref[k] + received_ref[k]).T
        for j in range(4):
            rows = pl.ds(pl.multiple_of((coords_ref[3] ^ j) * COLS, COLS), COLS)
            for c in range(len(cuts) - 1):
                outs[c * 4 + j][...] = rows_of[cuts[c] : cuts[c + 1], rows, :]

    counts = [cuts[c + 1] - cuts[c] for c in range(len(cuts) - 1)]
    return call(
        kernel,
        "front_parts",
        coords,
        [mine, received],
        [(count, COLS, BLK) for count in counts for _ in range(4)],
        after=after,
        through=through,
        scratch=[pltpu.VMEM(mine.shape, F32)],
    )


def preload(coords, sources, us=2.0, after=()):
    def kernel(coords_ref, *refs):
        count = len(sources)
        copies = []
        for k, (array, first, size) in enumerate(sources):
            part = refs[k].at[pl.ds(first, size)]
            copies.append(pltpu.make_async_copy(part, refs[count + k], refs[-1].at[k]))
            copies[-1].start()
        for copy in copies:
            copy.wait()

    return call(
        kernel,
        "preload",
        coords,
        [array for array, _, _ in sources],
        [(size, BLK, BLK) for _, _, size in sources],
        us=us,
        in_hbm=tuple(range(len(sources))),
        after=after,
        scratch=[pltpu.SemaphoreType.DMA((len(sources),))],
        limit=LARGE_VMEM_BYTES,
    )


def level12_message_kernel(coords, own, part1, part2, part3, keep, message):
    total = (own[...] + part1[...]) + (part2[...] + part3[...])
    y_at = coords[1]
    keep[0:6] = total[0:6]
    message[0:6] = total[0:6]

    def level3(j):
        row = pl.ds(6 + (y_at ^ j), 1)
        return (own[row] + part1[row]) + (part2[row] + part3[row])

    keep[6:7] = level3(0)
    keep[7:8] = level3(3)
    message[6:7] = level3(1)
    message[7:8] = level3(2)


def level12_kernel(
    coords, keep, received, own6, core6, y6, diagonal6, solved, message, left1, level1
):
    core, y_bit = coords[0], coords[1] & 1
    members = []
    for dy in range(2):
        for dc in range(2):
            members.append(((y_bit ^ dy) * 2 + (core ^ dc), dy, core ^ dc))
    mats = (own6, core6, y6, diagonal6)
    for (index, dy, at), mat in zip(members, mats):
        source = received if dy else keep
        here = times_transposed(-source[at], mat[0])
        solved[index] = here
        left1[index] = stacked(here)
    for (index, dy, at), mat in zip(members, mats):
        acc = sum_times_transposed([left1[m] for m in range(4)], [mat[2 + m] for m in range(4)])
        rhs = -(keep[2 + index] + received[2 + index]) - fold(acc)
        solved[4 + index] = times_transposed(rhs, mat[1])
    message[0:8] = solved[0:8]
    solved[8] = keep[6] + received[6]
    message[8] = keep[7] + received[7]


def level3_kernel(coords, solved, received, sums4, inverse, mats, y3, operand, left):
    core, y_at = coords[0], coords[1]
    half = y_at >> 1
    own = (y_at & 1) * 2 + core
    for level in range(2):
        for k in range(4):
            for source, part in ((solved, half), (received, 1 - half)):
                left[level * 8 + part * 4 + k] = stacked(source[level * 4 + k])
    acc = sum_times_transposed([left[m] for m in range(16)], [mats[m] for m in range(16)])
    rhs = -(solved[8] + received[8]) - fold(acc)
    here = times_transposed(rhs, inverse[2])
    y3[...] = here
    for p in range(16):
        operand[p, 0] = solved[own]
        operand[p, 1] = solved[4 + own]
        operand[p, 2] = here
        operand[p, 3] = sums4[p]


def level4_sums_kernel(coords, own, part1, part2, part3, sums4):
    half = coords[2] >> 1
    sums4[pl.ds((1 - half) * 8, 8)] = jnp.zeros((8, COLS, BLK), F32)
    sums4[pl.ds(half * 8, 8)] = (own[...] + part1[...]) + (part2[...] + part3[...])


def level5_sums_kernel(coords, own, part1, part2, part3, sums5):
    sums5[...] = (own[...] + part1[...]) + (part2[...] + part3[...])


def level4_kernel(
    coords, mine, other, sums5, inverse, mats, y4, operand, left
):
    core, half = coords[0], coords[2] >> 1
    total = mine[half * 8, 3]
    for p in range(1, 8):
        total = total + mine[half * 8 + p, 3]
    for level in range(3):
        for p in range(8):
            at = level * 16 + p * 2
            left[at + core] = stacked(mine[half * 8 + p, level])
            left[at + 1 - core] = stacked(other[half * 8 + p, level])
    terms = sum_times_transposed([left[m] for m in range(48)], [mats[m] for m in range(48)])
    here = times_transposed(-total - fold(terms), inverse[3])
    y4[...] = here
    for p in range(16):
        operand[p, 0] = here
        operand[p, 1] = sums5[p]


def add_products(coupling, first, count, start, acc, mats, sems, left):
    def step(i, total):
        fetched(coupling, first, mats, sems, i)
        at = i * CHUNK
        return total + sum_times_transposed(
            [left[at + m] for m in range(CHUNK)], [mats[at + m] for m in range(CHUNK)]
        )

    acc[...] = lax.fori_loop(0, count // CHUNK, step, start)


def level5_before_kernel(coords, mine, other, coupling, acc, mats54, mats, sems, left, sem):
    fetch(coupling, RUNS[5, 1], 96, mats, sems)
    last = pltpu.make_async_copy(coupling.at[pl.ds(RUNS[5, 4], 32)], mats54, sem)
    last.start()
    core = coords[0]
    for level in range(3):
        for p in range(16):
            at = level * 32 + p * 2
            left[at + core] = stacked(mine[p, level])
            left[at + 1 - core] = stacked(other[p, level])
    start = jnp.zeros((2 * COLS, 2 * BLK), F32)
    add_products(coupling, RUNS[5, 1], 96, start, acc, mats, sems, left)
    last.wait()


def level5_kernel(coords, acc, mine, other, inverse, mats, x5, own, theirs, left, pair):
    core = coords[0]
    total = mine[0, 1]
    for p in range(1, 16):
        total = total + mine[p, 1]
    for p in range(16):
        left[p * 2 + core] = stacked(mine[p, 0])
        left[p * 2 + 1 - core] = stacked(other[p, 0])
    terms = acc[...] + sum_times_transposed(
        [left[m] for m in range(32)], [mats[m] for m in range(32)]
    )
    solved = times_transposed(-total - fold(terms), inverse[4])
    here = times(solved, inverse[4])
    x5[...] = here
    wide = wide_left(here)
    for p in range(16):
        pair[2 * p], pair[2 * p + 1] = two_times(wide, mats[2 * p], mats[2 * p + 1])
    for p in range(16):
        own[p] = pair[2 * p + core]
        theirs[p] = pair[2 * p + 1 - core]


def level4_operand_kernel(coords, x5, own, received, operand):
    for p in range(16):
        operand[p, 0] = own[p] + received[p]
        operand[p, 1] = x5[...]


def level5_back_kernel(coords, x5, coupling, spread, mats4, mats, sems, sem):
    fetch(coupling, RUNS[5, 1], 96, mats, sems)
    last = pltpu.make_async_copy(coupling.at[pl.ds(RUNS[4, 1], 48)], mats4, sem)
    last.start()
    wide = wide_left(x5[...])

    def step(i, _):
        fetched(coupling, RUNS[5, 1], mats, sems, i)
        for k in range(0, CHUNK, 2):
            at = i * CHUNK + k
            spread[at], spread[at + 1] = two_times(wide, mats[at], mats[at + 1])
        return 0

    lax.fori_loop(0, 96 // CHUNK, step, 0)
    last.wait()


def level4_back_kernel(coords, parts, y4, spread, inverse, mats, x4, x5p, mine, theirs, all4):
    core, half = coords[0], coords[2] >> 1
    total = parts[0, 0]
    for p in range(1, 16):
        total = total + parts[p, 0]
    for p in range(16):
        x5p[p] = parts[p, 1]
    here = times(y4[...] - total, inverse[3])
    x4[...] = here
    wide = wide_left(here)
    for level in range(3):
        for pair in range(16):
            mine[pair, level] = spread[level * 32 + pair * 2 + core]
            theirs[pair, level] = spread[level * 32 + pair * 2 + 1 - core]
        for pair in range(8):
            at = level * 16 + pair * 2
            all4[0], all4[1] = two_times(wide, mats[at], mats[at + 1])
            mine[half * 8 + pair, level] += all4[core]
            theirs[half * 8 + pair, level] += all4[1 - core]


def level3_operand_kernel(coords, x4, mine, received, operand):
    for p in range(16):
        operand[p, 0:3] = mine[p] + received[p]
        operand[p, 3] = x4[...]


def level3_back_kernel(coords, parts, y3, inverse, mats, x3, x4p, mine, theirs, spread):
    core, y_at = coords[0], coords[1]
    sums = []
    for level in range(3):
        total = parts[0, level]
        for p in range(1, 16):
            total = total + parts[p, level]
        sums.append(total)
    for p in range(8):
        x4p[p] = parts[(coords[2] >> 1) * 8 + p, 3]
    here = times(y3[...] - sums[2], inverse[2])
    x3[...] = here
    wide = wide_left(here)
    for pair in range(8):
        spread[2 * pair], spread[2 * pair + 1] = two_times(wide, mats[2 * pair], mats[2 * pair + 1])
    for level in range(2):
        spread[level * 8 + y_at * 2 + core] += sums[level]
    for pair in range(8):
        mine[pair] = spread[2 * pair + core]
        theirs[pair] = spread[2 * pair + 1 - core]


def pair_message_kernel(coords, mine, received, x3, keep, message):
    half = coords[1] >> 1
    for level in range(2):
        for out, part in ((keep, half), (message, 1 - half)):
            rows = pl.ds(level * 4 + part * 2, 2)
            out[level * 2 : level * 2 + 2] = mine[rows] + received[rows]
    message[4] = x3[...]


def pair_sum_kernel(coords, keep, received, x3, message):
    message[0:4] = keep[...] + received[0:4]
    message[4] = x3[...]
    message[5] = received[4]


def pair_total_kernel(coords, message, received, out):
    out[0:4] = message[0:4] + received[0:4]
    out[4:6] = message[4:6]
    out[6:8] = received[4:6]


def level12_back_kernel(
    coords, mine, other, solved, own6, core6, y6, diagonal6, own1, own2, x123, terms
):
    core, y_at = coords[0], coords[1]
    y_bit = y_at & 1
    for source, parity in ((mine, core), (other, 1 - core)):
        for level in range(2):
            for y in range(2):
                terms[level * 4 + y * 2 + parity] = source[level * 2 + y]
        for k, dy in enumerate((0, 3, 1, 2)):
            x123[6 + (y_at ^ dy) * 2 + parity] = source[4 + k]
    members = [
        ((y_bit ^ dy) * 2 + (core ^ dc), dy, core ^ dc) for dy in range(2) for dc in range(2)
    ]
    mats = (own6, core6, y6, diagonal6)
    for k, ((index, dy, at), mat) in enumerate(zip(members, mats)):
        here = times(solved[4 + index] - terms[4 + index], mat[1])
        x123[2 + index] = here
        if k == 0:
            own2[...] = here
        wide = wide_left(here)
        for m in range(0, 4, 2):
            first, second = two_times(wide, mat[2 + m], mat[3 + m])
            terms[m] += first
            terms[m + 1] += second
    for k in range(2):
        index, dy, at = members[k]
        here = times(solved[index] - terms[index], mats[k][0])
        x123[at] = here
        if k == 0:
            own1[...] = here


LOW = 14
AT_ONCE = 4


def pack_kernel(coords, part0, part1, part2, part3, out):
    for j, part in enumerate((part0, part1, part2, part3)):
        out[j] = part[...]


def pack(coords, parts):
    return call(pack_kernel, "pack", coords, parts, [(4, *parts[0].shape)])[0]


def place(blocks, index, front, j, value):
    high, low = split(value)
    at = pl.multiple_of((front ^ j) * COLS, COLS)
    blocks[index, pl.ds(at, COLS), :] = high
    blocks[index, pl.ds(BLK + at, COLS), :] = low


def leaf_high_kernel(
    coords, pattern, load, inverse, coupling, x4m, x4o, x5m, x5o,
    rhs, couplings, items,
    loads, inverses, blocks, sems,
):
    count = couplings.shape[0]
    core, front = coords[0], coords[3]
    copies = leaf_copies(load, inverse, coupling, loads, inverses, couplings, sems, count)
    for copy in copies:
        copy.start()

    def note(i, found):
        items[1 + found] = i
        return found + (pattern[i >> 3, i & 7] < LOW).astype(jnp.int32)

    items[0] = lax.fori_loop(0, count * 8, note, jnp.int32(0))
    blocks[48] = jnp.zeros((2 * BLK, BLK), BF16)
    for j in range(4):
        for p in range(8):
            place(blocks, 2 * p + core, front, j, x4m[j, p])
            place(blocks, 2 * p + 1 - core, front, j, x4o[j, p])
        for p in range(16):
            place(blocks, 16 + 2 * p + core, front, j, x5m[j, p])
            place(blocks, 16 + 2 * p + 1 - core, front, j, x5o[j, p])
    copies[0].wait()
    copies[1].wait()
    for k in range(count // PER_COPY):
        copies[2 + k].wait()
        for b in range(k * PER_COPY, (k + 1) * PER_COPY):
            here = times_transposed(loads[:, b * BLK : (b + 1) * BLK], inverses[b])
            total = None
            for q in range(0, 8, 2):
                indices = [pattern[b, q + k2] for k2 in range(2)]
                chosen = [jnp.where(index < LOW, 48, index - LOW) for index in indices]
                left = jnp.concatenate([blocks[c] for c in chosen], axis=1)
                right = jnp.concatenate([beside(couplings[b, q + k2]) for k2 in range(2)], axis=0)
                part = dot_nn(left, right)
                total = part if total is None else total + part
            rhs[b] = here - fold(total)


def leaf_high(coords, pattern, load_leaf, leaf_inverse, leaf_coupling, gathered):
    blocks = leaf_inverse.shape[0]
    vmem = pl.BlockSpec(memory_space=pltpu.VMEM)
    return pl.pallas_call(
        leaf_high_kernel,
        name="leaf_high",
        out_shape=[
            jax.ShapeDtypeStruct((blocks, BLK, BLK), F32),
            jax.ShapeDtypeStruct(leaf_coupling.shape, F32),
            jax.ShapeDtypeStruct((blocks * 8 + 2,), jnp.int32),
        ],
        grid_spec=pltpu.PrefetchScalarGridSpec(
            num_scalar_prefetch=2,
            grid=(1,),
            in_specs=[pl.BlockSpec(memory_space=pltpu.HBM)] * 3 + [vmem] * 4,
            out_specs=[vmem, vmem, pl.BlockSpec(memory_space=pltpu.SMEM)],
            scratch_shapes=[
                pltpu.VMEM(load_leaf.shape, F32),
                pltpu.VMEM(leaf_inverse.shape, F32),
                pltpu.VMEM((49, 2 * BLK, BLK), BF16),
                pltpu.SemaphoreType.DMA((2 + blocks // PER_COPY,)),
            ],
        ),
        compiler_params=pltpu.CompilerParams(vmem_limit_bytes=VMEM_BYTES),
        cost_estimate=cost(8),
    )(coords, pattern, load_leaf, leaf_inverse, leaf_coupling, *gathered)


def leaf_low_kernel(
    coords, pattern, items, low0, low1, low2, low3, rhs, inverse, couplings,
    out,
    blocks, acc, solved, sems,
):
    front, count = coords[3], items[0]
    acc[...] = rhs[...]
    blocks[LOW] = jnp.zeros((2 * BLK, BLK), BF16)
    for j, low in enumerate((low0, low1, low2, low3)):
        for a in range(LOW):
            place(blocks, a, front, j, low[a])

    def step(t, _):
        for k in range(AT_ONCE):
            at = t * AT_ONCE + k
            item = jnp.where(at < count, items[1 + jnp.minimum(at, count)], 0)
            index = jnp.where(at < count, pattern[item >> 3, item & 7], LOW)
            right = beside(couplings[item >> 3, item & 7])
            acc[item >> 3] -= fold(dot_nn(blocks[index], right))
        return 0

    lax.fori_loop(0, (count + AT_ONCE - 1) // AT_ONCE, step, 0)
    copies = []
    for b in range(rhs.shape[0]):
        solved[b] = times(acc[b], inverse[b])
        copies.append(
            pltpu.make_async_copy(solved.at[b], out.at[:, b * BLK : (b + 1) * BLK], sems.at[b])
        )
        copies[-1].start()
    for copy in copies:
        copy.wait()


def leaf_low(coords, pattern, items, lows, rhs, leaf_inverse, couplings):
    blocks = leaf_inverse.shape[0]
    vmem = pl.BlockSpec(memory_space=pltpu.VMEM)
    return pl.pallas_call(
        leaf_low_kernel,
        name="leaf_low",
        out_shape=jax.ShapeDtypeStruct((BLK, blocks * BLK), F32),
        grid_spec=pltpu.PrefetchScalarGridSpec(
            num_scalar_prefetch=3,
            grid=(1,),
            in_specs=[vmem] * 7,
            out_specs=pl.BlockSpec(memory_space=pltpu.HBM),
            scratch_shapes=[
                pltpu.VMEM((LOW + 1, 2 * BLK, BLK), BF16),
                pltpu.VMEM((blocks, BLK, BLK), F32),
                pltpu.VMEM((blocks, BLK, BLK), F32),
                pltpu.SemaphoreType.DMA((blocks,)),
            ],
        ),
        compiler_params=pltpu.CompilerParams(vmem_limit_bytes=VMEM_BYTES),
        cost_estimate=cost(4),
    )(coords, pattern, items, *lows, rhs, leaf_inverse, couplings)


def across(value, mask):
    return lax.ppermute(value, "leaf", [(i, i ^ mask) for i in range(32)])


def across_front(value, mask):
    return lax.ppermute(value, "front", [(i, i ^ mask) for i in range(4)])


def swap16(value):
    groups = [[c + 2 * p for p in range(16)] for c in (0, 1)]
    return lax.all_to_all(value, "leaf", 0, 0, axis_index_groups=groups)


def local(
    load_leaf, leaf_inverse, leaf_coupling, leaf_pattern, load_sep, sep_inverse, sep_coupling
):
    leaf_at = lax.axis_index("leaf")
    coords = jnp.stack([leaf_at & 1, (leaf_at >> 1) & 3, leaf_at >> 3, lax.axis_index("front")])
    coords = coords.astype(jnp.int32)
    pattern = leaf_pattern
    one = (COLS, BLK)
    wide = (2 * COLS, 2 * BLK)
    left = lambda count: pltpu.VMEM((count, 2 * COLS, BLK), BF16)
    own6 = jnp.concatenate([sep_inverse[0:2], sep_coupling[0:4]], axis=0)
    mine13, theirs13, mine45, theirs45 = leaf_forward(
        coords, pattern, load_leaf, leaf_inverse, leaf_coupling, load_sep
    )
    *parts13, theirs45, own6 = front_parts(
        coords, mine13, across(theirs13, 1), (0, 10), through=[theirs45, own6]
    )
    parts13 = [parts13[0]] + [across_front(parts13[j], j) for j in (1, 2, 3)]
    y6 = across(own6, 2)
    core6 = across(own6, 1)
    parts45 = front_parts(coords, mine45, across(theirs45, 1), (0, 8, 24))
    parts4, parts5 = parts45[0:4], parts45[4:8]
    inverses, mats3 = preload(
        coords,
        [(sep_inverse, 0, 5), (sep_coupling, RUNS[3, 1], 16)],
        after=[parts45[0]],
    )
    keep, message, y6 = call(
        level12_message_kernel,
        "level12_message",
        coords,
        parts13,
        [(8, *one), (8, *one)],
        after=[parts45[0], mats3],
        through=[y6],
    )
    diagonal6 = across(y6, 1)
    group = [own6, core6, y6, diagonal6]
    parts4 = [parts4[0]] + [across_front(parts4[j], j) for j in (1, 2, 3)]
    solved12, message = call(
        level12_kernel,
        "level12",
        coords,
        [keep, across(message, 2), *group],
        [(9, *one), (9, *one)],
        us=2,
        scratch=[left(4), pltpu.VMEM((8, 128), F32)],
    )
    (sums4,) = call(
        level4_sums_kernel, "level4_sums", coords, parts4, [(16, *one)]
    )
    parts5 = [parts5[0]] + [across_front(parts5[j], j) for j in (1, 2, 3)]
    y3, operand = call(
        level3_kernel,
        "level3",
        coords,
        [solved12, across(message, 6), sums4, inverses, mats3],
        [one, (16, 4, *one)],
        us=2,
        scratch=[left(16)],
    )
    low_mine = swap16(operand)
    (mats4,) = preload(coords, [(sep_coupling, RUNS[4, 1], 48)], us=3, after=[y3])
    (sums5,) = call(
        level5_sums_kernel, "level5_sums", coords, parts5, [(16, *one)]
    )
    low_mine, mats4, sums5 = lax.optimization_barrier((low_mine, mats4, sums5))
    low_other = across(low_mine, 1)
    y4, operand = call(
        level4_kernel,
        "level4",
        coords,
        [low_mine, low_other, sums5, inverses, mats4],
        [one, (16, 2, *one)],
        us=3,
        scratch=[left(48)],
    )
    y4m = swap16(operand)
    acc5, mats54 = call(
        level5_before_kernel,
        "level5_before",
        coords,
        [low_mine, low_other, sep_coupling],
        [wide, (32, BLK, BLK)],
        us=6,
        in_hbm=(2,),
        scratch=[*matrices(96), left(96), pltpu.SemaphoreType.DMA],
        limit=LARGE_VMEM_BYTES,
    )
    y4m, acc5, mats54 = lax.optimization_barrier((y4m, acc5, mats54))
    y4o = across(y4m, 1)
    x5, own4, theirs4 = call(
        level5_kernel,
        "level5",
        coords,
        [acc5, y4m, y4o, inverses, mats54],
        [one, (16, *one), (16, *one)],
        us=4,
        scratch=[left(32), pltpu.VMEM((32, *one), F32)],
    )
    (operand,) = call(
        level4_operand_kernel,
        "level4_operand",
        coords,
        [x5, own4, across(theirs4, 1)],
        [(16, 2, *one)],
    )
    sums4 = swap16(operand)
    spread, mats4 = call(
        level5_back_kernel,
        "level5_back",
        coords,
        [x5, sep_coupling],
        [(96, *one), (48, BLK, BLK)],
        us=6,
        in_hbm=(1,),
        scratch=[*matrices(96), pltpu.SemaphoreType.DMA],
        limit=LARGE_VMEM_BYTES,
    )
    x4, x5p, mine, theirs = call(
        level4_back_kernel,
        "level4_back",
        coords,
        [sums4, y4, spread, inverses, mats4],
        [one, (16, *one), (16, 3, *one), (16, 3, *one)],
        us=2,
        scratch=[pltpu.VMEM((2, *one), F32)],
    )
    x5s = [x5p] + [across_front(x5p, j) for j in (1, 2, 3)]
    (operand,) = call(
        level3_operand_kernel,
        "level3_operand",
        coords,
        [x4, mine, across(theirs, 1)],
        [(16, 4, *one)],
    )
    parts3 = swap16(operand)
    x3, x4p, mine, theirs = call(
        level3_back_kernel,
        "level3_back",
        coords,
        [parts3, y3, inverses, mats3],
        [one, (8, *one), (8, *one), (8, *one)],
        us=1.5,
        scratch=[pltpu.VMEM((16, *one), F32)],
    )
    x5m = pack(coords, x5s)
    x5o = across(x5m, 1)
    x4s = [x4p] + [across_front(x4p, j) for j in (1, 2, 3)]
    keep, message = call(
        pair_message_kernel,
        "pair_message",
        coords,
        [mine, across(theirs, 1), x3],
        [(4, *one), (5, *one)],
        after=x5s[1:],
    )
    (message,) = call(
        pair_sum_kernel, "pair_sum", coords, [keep, across(message, 6), x3], [(6, *one)]
    )
    (mine,) = call(
        pair_total_kernel,
        "pair_total",
        coords,
        [message, across(message, 2)],
        [(8, *one)],
        after=x4s[1:],
    )
    x1, x2, x123 = call(
        level12_back_kernel,
        "level12_back",
        coords,
        [mine, across(mine, 1), solved12, *group],
        [one, one, (14, *one)],
        us=2,
        scratch=[pltpu.VMEM((8, *one), F32)],
    )
    x4m = pack(coords, x4s)
    x4o = across(x4m, 1)
    rhs, couplings, items = leaf_high(
        coords, pattern, load_leaf, leaf_inverse, leaf_coupling, [x4m, x4o, x5m, x5o]
    )
    lows = [x123] + [across_front(x123, j) for j in (1, 2, 3)]
    solution_leaf = leaf_low(coords, pattern, items, lows, rhs, leaf_inverse, couplings)
    solution_sep = jnp.concatenate([x1, x2, x3, x4, x5], axis=1)
    return solution_leaf, solution_sep


def solution(mesh):
    return jax.shard_map(
        local,
        mesh=mesh,
        in_specs=(
            P(None, ("leaf", "front")),
            P(("leaf", "front"), None, None),
            P(("leaf", "front"), None, None, None),
            P(("leaf", "front"), None),
            P("front", "leaf"),
            P("leaf", None, None),
            P("leaf", None, None),
        ),
        out_specs=(P(None, ("leaf", "front")), P("front", "leaf")),
        check_vma=False,
    )
```

time: 231 us -> 200 us (0.87)
  blocking collectives: 16.1 us -> 0 us
  Pallas kernels: 66.5 us -> 55 us
  starting transfers between devices: 71.6 us -> 61.9 us
  local copies, waits for them, and re-layouts: 5.75 us -> 15.2 us
    ppermute x27 -> x17, starting transfers between devices: 37.8 us -> 19.6 us  [across(): return lax.ppermute(value, 'leaf', [(i, i ^ mask) for i in range(32)])]
    all_to_all x1 -> x0, blocking collectives: 16.1 us -> none  [swap16(): return lax.all_to_all(value, 'leaf', 0, 0, axis_index_groups=groups)]
    ppermute x27 -> x17, waiting for transfers between devices: 30.6 us -> 15.9 us  [across(): return lax.ppermute(value, 'leaf', [(i, i ^ mask) for i in range(32)])]
    all_to_all x1 -> x4, starting transfers between devices: 5.35 us -> 19.6 us  [swap16(): return lax.all_to_all(value, 'leaf', 0, 0, axis_index_groups=groups)]
    all_to_all x1 -> x4, waiting for transfers between devices: 7.78 us -> 19.8 us  [swap16(): return lax.all_to_all(value, 'leaf', 0, 0, axis_index_groups=groups)]
    ppermute x15 -> x18, waiting for transfers between devices: 19.1 us -> 29 us  [across_front(): return lax.ppermute(value, 'front', [(i, i ^ mask) for i in range(4)])]
    unnamed x41 -> x67, local copies, waits for them, and re-layouts: 5.66 us -> 15.2 us
    all_to_all x2 -> x0, waiting for transfers between devices: 9.12 us -> none  [swap8(): return lax.all_to_all(value, 'leaf', 0, 0, axis_index_groups=groups)]
  transfers between devices with their start and end apart: 45 -> 39, of which waited for: 21 -> 25; matrix products, arithmetic and copies ran while one was open for 1% -> 0% of each run, Pallas kernels for 12% -> 15%
where the time goes in v3:
time: 200 us; the launch traced here: 198 us
  waiting for transfers between devices  64.8 us (32%)
  starting transfers between devices  61.9 us (31%)
  Pallas kernels  55 us (28%)
  local copies, waits for them, and re-layouts  15.2 us (8%)
    pallas_call x23, Pallas kernels, call(): pl.pallas_call(kernel, name=name, out_shape=[jax.ShapeDtypeStruct(shape,...  39.7 us
    ppermute x18, waiting for transfers between devices, across_front(): return lax.ppermute(value, 'front', [(i, i ^ mask) for i in range(4)])  29 us
    ppermute x18, starting transfers between devices, across_front(): return lax.ppermute(value, 'front', [(i, i ^ mask) for i in range(4)])  22.7 us
    all_to_all x4, waiting for transfers between devices, swap16(): return lax.all_to_all(value, 'leaf', 0, 0, axis_index_groups=groups)  19.8 us
    ppermute x17, starting transfers between devices, across(): return lax.ppermute(value, 'leaf', [(i, i ^ mask) for i in range(32)])  19.6 us
    all_to_all x4, starting transfers between devices, swap16(): return lax.all_to_all(value, 'leaf', 0, 0, axis_index_groups=groups)  19.6 us
    ppermute x17, waiting for transfers between devices, across(): return lax.ppermute(value, 'leaf', [(i, i ^ mask) for i in range(32)])  15.9 us
    unnamed x67, local copies, waits for them, and re-layouts  15.2 us
  transfers between devices with their start and end apart: 39, of which 25 were waited for; matrix products, arithmetic and copies ran while one was open for 0% of the time, Pallas kernels for 15%

profile of v3, /device:TPU:1, one launch (start us, length us, event | category | flops | bytes accessed | tf_op | source)
XLA Modules:
  0.0 198.2 jit_solution(2467878073903807402)
XLA Ops:
  4.6 5.4 %leaf_forward.1 = (f32[10,128,128]{2,1,0:T(8,128)S(1)}, f32[10,128,128]{2,1,0:T(8,128)S(1)}, f32[24,128,128]{2,1,0:T(8,128)S(1)}, f32[24,128,128]{2,1,0:T(8,128)S(1)}) custom-call(s32[4]{0:T(128)S(1)} %pad_add_fusion.coords.coords_ref, s32[12,8]{1,0:T(8,128)S(1)} %copy.14.pattern, f32[128,1536]{1,0:T(8,128)S(1)} %copy-done.11, ...), custom_call_target="tpu_custom_call" | custom-call | flops 600000000 | bytes 1800000 | tf_op jit(solution)/shard_map/leaf_forward/pallas_call | solution.py:209
  17.6 3.3 %collective-permute-start.2 = (f32[10,32,128]{2,1,0:T(8,128)S(1)}, f32[10,32,128]{2,1,0:T(8,128)S(1)}, u32[]{:S(2)}, u32[]{:S(2)}) collective-permute-start(f32[10,32,128]{2,1,0:T(8,128)S(1)} %get-tuple-element.65), channel_id=1, source_target_pairs={{0,2},{1,3},{2,0},{3,1},{4,6},{5,7},{6,4},{7,5},{8,10},{9,11},{10,... | collective-permute-start | bytes 491528 | tf_op jit(solution)/shard_map/ppermute | solution.py:696
  25.0 3.4 %collective-permute-done.2.refs_2_ = f32[10,32,128]{2,1,0:T(8,128)S(1)} collective-permute-done((f32[10,32,128]{2,1,0:T(8,128)S(1)}, f32[10,32,128]{2,1,0:T(8,128)S(1)}, u32[]{:S(2)}, u32[]{:S(2)}) %collective-permute-start.2) | collective-permute-done | bytes 163872 | tf_op jit(solution)/shard_map/ppermute | solution.py:696
  28.4 2.7 %collective-permute-done.3.refs_3_ = f32[10,32,128]{2,1,0:T(8,128)S(1)} collective-permute-done((f32[10,32,128]{2,1,0:T(8,128)S(1)}, f32[10,32,128]{2,1,0:T(8,128)S(1)}, u32[]{:S(2)}, u32[]{:S(2)}) %collective-permute-start.3) | collective-permute-done | bytes 163872 | tf_op jit(solution)/shard_map/ppermute | solution.py:696
  33.1 4.9 %collective-permute-done.6.refs_1_ = f32[8,32,128]{2,1,0:T(8,128)S(1)} collective-permute-done((f32[8,32,128]{2,1,0:T(8,128)S(1)}, f32[8,32,128]{2,1,0:T(8,128)S(1)}, u32[]{:S(2)}, u32[]{:S(2)}) %collective-permute-start.6) | collective-permute-done | bytes 131104 | tf_op jit(solution)/shard_map/ppermute | solution.py:692
  42.8 3.0 %collective-permute-start.12 = (f32[8,32,128]{2,1,0:T(8,128)S(1)}, f32[8,32,128]{2,1,0:T(8,128)S(1)}, u32[]{:S(2)}, u32[]{:S(2)}) collective-permute-start(f32[8,32,128]{2,1,0:T(8,128)S(1)} %get-tuple-element.79), channel_id=1, source_target_pairs={{0,3},{1,2},{2,1},{3,0},{4,7},{5,6},{6,5},{7,4},{8,11},{9,10},{10,... | collective-permute-start | bytes 393224 | tf_op jit(solution)/shard_map/ppermute | solution.py:696
  46.0 2.8 %collective-permute-done.11.refs_2_ = f32[8,32,128]{2,1,0:T(8,128)S(1)} collective-permute-done((f32[8,32,128]{2,1,0:T(8,128)S(1)}, f32[8,32,128]{2,1,0:T(8,128)S(1)}, u32[]{:S(2)}, u32[]{:S(2)}) %collective-permute-start.11) | collective-permute-done | bytes 131104 | tf_op jit(solution)/shard_map/ppermute | solution.py:696
  48.9 2.7 %collective-permute-done.12.refs_3_ = f32[8,32,128]{2,1,0:T(8,128)S(1)} collective-permute-done((f32[8,32,128]{2,1,0:T(8,128)S(1)}, f32[8,32,128]{2,1,0:T(8,128)S(1)}, u32[]{:S(2)}, u32[]{:S(2)}) %collective-permute-start.12) | collective-permute-done | bytes 131104 | tf_op jit(solution)/shard_map/ppermute | solution.py:696
  54.3 5.1 %all-to-all-start = ((f32[16,4,32,128]{3,2,1,0:T(8,128)}), f32[16,4,32,128]{3,2,1,0:T(8,128)}, u32[]{:S(2)}, u32[]{:S(2)}) async-start(f32[16,4,32,128]{3,2,1,0:T(8,128)} %get-tuple-element.81), calls=%async_computation | async-start | bytes 2097152 | tf_op jit(solution)/shard_map/all_to_all | solution.py:701
  59.5 3.0 %collective-permute-start.14 = (f32[16,32,128]{2,1,0:T(8,128)S(1)}, f32[16,32,128]{2,1,0:T(8,128)S(1)}, u32[]{:S(2)}, u32[]{:S(2)}) collective-permute-start(f32[16,32,128]{2,1,0:T(8,128)S(1)} %get-tuple-element.85), channel_id=1, source_target_pairs={{0,2},{1,3},{2,0},{3,1},{4,6},{5,7},{6,4},{7,5},{8,10},{9,11},{10,... | collective-permute-start | bytes 786440 | tf_op jit(solution)/shard_map/ppermute | solution.py:696
  63.4 3.1 %collective-permute-done.13.refs_1_ = f32[16,32,128]{2,1,0:T(8,128)S(1)} collective-permute-done((f32[16,32,128]{2,1,0:T(8,128)S(1)}, f32[16,32,128]{2,1,0:T(8,128)S(1)}, u32[]{:S(2)}, u32[]{:S(2)}) %collective-permute-start.13) | collective-permute-done | bytes 262176 | tf_op jit(solution)/shard_map/ppermute | solution.py:696
  66.5 6.6 %collective-permute-done.14.refs_2_ = f32[16,32,128]{2,1,0:T(8,128)S(1)} collective-permute-done((f32[16,32,128]{2,1,0:T(8,128)S(1)}, f32[16,32,128]{2,1,0:T(8,128)S(1)}, u32[]{:S(2)}, u32[]{:S(2)}) %collective-permute-start.14) | collective-permute-done | bytes 262176 | tf_op jit(solution)/shard_map/ppermute | solution.py:696
  73.0 3.0 %collective-permute-done.15.refs_3_ = f32[16,32,128]{2,1,0:T(8,128)S(1)} collective-permute-done((f32[16,32,128]{2,1,0:T(8,128)S(1)}, f32[16,32,128]{2,1,0:T(8,128)S(1)}, u32[]{:S(2)}, u32[]{:S(2)}) %collective-permute-start.15) | collective-permute-done | bytes 262176 | tf_op jit(solution)/shard_map/ppermute | solution.py:696
  77.3 2.4 %preload.3.refs_4_ = f32[48,128,128]{2,1,0:T(8,128)S(1)} custom-call(s32[4]{0:T(128)S(1)} %pad_add_fusion.coords.coords_ref, f32[196,128,128]{2,1,0:T(8,128)} %refs_1_.3, f32[32,128]{1,0:T(8,128)S(1)} %get-tuple-element.82.refs_1_), custom_call_target="tpu_custom_call" | custom-call | flops 300000000 | bytes 900000 | tf_op jit(solution)/shard_map/preload/pallas_call | solution.py:100
  82.1 2.5 %collective-permute-done.16.refs_1_ = f32[16,4,32,128]{3,2,1,0:T(8,128)S(1)} collective-permute-done((f32[16,4,32,128]{3,2,1,0:T(8,128)}, f32[16,4,32,128]{3,2,1,0:T(8,128)S(1)}, u32[]{:S(2)}, u32[]{:S(2)}) %collective-permute-start.16) | collective-permute-done | bytes 1048608 | tf_op jit(solution)/shard_map/ppermute | solution.py:692
  85.6 3.0 %level4.1 = (f32[32,128]{1,0:T(8,128)S(1)}, f32[16,2,32,128]{3,2,1,0:T(8,128)S(1)}) custom-call(s32[4]{0:T(128)S(1)} %pad_add_fusion.coords.coords_ref, f32[16,4,32,128]{3,2,1,0:T(8,128)} %all-to-all-done.refs_0_, f32[16,4,32,128]{3,2,1,0:T(8,128)S(1)} %collective-permute-done.16.refs_1_, f32[16,32,128]{2,1,0:T(8,128)S(1)} %copy-done.20, ...), custom_call_target="tpu_custom_call" | custom-call | flops 300000000 | bytes 900000 | tf_op jit(solution)/shard_map/level4/pallas_call | solution.py:100
  89.4 6.5 %all-to-all-start.1 = ((f32[16,2,32,128]{3,2,1,0:T(8,128)}), f32[16,2,32,128]{3,2,1,0:T(8,128)S(1)}, u32[]{:S(2)}, u32[]{:S(2)}) async-start(f32[16,2,32,128]{3,2,1,0:T(8,128)} %copy-done.24), calls=%async_computation.1 | async-start | bytes 1048576 | tf_op jit(solution)/shard_map/all_to_all | solution.py:701
  97.2 6.5 %level5_before.1 = (f32[64,256]{1,0:T(8,128)S(1)}, f32[32,128,128]{2,1,0:T(8,128)S(1)}) custom-call(s32[4]{0:T(128)S(1)} %pad_add_fusion.coords.coords_ref, f32[16,4,32,128]{3,2,1,0:T(8,128)} %all-to-all-done.refs_0_, f32[16,4,32,128]{3,2,1,0:T(8,128)S(1)} %copy-done.8, f32[196,128,128]{2,1,0:T(8,128)} %refs_1_.3), custom_call_target="tpu_custom_call" | custom-call | flops 600000000 | bytes 1800000 | tf_op jit(solution)/shard_map/level5_before/pallas_call | solution.py:100
  110.8 2.5 %level5.1 = (f32[32,128]{1,0:T(8,128)S(1)}, f32[16,32,128]{2,1,0:T(8,128)S(1)}, f32[16,32,128]{2,1,0:T(8,128)S(1)}) custom-call(s32[4]{0:T(128)S(1)} %pad_add_fusion.coords.coords_ref, f32[64,256]{1,0:T(8,128)S(1)} %copy-done.29, f32[16,2,32,128]{3,2,1,0:T(8,128)S(1)} %all-to-all-done.1.refs_1_, f32[16,2,32,128]{3,2,1,0:T(8,128)S(1)} %collective-permute-done.17.refs_2_, ...), custom_call_target="tpu_custom_call" | custom-call | flops 400000000 | bytes 1200000 | tf_op jit(solution)/shard_map/level5/pallas_call | solution.py:100
  116.2 4.2 %all-to-all-start.2 = ((f32[16,2,32,128]{3,2,1,0:T(8,128)}), f32[16,2,32,128]{3,2,1,0:T(8,128)}, u32[]{:S(2)}, u32[]{:S(2)}) async-start(f32[16,2,32,128]{3,2,1,0:T(8,128)} %level4_operand.1), calls=%async_computation.2 | async-start | bytes 1048576 | tf_op jit(solution)/shard_map/all_to_all | solution.py:701
  120.5 4.5 %level5_back.1 = (f32[96,32,128]{2,1,0:T(8,128)S(1)}, f32[48,128,128]{2,1,0:T(8,128)S(1)}) custom-call(s32[4]{0:T(128)S(1)} %pad_add_fusion.coords.coords_ref, f32[32,128]{1,0:T(8,128)S(1)} %get-tuple-element.96.refs_0_, f32[196,128,128]{2,1,0:T(8,128)} %refs_1_.3), custom_call_target="tpu_custom_call" | custom-call | flops 600000000 | bytes 1800000 | tf_op jit(solution)/shard_map/level5_back/pallas_call | solution.py:100
  126.1 4.6 %all-to-all-done.2.refs_0_ = f32[16,2,32,128]{3,2,1,0:T(8,128)} async-done(((f32[16,2,32,128]{3,2,1,0:T(8,128)}), f32[16,2,32,128]{3,2,1,0:T(8,128)}, u32[]{:S(2)}, u32[]{:S(2)}) %all-to-all-start.2) | async-done | bytes 524320 | tf_op jit(solution)/shard_map/all_to_all | solution.py:701
  132.2 2.6 %level4_back.1 = (f32[32,128]{1,0:T(8,128)S(1)}, f32[16,32,128]{2,1,0:T(8,128)S(1)}, f32[16,3,32,128]{3,2,1,0:T(8,128)S(1)}, f32[16,3,32,128]{3,2,1,0:T(8,128)S(1)}) custom-call(s32[4]{0:T(128)S(1)} %pad_add_fusion.coords.coords_ref, f32[16,2,32,128]{3,2,1,0:T(8,128)} %all-to-all-done.2.refs_0_, f32[32,128]{1,0:T(8,128)S(1)} %get-tuple-element.99.refs_1_, ...), custom_call_target="tpu_custom_call" | custom-call | flops 200000000 | bytes 600000 | tf_op jit(solution)/shard_map/level4_back/pallas_call | solution.py:100
  141.2 3.7 %all-to-all-start.3 = ((f32[16,4,32,128]{3,2,1,0:T(8,128)}), f32[16,4,32,128]{3,2,1,0:T(8,128)S(1)}, u32[]{:S(2)}, u32[]{:S(2)}) async-start(f32[16,4,32,128]{3,2,1,0:T(8,128)} %level3_operand.1), calls=%async_computation.3 | async-start | bytes 2097152 | tf_op jit(solution)/shard_map/all_to_all | solution.py:701
  145.8 2.4 %collective-permute-start.24 = (f32[16,32,128]{2,1,0:T(8,128)S(1)}, f32[16,32,128]{2,1,0:T(8,128)S(1)}, u32[]{:S(2)}, u32[]{:S(2)}) collective-permute-start(f32[16,32,128]{2,1,0:T(8,128)S(1)} %copy-done.26), channel_id=1, source_target_pairs={{0,1},{1,0},{2,3},{3,2},{4,5},{5,4},{6,7},{7,6},{8,9},{9,8},{10,11... | collective-permute-start | bytes 786440 | tf_op jit(solution)/shard_map/ppermute | solution.py:696
  148.2 13.2 %all-to-all-done.3.refs_0_ = f32[16,4,32,128]{3,2,1,0:T(8,128)S(1)} async-done(((f32[16,4,32,128]{3,2,1,0:T(8,128)}), f32[16,4,32,128]{3,2,1,0:T(8,128)S(1)}, u32[]{:S(2)}, u32[]{:S(2)}) %all-to-all-start.3) | async-done | bytes 1048608 | tf_op jit(solution)/shard_map/all_to_all | solution.py:701
  167.2 2.4 %collective-permute-start.20 = (f32[8,32,128]{2,1,0:T(8,128)S(1)}, f32[8,32,128]{2,1,0:T(8,128)S(1)}, u32[]{:S(2)}, u32[]{:S(2)}) collective-permute-start(f32[8,32,128]{2,1,0:T(8,128)S(1)} %get-tuple-element.105.refs_0_), channel_id=1, source_target_pairs={{0,1},{1,0},{2,3},{3,2},{4,5},{5,4},{6,7},{7,6},{8,9},{9,8},{10,11... | collective-permute-start | bytes 393224 | tf_op jit(solution)/shard_map/ppermute | solution.py:696
  171.8 2.8 %collective-permute-done.22.refs_3_.refs_4_ = f32[8,32,128]{2,1,0:T(8,128)S(1)} collective-permute-done((f32[8,32,128]{2,1,0:T(8,128)S(1)}, f32[8,32,128]{2,1,0:T(8,128)S(1)}, u32[]{:S(2)}, u32[]{:S(2)}) %collective-permute-start.22) | collective-permute-done | bytes 131104 | tf_op jit(solution)/shard_map/ppermute | solution.py:696
  182.0 2.4 %collective-permute-start.32 = (f32[14,32,128]{2,1,0:T(8,128)S(1)}, f32[14,32,128]{2,1,0:T(8,128)S(1)}, u32[]{:S(2)}, u32[]{:S(2)}) collective-permute-start(f32[14,32,128]{2,1,0:T(8,128)S(1)} %get-tuple-element.113.low0), channel_id=1, source_target_pairs={{0,1},{1,0},{2,3},{3,2},{4,5},{5,4},{6,7},{7,6},{8,9},{9,8},{10,11... | collective-permute-start | bytes 688136 | tf_op jit(solution)/shard_map/ppermute | solution.py:696
  184.5 2.8 %copy-done = f32[12,8,128,128]{3,2,1,0:T(8,128)S(1)} copy-done((f32[12,8,128,128]{3,2,1,0:T(8,128)S(1)}, f32[12,8,128,128]{3,2,1,0:T(8,128)}, u32[]{:S(2)}) %copy-start) | copy-done | bytes 6291480
  187.2 6.2 %leaf_high.1 = (f32[12,128,128]{2,1,0:T(8,128)S(1)}, f32[12,8,128,128]{3,2,1,0:T(8,128)S(1)}, s32[98]{0:T(128)S(1)}) custom-call(s32[4]{0:T(128)S(1)} %pad_add_fusion.coords.coords_ref, s32[12,8]{1,0:T(8,128)S(1)} %copy.14.pattern, f32[128,1536]{1,0:T(8,128)S(1)} %copy-done.12, f32[12,128,128]{2,1,0:T(8,128)S(1)} %copy-done.4, ...), custom_call_target="tpu_custom_call" | custom-call | flops 800000000 | bytes 2400000 | tf_op jit(solution)/shard_map/leaf_high/pallas_call | solution.py:609
  194.4 3.6 %leaf_low.1 = f32[128,1536]{1,0:T(8,128)} custom-call(s32[4]{0:T(128)S(1)} %pad_add_fusion.coords.coords_ref, s32[12,8]{1,0:T(8,128)S(1)} %copy.14.pattern, s32[98]{0:T(128)S(1)} %get-tuple-element.107.items, f32[14,32,128]{2,1,0:T(8,128)S(1)} %get-tuple-element.113.low0, f32[14,32,128]{2,1,0:T(8,128)S(1)} %collective-permute-done.32.low1, ...), custom_call_target="tpu_custom_call" | custom-call | flops 400000000 | bytes 1200000 | tf_op jit(solution)/shard_map/leaf_low/pallas_call | solution.py:670
  (146 shorter events, 69.0 us)
Async XLA Ops:
  14.2 6.8 %collective-permute-start.4 = (f32[24,128,128]{2,1,0:T(8,128)S(1)}, f32[24,128,128]{2,1,0:T(8,128)S(1)}, u32[]{:S(2)}, u32[]{:S(2)}) collective-permute-start(f32[24,128,128]{2,1,0:T(8,128)S(1)} %get-tuple-element.68), channel_id=1, source_target_pairs={{0,4},{4,0},{8,12},{12,8},{16,20},{20,16},{24,28},{28,24},{32,36},... | collective-permute-start | bytes 4718600 | tf_op jit(solution)/shard_map/ppermute | solution.py:692
  14.6 16.5 %collective-permute-start.5 = (f32[6,128,128]{2,1,0:T(8,128)S(1)}, f32[6,128,128]{2,1,0:T(8,128)S(1)}, u32[]{:S(2)}, u32[]{:S(2)}) collective-permute-start(f32[6,128,128]{2,1,0:T(8,128)S(1)} %get-tuple-element.71.refs_2_.refs_3_), channel_id=1, source_target_pairs={{0,8},{4,12},{8,0},{12,4},{16,24},{20,28},{24,16},{28,20},{32,40},... | collective-permute-start | bytes 1179656 | tf_op jit(solution)/shard_map/ppermute | solution.py:692
  16.0 9.0 %collective-permute-start.1 = (f32[10,32,128]{2,1,0:T(8,128)S(1)}, f32[10,32,128]{2,1,0:T(8,128)S(1)}, u32[]{:S(2)}, u32[]{:S(2)}) collective-permute-start(f32[10,32,128]{2,1,0:T(8,128)S(1)} %get-tuple-element.64), channel_id=1, source_target_pairs={{0,1},{1,0},{2,3},{3,2},{4,5},{5,4},{6,7},{7,6},{8,9},{9,8},{10,11... | collective-permute-start | bytes 491528 | tf_op jit(solution)/shard_map/ppermute | solution.py:696
  17.6 10.7 %collective-permute-start.2 = (f32[10,32,128]{2,1,0:T(8,128)S(1)}, f32[10,32,128]{2,1,0:T(8,128)S(1)}, u32[]{:S(2)}, u32[]{:S(2)}) collective-permute-start(f32[10,32,128]{2,1,0:T(8,128)S(1)} %get-tuple-element.65), channel_id=1, source_target_pairs={{0,2},{1,3},{2,0},{3,1},{4,6},{5,7},{6,4},{7,5},{8,10},{9,11},{10,... | collective-permute-start | bytes 491528 | tf_op jit(solution)/shard_map/ppermute | solution.py:696
  21.0 10.1 %collective-permute-start.3 = (f32[10,32,128]{2,1,0:T(8,128)S(1)}, f32[10,32,128]{2,1,0:T(8,128)S(1)}, u32[]{:S(2)}, u32[]{:S(2)}) collective-permute-start(f32[10,32,128]{2,1,0:T(8,128)S(1)} %get-tuple-element.66), channel_id=1, source_target_pairs={{0,3},{1,2},{2,1},{3,0},{4,7},{5,6},{6,5},{7,4},{8,11},{9,10},{10,... | collective-permute-start | bytes 491528 | tf_op jit(solution)/shard_map/ppermute | solution.py:696
  21.0 12.2 %collective-permute-start.7 = (f32[6,128,128]{2,1,0:T(8,128)S(1)}, f32[6,128,128]{2,1,0:T(8,128)S(1)}, u32[]{:S(2)}, u32[]{:S(2)}) collective-permute-start(f32[6,128,128]{2,1,0:T(8,128)S(1)} %get-tuple-element.71.refs_2_.refs_3_), channel_id=1, source_target_pairs={{0,4},{4,0},{8,12},{12,8},{16,20},{20,16},{24,28},{28,24},{32,36},... | collective-permute-start | bytes 1179656 | tf_op jit(solution)/shard_map/ppermute | solution.py:692
  31.7 6.3 %collective-permute-start.8 = (f32[6,128,128]{2,1,0:T(8,128)S(1)}, f32[6,128,128]{2,1,0:T(8,128)S(1)}, u32[]{:S(2)}, u32[]{:S(2)}) collective-permute-start(f32[6,128,128]{2,1,0:T(8,128)S(1)} %get-tuple-element.74.refs_4_.refs_5_), channel_id=1, source_target_pairs={{0,4},{4,0},{8,12},{12,8},{16,20},{20,16},{24,28},{28,24},{32,36},... | collective-permute-start | bytes 1179656 | tf_op jit(solution)/shard_map/ppermute | solution.py:692
  32.9 5.1 %collective-permute-start.6 = (f32[8,32,128]{2,1,0:T(8,128)S(1)}, f32[8,32,128]{2,1,0:T(8,128)S(1)}, u32[]{:S(2)}, u32[]{:S(2)}) collective-permute-start(f32[8,32,128]{2,1,0:T(8,128)S(1)} %get-tuple-element.73), channel_id=1, source_target_pairs={{0,8},{4,12},{8,0},{12,4},{16,24},{20,28},{24,16},{28,20},{32,40},... | collective-permute-start | bytes 393224 | tf_op jit(solution)/shard_map/ppermute | solution.py:692
  40.0 12.2 %collective-permute-start.9 = (f32[9,32,128]{2,1,0:T(8,128)S(1)}, f32[9,32,128]{2,1,0:T(8,128)S(1)}, u32[]{:S(2)}, u32[]{:S(2)}) collective-permute-start(f32[9,32,128]{2,1,0:T(8,128)S(1)} %get-tuple-element.76), channel_id=1, source_target_pairs={{0,24},{4,28},{8,16},{12,20},{16,8},{20,12},{24,0},{28,4},{32,56},... | collective-permute-start | bytes 442376 | tf_op jit(solution)/shard_map/ppermute | solution.py:692
  41.9 4.1 %collective-permute-start.10 = (f32[8,32,128]{2,1,0:T(8,128)S(1)}, f32[8,32,128]{2,1,0:T(8,128)S(1)}, u32[]{:S(2)}, u32[]{:S(2)}) collective-permute-start(f32[8,32,128]{2,1,0:T(8,128)S(1)} %get-tuple-element.77), channel_id=1, source_target_pairs={{0,1},{1,0},{2,3},{3,2},{4,5},{5,4},{6,7},{7,6},{8,9},{9,8},{10,11... | collective-permute-start | bytes 393224 | tf_op jit(solution)/shard_map/ppermute | solution.py:696
  41.9 7.0 %collective-permute-start.11 = (f32[8,32,128]{2,1,0:T(8,128)S(1)}, f32[8,32,128]{2,1,0:T(8,128)S(1)}, u32[]{:S(2)}, u32[]{:S(2)}) collective-permute-start(f32[8,32,128]{2,1,0:T(8,128)S(1)} %get-tuple-element.78), channel_id=1, source_target_pairs={{0,2},{1,3},{2,0},{3,1},{4,6},{5,7},{6,4},{7,5},{8,10},{9,11},{10,... | collective-permute-start | bytes 393224 | tf_op jit(solution)/shard_map/ppermute | solution.py:696
  42.8 8.8 %collective-permute-start.12 = (f32[8,32,128]{2,1,0:T(8,128)S(1)}, f32[8,32,128]{2,1,0:T(8,128)S(1)}, u32[]{:S(2)}, u32[]{:S(2)}) collective-permute-start(f32[8,32,128]{2,1,0:T(8,128)S(1)} %get-tuple-element.79), channel_id=1, source_target_pairs={{0,3},{1,2},{2,1},{3,0},{4,7},{5,6},{6,5},{7,4},{8,11},{9,10},{10,... | collective-permute-start | bytes 393224 | tf_op jit(solution)/shard_map/ppermute | solution.py:696
  54.3 25.5 %all-to-all-start = ((f32[16,4,32,128]{3,2,1,0:T(8,128)}), f32[16,4,32,128]{3,2,1,0:T(8,128)}, u32[]{:S(2)}, u32[]{:S(2)}) async-start(f32[16,4,32,128]{3,2,1,0:T(8,128)} %get-tuple-element.81), calls=%async_computation | async-start | bytes 2097152 | tf_op jit(solution)/shard_map/all_to_all | solution.py:701
  59.4 7.0 %collective-permute-start.13 = (f32[16,32,128]{2,1,0:T(8,128)S(1)}, f32[16,32,128]{2,1,0:T(8,128)S(1)}, u32[]{:S(2)}, u32[]{:S(2)}) collective-permute-start(f32[16,32,128]{2,1,0:T(8,128)S(1)} %get-tuple-element.84), channel_id=1, source_target_pairs={{0,1},{1,0},{2,3},{3,2},{4,5},{5,4},{6,7},{7,6},{8,9},{9,8},{10,11... | collective-permute-start | bytes 786440 | tf_op jit(solution)/shard_map/ppermute | solution.py:696
  59.5 13.5 %collective-permute-start.14 = (f32[16,32,128]{2,1,0:T(8,128)S(1)}, f32[16,32,128]{2,1,0:T(8,128)S(1)}, u32[]{:S(2)}, u32[]{:S(2)}) collective-permute-start(f32[16,32,128]{2,1,0:T(8,128)S(1)} %get-tuple-element.85), channel_id=1, source_target_pairs={{0,2},{1,3},{2,0},{3,1},{4,6},{5,7},{6,4},{7,5},{8,10},{9,11},{10,... | collective-permute-start | bytes 786440 | tf_op jit(solution)/shard_map/ppermute | solution.py:696
  62.5 13.5 %collective-permute-start.15 = (f32[16,32,128]{2,1,0:T(8,128)S(1)}, f32[16,32,128]{2,1,0:T(8,128)S(1)}, u32[]{:S(2)}, u32[]{:S(2)}) collective-permute-start(f32[16,32,128]{2,1,0:T(8,128)S(1)} %get-tuple-element.86), channel_id=1, source_target_pairs={{0,3},{1,2},{2,1},{3,0},{4,7},{5,6},{6,5},{7,4},{8,11},{9,10},{10,... | collective-permute-start | bytes 786440 | tf_op jit(solution)/shard_map/ppermute | solution.py:696
  79.8 4.8 %collective-permute-start.16 = (f32[16,4,32,128]{3,2,1,0:T(8,128)}, f32[16,4,32,128]{3,2,1,0:T(8,128)S(1)}, u32[]{:S(2)}, u32[]{:S(2)}) collective-permute-start(f32[16,4,32,128]{3,2,1,0:T(8,128)} %all-to-all-done.refs_0_), channel_id=1, source_target_pairs={{0,4},{4,0},{8,12},{12,8},{16,20},{20,16},{24,28},{28,24},{32,36},... | collective-permute-start | bytes 3145736 | tf_op jit(solution)/shard_map/ppermute | solution.py:692
  89.4 16.9 %all-to-all-start.1 = ((f32[16,2,32,128]{3,2,1,0:T(8,128)}), f32[16,2,32,128]{3,2,1,0:T(8,128)S(1)}, u32[]{:S(2)}, u32[]{:S(2)}) async-start(f32[16,2,32,128]{3,2,1,0:T(8,128)} %copy-done.24), calls=%async_computation.1 | async-start | bytes 1048576 | tf_op jit(solution)/shard_map/all_to_all | solution.py:701
  116.2 14.5 %all-to-all-start.2 = ((f32[16,2,32,128]{3,2,1,0:T(8,128)}), f32[16,2,32,128]{3,2,1,0:T(8,128)}, u32[]{:S(2)}, u32[]{:S(2)}) async-start(f32[16,2,32,128]{3,2,1,0:T(8,128)} %level4_operand.1), calls=%async_computation.2 | async-start | bytes 1048576 | tf_op jit(solution)/shard_map/all_to_all | solution.py:701
  141.2 20.2 %all-to-all-start.3 = ((f32[16,4,32,128]{3,2,1,0:T(8,128)}), f32[16,4,32,128]{3,2,1,0:T(8,128)S(1)}, u32[]{:S(2)}, u32[]{:S(2)}) async-start(f32[16,4,32,128]{3,2,1,0:T(8,128)} %level3_operand.1), calls=%async_computation.3 | async-start | bytes 2097152 | tf_op jit(solution)/shard_map/all_to_all | solution.py:701
  144.9 19.8 %collective-permute-start.26 = (f32[16,32,128]{2,1,0:T(8,128)S(1)}, f32[16,32,128]{2,1,0:T(8,128)S(1)}, u32[]{:S(2)}, u32[]{:S(2)}) collective-permute-start(f32[16,32,128]{2,1,0:T(8,128)S(1)} %copy-done.26), channel_id=1, source_target_pairs={{0,3},{1,2},{2,1},{3,0},{4,7},{5,6},{6,5},{7,4},{8,11},{9,10},{10,... | collective-permute-start | bytes 786440 | tf_op jit(solution)/shard_map/ppermute | solution.py:696
  145.8 18.9 %collective-permute-start.25 = (f32[16,32,128]{2,1,0:T(8,128)S(1)}, f32[16,32,128]{2,1,0:T(8,128)S(1)}, u32[]{:S(2)}, u32[]{:S(2)}) collective-permute-start(f32[16,32,128]{2,1,0:T(8,128)S(1)} %copy-done.26), channel_id=1, source_target_pairs={{0,2},{1,3},{2,0},{3,1},{4,6},{5,7},{6,4},{7,5},{8,10},{9,11},{10,... | collective-permute-start | bytes 786440 | tf_op jit(solution)/shard_map/ppermute | solution.py:696
  145.8 18.9 %collective-permute-start.24 = (f32[16,32,128]{2,1,0:T(8,128)S(1)}, f32[16,32,128]{2,1,0:T(8,128)S(1)}, u32[]{:S(2)}, u32[]{:S(2)}) collective-permute-start(f32[16,32,128]{2,1,0:T(8,128)S(1)} %copy-done.26), channel_id=1, source_target_pairs={{0,1},{1,0},{2,3},{3,2},{4,5},{5,4},{6,7},{7,6},{8,9},{9,8},{10,11... | collective-permute-start | bytes 786440 | tf_op jit(solution)/shard_map/ppermute | solution.py:696
  165.3 19.1 %collective-permute-start.27 = (f32[4,16,32,128]{3,2,1,0:T(8,128)S(1)}, f32[4,16,32,128]{3,2,1,0:T(8,128)S(1)}, u32[]{:S(2)}, u32[]{:S(2)}) collective-permute-start(f32[4,16,32,128]{3,2,1,0:T(8,128)S(1)} %pack.3.x5m), channel_id=1, source_target_pairs={{0,4},{4,0},{8,12},{12,8},{16,20},{20,16},{24,28},{28,24},{32,36},... | collective-permute-start | bytes 3145736 | tf_op jit(solution)/shard_map/ppermute | solution.py:692
  166.2 5.0 %collective-permute-start.29 = (f32[5,32,128]{2,1,0:T(8,128)S(1)}, f32[5,32,128]{2,1,0:T(8,128)S(1)}, u32[]{:S(2)}, u32[]{:S(2)}) collective-permute-start(f32[5,32,128]{2,1,0:T(8,128)S(1)} %get-tuple-element.112), channel_id=1, source_target_pairs={{0,24},{4,28},{8,16},{12,20},{16,8},{20,12},{24,0},{28,4},{32,56},... | collective-permute-start | bytes 245768 | tf_op jit(solution)/shard_map/ppermute | solution.py:692
  166.3 8.3 %collective-permute-start.22 = (f32[8,32,128]{2,1,0:T(8,128)S(1)}, f32[8,32,128]{2,1,0:T(8,128)S(1)}, u32[]{:S(2)}, u32[]{:S(2)}) collective-permute-start(f32[8,32,128]{2,1,0:T(8,128)S(1)} %get-tuple-element.105.refs_0_), channel_id=1, source_target_pairs={{0,3},{1,2},{2,1},{3,0},{4,7},{5,6},{6,5},{7,4},{8,11},{9,10},{10,... | collective-permute-start | bytes 393224 | tf_op jit(solution)/shard_map/ppermute | solution.py:696
  167.2 7.4 %collective-permute-start.21 = (f32[8,32,128]{2,1,0:T(8,128)S(1)}, f32[8,32,128]{2,1,0:T(8,128)S(1)}, u32[]{:S(2)}, u32[]{:S(2)}) collective-permute-start(f32[8,32,128]{2,1,0:T(8,128)S(1)} %get-tuple-element.105.refs_0_), channel_id=1, source_target_pairs={{0,2},{1,3},{2,0},{3,1},{4,6},{5,7},{6,4},{7,5},{8,10},{9,11},{10,... | collective-permute-start | bytes 393224 | tf_op jit(solution)/shard_map/ppermute | solution.py:696
  167.2 8.2 %collective-permute-start.20 = (f32[8,32,128]{2,1,0:T(8,128)S(1)}, f32[8,32,128]{2,1,0:T(8,128)S(1)}, u32[]{:S(2)}, u32[]{:S(2)}) collective-permute-start(f32[8,32,128]{2,1,0:T(8,128)S(1)} %get-tuple-element.105.refs_0_), channel_id=1, source_target_pairs={{0,1},{1,0},{2,3},{3,2},{4,5},{5,4},{6,7},{7,6},{8,9},{9,8},{10,11... | collective-permute-start | bytes 393224 | tf_op jit(solution)/shard_map/ppermute | solution.py:696
  178.8 5.6 %collective-permute-start.23 = (f32[4,8,32,128]{3,2,1,0:T(8,128)S(1)}, f32[4,8,32,128]{3,2,1,0:T(8,128)S(1)}, u32[]{:S(2)}, u32[]{:S(2)}) collective-permute-start(f32[4,8,32,128]{3,2,1,0:T(8,128)S(1)} %pack.2.x4m), channel_id=1, source_target_pairs={{0,4},{4,0},{8,12},{12,8},{16,20},{20,16},{24,28},{28,24},{32,36},... | collective-permute-start | bytes 1572872 | tf_op jit(solution)/shard_map/ppermute | solution.py:692
  181.0 13.0 %collective-permute-start.34 = (f32[14,32,128]{2,1,0:T(8,128)S(1)}, f32[14,32,128]{2,1,0:T(8,128)S(1)}, u32[]{:S(2)}, u32[]{:S(2)}) collective-permute-start(f32[14,32,128]{2,1,0:T(8,128)S(1)} %get-tuple-element.113.low0), channel_id=1, source_target_pairs={{0,3},{1,2},{2,1},{3,0},{4,7},{5,6},{6,5},{7,4},{8,11},{9,10},{10,... | collective-permute-start | bytes 688136 | tf_op jit(solution)/shard_map/ppermute | solution.py:696
  181.9 12.1 %collective-permute-start.33 = (f32[14,32,128]{2,1,0:T(8,128)S(1)}, f32[14,32,128]{2,1,0:T(8,128)S(1)}, u32[]{:S(2)}, u32[]{:S(2)}) collective-permute-start(f32[14,32,128]{2,1,0:T(8,128)S(1)} %get-tuple-element.113.low0), channel_id=1, source_target_pairs={{0,2},{1,3},{2,0},{3,1},{4,6},{5,7},{6,4},{7,5},{8,10},{9,11},{10,... | collective-permute-start | bytes 688136 | tf_op jit(solution)/shard_map/ppermute | solution.py:696
  182.0 12.5 %collective-permute-start.32 = (f32[14,32,128]{2,1,0:T(8,128)S(1)}, f32[14,32,128]{2,1,0:T(8,128)S(1)}, u32[]{:S(2)}, u32[]{:S(2)}) collective-permute-start(f32[14,32,128]{2,1,0:T(8,128)S(1)} %get-tuple-element.113.low0), channel_id=1, source_target_pairs={{0,1},{1,0},{2,3},{3,2},{4,5},{5,4},{6,7},{7,6},{8,9},{9,8},{10,11... | collective-permute-start | bytes 688136 | tf_op jit(solution)/shard_map/ppermute | solution.py:696
  (40 other events, 306.5 us)

commit v4 on v3

--- a/solution.py
+++ b/solution.py
@@ -76,7 +76,7 @@
 
 def cost(us):
     return pl.CostEstimate(
-        flops=int(us * 1e8), bytes_accessed=int(us * 3e5), transcendentals=0
+        flops=int(us * 1e9), bytes_accessed=int(us * 3e6), transcendentals=0
     )
 
 
@@ -319,78 +319,128 @@
     message[8] = keep[7] + received[7]
 
 
-def level3_kernel(coords, solved, received, sums4, inverse, mats, y3, operand, left):
-    core, y_at = coords[0], coords[1]
+def level3_kernel(
+    coords, solved, received, sums4, inverse, mats, y3, message, y12, y12p, left
+):
+    core, y_at, x_bit = coords[0], coords[1], coords[2] & 1
     half = y_at >> 1
-    own = (y_at & 1) * 2 + core
     for level in range(2):
         for k in range(4):
             for source, part in ((solved, half), (received, 1 - half)):
-                left[level * 8 + part * 4 + k] = stacked(source[level * 4 + k])
+                at = level * 8 + part * 4 + k
+                y12[at] = source[level * 4 + k]
+                left[at] = stacked(source[level * 4 + k])
     acc = sum_times_transposed([left[m] for m in range(16)], [mats[m] for m in range(16)])
     rhs = -(solved[8] + received[8]) - fold(acc)
     here = times_transposed(rhs, inverse[2])
     y3[...] = here
-    for p in range(16):
-        operand[p, 0] = solved[own]
-        operand[p, 1] = solved[4 + own]
-        operand[p, 2] = here
-        operand[p, 3] = sums4[p]
+    message[0] = here
+    message[1:5] = sums4[pl.ds((1 - x_bit) * 4, 4)]
+    for level in range(2):
+        for y in range(4):
+            y12p[level * 4 + y] = y12[level * 8 + y * 2 + core]
 
 
 def level4_sums_kernel(coords, own, part1, part2, part3, sums4):
-    half = coords[2] >> 1
-    sums4[pl.ds((1 - half) * 8, 8)] = jnp.zeros((8, COLS, BLK), F32)
-    sums4[pl.ds(half * 8, 8)] = (own[...] + part1[...]) + (part2[...] + part3[...])
+    sums4[...] = (own[...] + part1[...]) + (part2[...] + part3[...])
+
+
+def level4_pair_kernel(coords, y3, sums4, received, own, message1, message2, message3):
+    y_at, x_bit = coords[1], coords[2] & 1
+    for j, out in enumerate((own, message1, message2, message3)):
+        row = y_at ^ j
+        out[0] = y3[...]
+        out[1] = received[0]
+        out[2] = sums4[x_bit * 4 + row] + received[1 + row]
+
+
+def level4_pack_kernel(coords, own, part1, part2, part3, r8, low16, total):
+    y_at, x_bit = coords[1], coords[2] & 1
+    for j, part in enumerate((own, part1, part2, part3)):
+        low16[x_bit * 4 + (y_at ^ j)] = part[0]
+        low16[(1 - x_bit) * 4 + (y_at ^ j)] = part[1]
+    low16[8:16] = r8[...]
+    total[...] = (own[2] + part1[2]) + (part2[2] + part3[2])
 
 
 def level5_sums_kernel(coords, own, part1, part2, part3, sums5):
     sums5[...] = (own[...] + part1[...]) + (part2[...] + part3[...])
 
 
+def half_lefts(left, core, line, mine, other, rest):
+    for p in range(8):
+        left[32 + 2 * p + core] = stacked(mine[p])
+        left[32 + 2 * p + 1 - core] = stacked(other[p])
+    for level in range(2):
+        for y in range(4):
+            at = level * 16 + line * 8 + 2 * y
+            left[at + core] = stacked(mine[8 + level * 4 + y])
+            left[at + 1 - core] = stacked(other[8 + level * 4 + y])
+        rest(level, level * 16 + (1 - line) * 8)
+
+
+def own_half_lefts(left, coords, low, other, y12):
+    def rest(level, at):
+        for m in range(8):
+            left[at + m] = stacked(y12[level * 8 + m])
+
+    half_lefts(left, coords[0], 1 - (coords[2] & 1), low, other, rest)
+
+
 def level4_kernel(
-    coords, mine, other, sums5, inverse, mats, y4, operand, left
+    coords, low, other, y12, total, sums5, inverse, mats, y4, operand, left
 ):
-    core, half = coords[0], coords[2] >> 1
-    total = mine[half * 8, 3]
-    for p in range(1, 8):
-        total = total + mine[half * 8 + p, 3]
-    for level in range(3):
-        for p in range(8):
-            at = level * 16 + p * 2
-            left[at + core] = stacked(mine[half * 8 + p, level])
-            left[at + 1 - core] = stacked(other[half * 8 + p, level])
+    own_half_lefts(left, coords, low, other, y12)
     terms = sum_times_transposed([left[m] for m in range(48)], [mats[m] for m in range(48)])
-    here = times_transposed(-total - fold(terms), inverse[3])
+    here = times_transposed(-total[...] - fold(terms), inverse[3])
     y4[...] = here
     for p in range(16):
         operand[p, 0] = here
         operand[p, 1] = sums5[p]
 
 
-def add_products(coupling, first, count, start, acc, mats, sems, left):
-    def step(i, total):
-        fetched(coupling, first, mats, sems, i)
-        at = i * CHUNK
-        return total + sum_times_transposed(
-            [left[at + m] for m in range(CHUNK)], [mats[at + m] for m in range(CHUNK)]
+def fetch_half(coupling, half, target, sems):
+    copies = []
+    for level in range(3):
+        source = coupling.at[pl.ds(RUNS[5, 1] + level * 32 + half * 16, 16)]
+        copies.append(
+            pltpu.make_async_copy(source, target.at[pl.ds(level * 16, 16)], sems.at[level])
         )
-
-    acc[...] = lax.fori_loop(0, count // CHUNK, step, start)
-
-
-def level5_before_kernel(coords, mine, other, coupling, acc, mats54, mats, sems, left, sem):
-    fetch(coupling, RUNS[5, 1], 96, mats, sems)
+        copies[-1].start()
+    return copies
+
+
+def half_products(copies, left, mats):
+    total = None
+    for level, copy in enumerate(copies):
+        copy.wait()
+        rows = range(level * 16, level * 16 + 16)
+        part = sum_times_transposed([left[m] for m in rows], [mats[m] for m in rows])
+        total = part if total is None else total + part
+    return total
+
+
+def level5_own_kernel(coords, low, other, y12, coupling, acc, mats, sems, left):
+    copies = fetch_half(coupling, coords[2] >> 1, mats, sems)
+    own_half_lefts(left, coords, low, other, y12)
+    acc[...] = half_products(copies, left, mats)
+
+
+def level5_far_kernel(
+    coords, low, other, line, line_other, own, coupling, acc, mats54, mats, sems, left, sem
+):
+    copies = fetch_half(coupling, 1 - (coords[2] >> 1), mats, sems)
     last = pltpu.make_async_copy(coupling.at[pl.ds(RUNS[5, 4], 32)], mats54, sem)
     last.start()
     core = coords[0]
-    for level in range(3):
-        for p in range(16):
-            at = level * 32 + p * 2
-            left[at + core] = stacked(mine[p, level])
-            left[at + 1 - core] = stacked(other[p, level])
-    start = jnp.zeros((2 * COLS, 2 * BLK), F32)
-    add_products(coupling, RUNS[5, 1], 96, start, acc, mats, sems, left)
+
+    def rest(level, at):
+        for y in range(4):
+            left[at + 2 * y + core] = stacked(line[level * 4 + y])
+            left[at + 2 * y + 1 - core] = stacked(line_other[level * 4 + y])
+
+    half_lefts(left, core, coords[2] & 1, low, other, rest)
+    acc[...] = own[...] + half_products(copies, left, mats)
     last.wait()
 
 
@@ -723,9 +773,9 @@
     core6 = across(own6, 1)
     parts45 = front_parts(coords, mine45, across(theirs45, 1), (0, 8, 24))
     parts4, parts5 = parts45[0:4], parts45[4:8]
-    inverses, mats3 = preload(
-        coords,
-        [(sep_inverse, 0, 5), (sep_coupling, RUNS[3, 1], 16)],
+    inverses, mats3, mats4 = preload(
+        coords,
+        [(sep_inverse, 0, 5), (sep_coupling, RUNS[3, 1], 16), (sep_coupling, RUNS[4, 1], 48)],
         after=[parts45[0]],
     )
     keep, message, y6 = call(
@@ -750,44 +800,76 @@
         scratch=[left(4), pltpu.VMEM((8, 128), F32)],
     )
     (sums4,) = call(
-        level4_sums_kernel, "level4_sums", coords, parts4, [(16, *one)]
+        level4_sums_kernel, "level4_sums", coords, parts4, [(8, *one)]
     )
     parts5 = [parts5[0]] + [across_front(parts5[j], j) for j in (1, 2, 3)]
-    y3, operand = call(
+    y3, message, y12, y12p = call(
         level3_kernel,
         "level3",
         coords,
         [solved12, across(message, 6), sums4, inverses, mats3],
-        [one, (16, 4, *one)],
+        [one, (5, *one), (16, *one), (8, *one)],
         us=2,
         scratch=[left(16)],
     )
-    low_mine = swap16(operand)
-    (mats4,) = preload(coords, [(sep_coupling, RUNS[4, 1], 48)], us=3, after=[y3])
-    (sums5,) = call(
-        level5_sums_kernel, "level5_sums", coords, parts5, [(16, *one)]
-    )
-    low_mine, mats4, sums5 = lax.optimization_barrier((low_mine, mats4, sums5))
-    low_other = across(low_mine, 1)
+    (sums5,) = call(level5_sums_kernel, "level5_sums", coords, parts5, [(16, *one)])
+    r8 = across(y12p, 8)
+    own, *messages = call(
+        level4_pair_kernel,
+        "level4_pair",
+        coords,
+        [y3, sums4, across(message, 8)],
+        [(3, *one)] * 4,
+    )
+    parts = [own] + [across(messages[j - 1], 2 * j) for j in (1, 2, 3)]
+    low16, total4 = call(
+        level4_pack_kernel,
+        "level4_pack",
+        coords,
+        [*parts, r8],
+        [(16, *one), one],
+        after=[sums5],
+    )
+    other16 = across(low16, 1)
+    far16 = across(low16, 24)
+    line8 = across(y12p, 24)
+    line_other8 = across(line8, 1)
     y4, operand = call(
         level4_kernel,
         "level4",
         coords,
-        [low_mine, low_other, sums5, inverses, mats4],
+        [low16, other16, y12, total4, sums5, inverses, mats4],
         [one, (16, 2, *one)],
         us=3,
         scratch=[left(48)],
     )
     y4m = swap16(operand)
+    far_other16 = across(far16, 1)
+    (own5,) = call(
+        level5_own_kernel,
+        "level5_own",
+        coords,
+        [low16, other16, y12, sep_coupling],
+        [wide],
+        us=4,
+        in_hbm=(3,),
+        scratch=[pltpu.VMEM((48, BLK, BLK), F32), pltpu.SemaphoreType.DMA((3,)), left(48)],
+        limit=LARGE_VMEM_BYTES,
+    )
     acc5, mats54 = call(
-        level5_before_kernel,
-        "level5_before",
-        coords,
-        [low_mine, low_other, sep_coupling],
+        level5_far_kernel,
+        "level5_far",
+        coords,
+        [far16, far_other16, line8, line_other8, own5, sep_coupling],
         [wide, (32, BLK, BLK)],
-        us=6,
-        in_hbm=(2,),
-        scratch=[*matrices(96), left(96), pltpu.SemaphoreType.DMA],
+        us=4,
+        in_hbm=(5,),
+        scratch=[
+            pltpu.VMEM((48, BLK, BLK), F32),
+            pltpu.SemaphoreType.DMA((3,)),
+            left(48),
+            pltpu.SemaphoreType.DMA,
+        ],
         limit=LARGE_VMEM_BYTES,
     )
     y4m, acc5, mats54 = lax.optimization_barrier((y4m, acc5, mats54))

time: 200 us -> 190 us (0.950)
  waiting for transfers between devices: 64.8 us -> 44.4 us
  starting transfers between devices: 61.9 us -> 69 us
  Pallas kernels: 55 us -> 57.7 us
    ppermute x18, waiting for transfers between devices: 29 us -> 11.1 us  [across_front(): return lax.ppermute(value, 'front', [(i, i ^ mask) for i in range(4)])]
    ppermute x17 -> x26, starting transfers between devices: 19.6 us -> 30.3 us  [across(): return lax.ppermute(value, 'leaf', [(i, i ^ mask) for i in range(32)])]
    all_to_all x4 -> x3, waiting for transfers between devices: 19.8 us -> 16.1 us  [swap16(): return lax.all_to_all(value, 'leaf', 0, 0, axis_index_groups=groups)]
    all_to_all x4 -> x3, starting transfers between devices: 19.6 us -> 15.9 us  [swap16(): return lax.all_to_all(value, 'leaf', 0, 0, axis_index_groups=groups)]
    pallas_call x23 -> x25, Pallas kernels: 39.7 us -> 42.1 us  [call(): pl.pallas_call(kernel, name=name, out_shape=[jax.ShapeDtypeStruct(shape,...]
    unnamed x67 -> x59, local copies, waits for them, and re-layouts: 15.2 us -> 16.6 us
    ppermute x17 -> x26, waiting for transfers between devices: 15.9 us -> 17.3 us  [across(): return lax.ppermute(value, 'leaf', [(i, i ^ mask) for i in range(32)])]
  transfers between devices with their start and end apart: 39 -> 47, of which waited for: 25 -> 20; matrix products, arithmetic and copies ran while one was open for 0% -> 0% of each run, Pallas kernels for 15% -> 20%
where the time goes in v4:
time: 190 us; the launch traced here: 189 us
  starting transfers between devices  69 us (36%)
  Pallas kernels  57.7 us (30%)
  waiting for transfers between devices  44.4 us (23%)
  local copies, waits for them, and re-layouts  16.6 us (9%)
    pallas_call x25, Pallas kernels, call(): pl.pallas_call(kernel, name=name, out_shape=[jax.ShapeDtypeStruct(shape,...  42.1 us
    ppermute x26, starting transfers between devices, across(): return lax.ppermute(value, 'leaf', [(i, i ^ mask) for i in range(32)])  30.3 us
    ppermute x18, starting transfers between devices, across_front(): return lax.ppermute(value, 'front', [(i, i ^ mask) for i in range(4)])  22.8 us
    ppermute x26, waiting for transfers between devices, across(): return lax.ppermute(value, 'leaf', [(i, i ^ mask) for i in range(32)])  17.3 us
    unnamed x59, local copies, waits for them, and re-layouts  16.6 us
    all_to_all x3, waiting for transfers between devices, swap16(): return lax.all_to_all(value, 'leaf', 0, 0, axis_index_groups=groups)  16.1 us
    all_to_all x3, starting transfers between devices, swap16(): return lax.all_to_all(value, 'leaf', 0, 0, axis_index_groups=groups)  15.9 us
    ppermute x18, waiting for transfers between devices, across_front(): return lax.ppermute(value, 'front', [(i, i ^ mask) for i in range(4)])  11.1 us
  transfers between devices with their start and end apart: 47, of which 20 were waited for; matrix products, arithmetic and copies ran while one was open for 0% of the time, Pallas kernels for 20%

profile of v4, /device:TPU:1, one launch (start us, length us, event | category | flops | bytes accessed | tf_op | source)
XLA Modules:
  0.0 189.2 jit_solution(18189642637192507795)
XLA Ops:
  4.6 5.4 %leaf_forward.1 = (f32[10,128,128]{2,1,0:T(8,128)S(1)}, f32[10,128,128]{2,1,0:T(8,128)S(1)}, f32[24,128,128]{2,1,0:T(8,128)S(1)}, f32[24,128,128]{2,1,0:T(8,128)S(1)}) custom-call(s32[4]{0:T(128)S(1)} %pad_add_fusion.coords.coords_ref, s32[12,8]{1,0:T(8,128)S(1)} %copy.14.pattern, f32[128,1536]{1,0:T(8,128)S(1)} %copy-done.1, f32[12,128,128]{2,1,0:T(8,128)S(1)} %copy-done.3, ...), custom_call_target="tpu_custom_call" | custom-call | flops 6000000000 | bytes 18000000 | tf_op jit(solution)/shard_map/leaf_forward/pallas_call | solution.py:209
  18.1 3.3 %collective-permute-start.2 = (f32[10,32,128]{2,1,0:T(8,128)S(1)}, f32[10,32,128]{2,1,0:T(8,128)S(1)}, u32[]{:S(2)}, u32[]{:S(2)}) collective-permute-start(f32[10,32,128]{2,1,0:T(8,128)S(1)} %get-tuple-element.71), channel_id=1, source_target_pairs={{0,2},{1,3},{2,0},{3,1},{4,6},{5,7},{6,4},{7,5},{8,10},{9,11},{10,... | collective-permute-start | bytes 491528 | tf_op jit(solution)/shard_map/ppermute | solution.py:746
  22.6 2.9 %preload.1 = (f32[5,128,128]{2,1,0:T(8,128)S(1)}, f32[16,128,128]{2,1,0:T(8,128)S(1)}, f32[48,128,128]{2,1,0:T(8,128)S(1)}) custom-call(s32[4]{0:T(128)S(1)} %pad_add_fusion.coords.coords_ref, f32[5,128,128]{2,1,0:T(8,128)S(1)} %copy-done, f32[196,128,128]{2,1,0:T(8,128)} %refs_1_.3, f32[196,128,128]{2,1,0:T(8,128)} %refs_1_.3, ...), custom_call_target="tpu_custom_call" | custom-call | flops 2000000000 | bytes 6000000 | tf_op jit(solution)/shard_map/preload/pallas_call | solution.py:100
  25.5 3.7 %collective-permute-done.2.refs_2_ = f32[10,32,128]{2,1,0:T(8,128)S(1)} collective-permute-done((f32[10,32,128]{2,1,0:T(8,128)S(1)}, f32[10,32,128]{2,1,0:T(8,128)S(1)}, u32[]{:S(2)}, u32[]{:S(2)}) %collective-permute-start.2) | collective-permute-done | bytes 163872 | tf_op jit(solution)/shard_map/ppermute | solution.py:746
  29.2 2.3 %collective-permute-done.3.refs_3_ = f32[10,32,128]{2,1,0:T(8,128)S(1)} collective-permute-done((f32[10,32,128]{2,1,0:T(8,128)S(1)}, f32[10,32,128]{2,1,0:T(8,128)S(1)}, u32[]{:S(2)}, u32[]{:S(2)}) %collective-permute-start.3) | collective-permute-done | bytes 163872 | tf_op jit(solution)/shard_map/ppermute | solution.py:746
  34.7 2.8 %collective-permute-start.12 = (f32[8,32,128]{2,1,0:T(8,128)S(1)}, f32[8,32,128]{2,1,0:T(8,128)S(1)}, u32[]{:S(2)}, u32[]{:S(2)}) collective-permute-start(f32[8,32,128]{2,1,0:T(8,128)S(1)} %get-tuple-element.85), channel_id=1, source_target_pairs={{0,3},{1,2},{2,1},{3,0},{4,7},{5,6},{6,5},{7,4},{8,11},{9,10},{10,... | collective-permute-start | bytes 393224 | tf_op jit(solution)/shard_map/ppermute | solution.py:746
  38.5 1.9 %level12.1 = (f32[9,32,128]{2,1,0:T(8,128)S(1)}, f32[9,32,128]{2,1,0:T(8,128)S(1)}) custom-call(s32[4]{0:T(128)S(1)} %pad_add_fusion.coords.coords_ref, f32[8,32,128]{2,1,0:T(8,128)S(1)} %get-tuple-element.78.refs_0_, f32[8,32,128]{2,1,0:T(8,128)S(1)} %collective-permute-done.6.refs_1_, f32[6,128,128]{2,1,0:T(8,128)S(1)} %get-tuple-element.77.refs_2_.refs_3_, ...), custom_call_target="tpu_custom_call" | custom-call | flops 2000000000 | bytes 6000000 | tf_op jit(solution)/shard_map/level12/pallas_call | solution.py:100
  40.4 2.0 %collective-permute-start.9 = (f32[9,32,128]{2,1,0:T(8,128)S(1)}, f32[9,32,128]{2,1,0:T(8,128)S(1)}, u32[]{:S(2)}, u32[]{:S(2)}) collective-permute-start(f32[9,32,128]{2,1,0:T(8,128)S(1)} %get-tuple-element.82), channel_id=1, source_target_pairs={{0,24},{4,28},{8,16},{12,20},{16,8},{20,12},{24,0},{28,4},{32,56},... | collective-permute-start | bytes 442376 | tf_op jit(solution)/shard_map/ppermute | solution.py:742
  43.5 2.8 %collective-permute-start.20 = (f32[16,32,128]{2,1,0:T(8,128)S(1)}, f32[16,32,128]{2,1,0:T(8,128)S(1)}, u32[]{:S(2)}, u32[]{:S(2)}) collective-permute-start(f32[16,32,128]{2,1,0:T(8,128)S(1)} %get-tuple-element.97), channel_id=1, source_target_pairs={{0,3},{1,2},{2,1},{3,0},{4,7},{5,6},{6,5},{7,4},{8,11},{9,10},{10,... | collective-permute-start | bytes 786440 | tf_op jit(solution)/shard_map/ppermute | solution.py:746
  49.6 2.1 %collective-permute-done.13.refs_2_ = f32[5,32,128]{2,1,0:T(8,128)S(1)} collective-permute-done((f32[5,32,128]{2,1,0:T(8,128)S(1)}, f32[5,32,128]{2,1,0:T(8,128)S(1)}, u32[]{:S(2)}, u32[]{:S(2)}) %collective-permute-start.13) | collective-permute-done | bytes 81952 | tf_op jit(solution)/shard_map/ppermute | solution.py:742
  60.0 4.7 %collective-permute-start.21 = (f32[16,32,128]{2,1,0:T(8,128)}, f32[16,32,128]{2,1,0:T(8,128)S(1)}, u32[]{:S(2)}, u32[]{:S(2)}) collective-permute-start(f32[16,32,128]{2,1,0:T(8,128)} %get-tuple-element.98.refs_0_), channel_id=1, source_target_pairs={{0,4},{4,0},{8,12},{12,8},{16,20},{20,16},{24,28},{28,24},{32,36},... | collective-permute-start | bytes 786440 | tf_op jit(solution)/shard_map/ppermute | solution.py:742
  64.7 2.3 %collective-permute-start.24 = (f32[8,32,128]{2,1,0:T(8,128)S(1)}, f32[8,32,128]{2,1,0:T(8,128)S(1)}, u32[]{:S(2)}, u32[]{:S(2)}) collective-permute-start(f32[8,32,128]{2,1,0:T(8,128)S(1)} %get-tuple-element.93), channel_id=1, source_target_pairs={{0,96},{4,100},{8,104},{12,108},{16,112},{20,116},{24,120},{28,124... | collective-permute-start | bytes 393224 | tf_op jit(solution)/shard_map/ppermute | solution.py:742
  67.4 3.7 %collective-permute-done.24.refs_2_ = f32[8,32,128]{2,1,0:T(8,128)S(1)} collective-permute-done((f32[8,32,128]{2,1,0:T(8,128)S(1)}, f32[8,32,128]{2,1,0:T(8,128)S(1)}, u32[]{:S(2)}, u32[]{:S(2)}) %collective-permute-start.24) | collective-permute-done | bytes 131104 | tf_op jit(solution)/shard_map/ppermute | solution.py:742
  72.1 3.6 %level4.1 = (f32[32,128]{1,0:T(8,128)S(1)}, f32[16,2,32,128]{3,2,1,0:T(8,128)}) custom-call(s32[4]{0:T(128)S(1)} %pad_add_fusion.coords.coords_ref, f32[16,32,128]{2,1,0:T(8,128)} %get-tuple-element.98.refs_0_, f32[16,32,128]{2,1,0:T(8,128)S(1)} %collective-permute-done.21.refs_1_, f32[16,32,128]{2,1,0:T(8,128)S(1)} %get-tuple-element.99.refs_2_, ...), custom_call_target="tpu_custom_call" | custom-call | flops 3000000000 | bytes 9000000 | tf_op jit(solution)/shard_map/level4/pallas_call | solution.py:100
  75.7 5.3 %all-to-all-start = ((f32[16,2,32,128]{3,2,1,0:T(8,128)}), f32[16,2,32,128]{3,2,1,0:T(8,128)S(1)}, u32[]{:S(2)}, u32[]{:S(2)}) async-start(f32[16,2,32,128]{3,2,1,0:T(8,128)} %get-tuple-element.102), calls=%async_computation | async-start | bytes 1048576 | tf_op jit(solution)/shard_map/all_to_all | solution.py:751
  83.3 4.4 %level5_own.1.refs_4_ = f32[64,256]{1,0:T(8,128)S(1)} custom-call(s32[4]{0:T(128)S(1)} %pad_add_fusion.coords.coords_ref, f32[16,32,128]{2,1,0:T(8,128)} %get-tuple-element.98.refs_0_, f32[16,32,128]{2,1,0:T(8,128)S(1)} %copy-done.12, f32[16,32,128]{2,1,0:T(8,128)S(1)} %copy-done.21, f32[196,128,128]{2,1,0:T(8,128)} %refs_1_.3), custom_call_target="tpu_custom_call" | custom-call | flops 4000000000 | bytes 12000000 | tf_op jit(solution)/shard_map/level5_own/pallas_call | solution.py:100
  87.8 4.5 %level5_far.1 = (f32[64,256]{1,0:T(8,128)S(1)}, f32[32,128,128]{2,1,0:T(8,128)S(1)}) custom-call(s32[4]{0:T(128)S(1)} %pad_add_fusion.coords.coords_ref, f32[16,32,128]{2,1,0:T(8,128)} %collective-permute-done.22.refs_0_, f32[16,32,128]{2,1,0:T(8,128)S(1)} %collective-permute-done.23.refs_1_, f32[8,32,128]{2,1,0:T(8,128)S(1)} %collective-permute-done.24.refs_2_, ...), custom_call_target="tpu_custom_call" | custom-call | flops 4000000000 | bytes 12000000 | tf_op jit(solution)/shard_map/level5_far/pallas_call | solution.py:100
  97.0 2.5 %level5.1 = (f32[32,128]{1,0:T(8,128)S(1)}, f32[16,32,128]{2,1,0:T(8,128)S(1)}, f32[16,32,128]{2,1,0:T(8,128)S(1)}) custom-call(s32[4]{0:T(128)S(1)} %pad_add_fusion.coords.coords_ref, f32[64,256]{1,0:T(8,128)S(1)} %get-tuple-element.105.refs_0_, f32[16,2,32,128]{3,2,1,0:T(8,128)S(1)} %all-to-all-done.refs_1_, ...), custom_call_target="tpu_custom_call" | custom-call | flops 4000000000 | bytes 12000000 | tf_op jit(solution)/shard_map/level5/pallas_call | solution.py:100
  102.5 6.9 %all-to-all-start.1 = ((f32[16,2,32,128]{3,2,1,0:T(8,128)}), f32[16,2,32,128]{3,2,1,0:T(8,128)S(1)}, u32[]{:S(2)}, u32[]{:S(2)}) async-start(f32[16,2,32,128]{3,2,1,0:T(8,128)} %level4_operand.1), calls=%async_computation.1 | async-start | bytes 1048576 | tf_op jit(solution)/shard_map/all_to_all | solution.py:751
  109.5 4.5 %level5_back.1 = (f32[96,32,128]{2,1,0:T(8,128)S(1)}, f32[48,128,128]{2,1,0:T(8,128)S(1)}) custom-call(s32[4]{0:T(128)S(1)} %pad_add_fusion.coords.coords_ref, f32[32,128]{1,0:T(8,128)S(1)} %get-tuple-element.108.refs_0_, f32[196,128,128]{2,1,0:T(8,128)} %refs_1_.3), custom_call_target="tpu_custom_call" | custom-call | flops 6000000000 | bytes 18000000 | tf_op jit(solution)/shard_map/level5_back/pallas_call | solution.py:100
  116.7 2.9 %all-to-all-done.1.refs_0_ = f32[16,2,32,128]{3,2,1,0:T(8,128)S(1)} async-done(((f32[16,2,32,128]{3,2,1,0:T(8,128)}), f32[16,2,32,128]{3,2,1,0:T(8,128)S(1)}, u32[]{:S(2)}, u32[]{:S(2)}) %all-to-all-start.1) | async-done | bytes 524320 | tf_op jit(solution)/shard_map/all_to_all | solution.py:751
  125.2 2.3 %collective-permute-start.28 = (f32[16,3,32,128]{3,2,1,0:T(8,128)S(1)}, f32[16,3,32,128]{3,2,1,0:T(8,128)S(1)}, u32[]{:S(2)}, u32[]{:S(2)}) collective-permute-start(f32[16,3,32,128]{3,2,1,0:T(8,128)S(1)} %get-tuple-element.116), channel_id=1, source_target_pairs={{0,4},{4,0},{8,12},{12,8},{16,20},{20,16},{24,28},{28,24},{32,36},... | collective-permute-start | bytes 2359304 | tf_op jit(solution)/shard_map/ppermute | solution.py:742
  131.0 3.7 %all-to-all-start.2 = ((f32[16,4,32,128]{3,2,1,0:T(8,128)}), f32[16,4,32,128]{3,2,1,0:T(8,128)S(1)}, u32[]{:S(2)}, u32[]{:S(2)}) async-start(f32[16,4,32,128]{3,2,1,0:T(8,128)} %level3_operand.1), calls=%async_computation.2 | async-start | bytes 2097152 | tf_op jit(solution)/shard_map/all_to_all | solution.py:751
  135.0 3.0 %collective-permute-start.33 = (f32[16,32,128]{2,1,0:T(8,128)}, f32[16,32,128]{2,1,0:T(8,128)}, u32[]{:S(2)}, u32[]{:S(2)}) collective-permute-start(f32[16,32,128]{2,1,0:T(8,128)} %copy-done.9), channel_id=1, source_target_pairs={{0,1},{1,0},{2,3},{3,2},{4,5},{5,4},{6,7},{7,6},{8,9},{9,8},{10,11... | collective-permute-start | bytes 786440 | tf_op jit(solution)/shard_map/ppermute | solution.py:746
  138.0 13.2 %all-to-all-done.2.refs_0_ = f32[16,4,32,128]{3,2,1,0:T(8,128)S(1)} async-done(((f32[16,4,32,128]{3,2,1,0:T(8,128)}), f32[16,4,32,128]{3,2,1,0:T(8,128)S(1)}, u32[]{:S(2)}, u32[]{:S(2)}) %all-to-all-start.2) | async-done | bytes 1048608 | tf_op jit(solution)/shard_map/all_to_all | solution.py:751
  153.2 2.3 %collective-permute-start.37 = (f32[8,32,128]{2,1,0:T(8,128)S(1)}, f32[8,32,128]{2,1,0:T(8,128)S(1)}, u32[]{:S(2)}, u32[]{:S(2)}) collective-permute-start(f32[8,32,128]{2,1,0:T(8,128)S(1)} %get-tuple-element.121), channel_id=1, source_target_pairs={{0,4},{4,0},{8,12},{12,8},{16,20},{20,16},{24,28},{28,24},{32,36},... | collective-permute-start | bytes 393224 | tf_op jit(solution)/shard_map/ppermute | solution.py:742
  157.4 3.0 %collective-permute-start.29 = (f32[8,32,128]{2,1,0:T(8,128)S(1)}, f32[8,32,128]{2,1,0:T(8,128)S(1)}, u32[]{:S(2)}, u32[]{:S(2)}) collective-permute-start(f32[8,32,128]{2,1,0:T(8,128)S(1)} %get-tuple-element.117.refs_0_), channel_id=1, source_target_pairs={{0,1},{1,0},{2,3},{3,2},{4,5},{5,4},{6,7},{7,6},{8,9},{9,8},{10,11... | collective-permute-start | bytes 393224 | tf_op jit(solution)/shard_map/ppermute | solution.py:746
  166.9 2.1 %collective-permute-start.40 = (f32[8,32,128]{2,1,0:T(8,128)S(1)}, f32[8,32,128]{2,1,0:T(8,128)S(1)}, u32[]{:S(2)}, u32[]{:S(2)}) collective-permute-start(f32[8,32,128]{2,1,0:T(8,128)S(1)} %pair_total.1.refs_0_), channel_id=1, source_target_pairs={{0,4},{4,0},{8,12},{12,8},{16,20},{20,16},{24,28},{28,24},{32,36},... | collective-permute-start | bytes 393224 | tf_op jit(solution)/shard_map/ppermute | solution.py:742
  172.3 2.9 %collective-permute-start.41 = (f32[14,32,128]{2,1,0:T(8,128)S(1)}, f32[14,32,128]{2,1,0:T(8,128)S(1)}, u32[]{:S(2)}, u32[]{:S(2)}) collective-permute-start(f32[14,32,128]{2,1,0:T(8,128)S(1)} %get-tuple-element.125.low0), channel_id=1, source_target_pairs={{0,1},{1,0},{2,3},{3,2},{4,5},{5,4},{6,7},{7,6},{8,9},{9,8},{10,11... | collective-permute-start | bytes 688136 | tf_op jit(solution)/shard_map/ppermute | solution.py:746
  175.3 6.2 %leaf_high.1 = (f32[12,128,128]{2,1,0:T(8,128)S(1)}, f32[12,8,128,128]{3,2,1,0:T(8,128)S(1)}, s32[98]{0:T(128)S(1)}) custom-call(s32[4]{0:T(128)S(1)} %pad_add_fusion.coords.coords_ref, s32[12,8]{1,0:T(8,128)S(1)} %copy.14.pattern, f32[128,1536]{1,0:T(8,128)S(1)} %copy-done.2, f32[12,128,128]{2,1,0:T(8,128)S(1)} %copy-done.4, ...), custom_call_target="tpu_custom_call" | custom-call | flops 8000000000 | bytes 24000000 | tf_op jit(solution)/shard_map/leaf_high/pallas_call | solution.py:659
  181.5 3.5 %collective-permute-done.43.low3 = f32[14,32,128]{2,1,0:T(8,128)S(1)} collective-permute-done((f32[14,32,128]{2,1,0:T(8,128)S(1)}, f32[14,32,128]{2,1,0:T(8,128)S(1)}, u32[]{:S(2)}, u32[]{:S(2)}) %collective-permute-start.43) | collective-permute-done | bytes 229408 | tf_op jit(solution)/shard_map/ppermute | solution.py:746
  185.1 4.0 %leaf_low.1 = f32[128,1536]{1,0:T(8,128)} custom-call(s32[4]{0:T(128)S(1)} %pad_add_fusion.coords.coords_ref, s32[12,8]{1,0:T(8,128)S(1)} %copy.14.pattern, s32[98]{0:T(128)S(1)} %get-tuple-element.119.items, f32[14,32,128]{2,1,0:T(8,128)S(1)} %get-tuple-element.125.low0, f32[14,32,128]{2,1,0:T(8,128)S(1)} %collective-permute-done.41.low1, ...), custom_call_target="tpu_custom_call" | custom-call | flops 4000000000 | bytes 12000000 | tf_op jit(solution)/shard_map/leaf_low/pallas_call | solution.py:720
  (157 shorter events, 67.4 us)
Async XLA Ops:
  14.2 7.2 %collective-permute-start.4 = (f32[24,128,128]{2,1,0:T(8,128)S(1)}, f32[24,128,128]{2,1,0:T(8,128)S(1)}, u32[]{:S(2)}, u32[]{:S(2)}) collective-permute-start(f32[24,128,128]{2,1,0:T(8,128)S(1)} %get-tuple-element.74), channel_id=1, source_target_pairs={{0,4},{4,0},{8,12},{12,8},{16,20},{20,16},{24,28},{28,24},{32,36},... | collective-permute-start | bytes 4718600 | tf_op jit(solution)/shard_map/ppermute | solution.py:742
  14.6 17.0 %collective-permute-start.5 = (f32[6,128,128]{2,1,0:T(8,128)S(1)}, f32[6,128,128]{2,1,0:T(8,128)S(1)}, u32[]{:S(2)}, u32[]{:S(2)}) collective-permute-start(f32[6,128,128]{2,1,0:T(8,128)S(1)} %get-tuple-element.77.refs_2_.refs_3_), channel_id=1, source_target_pairs={{0,8},{4,12},{8,0},{12,4},{16,24},{20,28},{24,16},{28,20},{32,40},... | collective-permute-start | bytes 1179656 | tf_op jit(solution)/shard_map/ppermute | solution.py:742
  16.0 18.7 %collective-permute-start.7 = (f32[6,128,128]{2,1,0:T(8,128)S(1)}, f32[6,128,128]{2,1,0:T(8,128)S(1)}, u32[]{:S(2)}, u32[]{:S(2)}) collective-permute-start(f32[6,128,128]{2,1,0:T(8,128)S(1)} %get-tuple-element.77.refs_2_.refs_3_), channel_id=1, source_target_pairs={{0,4},{4,0},{8,12},{12,8},{16,20},{20,16},{24,28},{28,24},{32,36},... | collective-permute-start | bytes 1179656 | tf_op jit(solution)/shard_map/ppermute | solution.py:742
  16.4 9.1 %collective-permute-start.1 = (f32[10,32,128]{2,1,0:T(8,128)S(1)}, f32[10,32,128]{2,1,0:T(8,128)S(1)}, u32[]{:S(2)}, u32[]{:S(2)}) collective-permute-start(f32[10,32,128]{2,1,0:T(8,128)S(1)} %get-tuple-element.70), channel_id=1, source_target_pairs={{0,1},{1,0},{2,3},{3,2},{4,5},{5,4},{6,7},{7,6},{8,9},{9,8},{10,11... | collective-permute-start | bytes 491528 | tf_op jit(solution)/shard_map/ppermute | solution.py:746
  18.1 11.2 %collective-permute-start.2 = (f32[10,32,128]{2,1,0:T(8,128)S(1)}, f32[10,32,128]{2,1,0:T(8,128)S(1)}, u32[]{:S(2)}, u32[]{:S(2)}) collective-permute-start(f32[10,32,128]{2,1,0:T(8,128)S(1)} %get-tuple-element.71), channel_id=1, source_target_pairs={{0,2},{1,3},{2,0},{3,1},{4,6},{5,7},{6,4},{7,5},{8,10},{9,11},{10,... | collective-permute-start | bytes 491528 | tf_op jit(solution)/shard_map/ppermute | solution.py:746
  21.4 10.2 %collective-permute-start.3 = (f32[10,32,128]{2,1,0:T(8,128)S(1)}, f32[10,32,128]{2,1,0:T(8,128)S(1)}, u32[]{:S(2)}, u32[]{:S(2)}) collective-permute-start(f32[10,32,128]{2,1,0:T(8,128)S(1)} %get-tuple-element.72), channel_id=1, source_target_pairs={{0,3},{1,2},{2,1},{3,0},{4,7},{5,6},{6,5},{7,4},{8,11},{9,10},{10,... | collective-permute-start | bytes 491528 | tf_op jit(solution)/shard_map/ppermute | solution.py:746
  33.6 8.8 %collective-permute-start.10 = (f32[8,32,128]{2,1,0:T(8,128)S(1)}, f32[8,32,128]{2,1,0:T(8,128)S(1)}, u32[]{:S(2)}, u32[]{:S(2)}) collective-permute-start(f32[8,32,128]{2,1,0:T(8,128)S(1)} %get-tuple-element.83), channel_id=1, source_target_pairs={{0,1},{1,0},{2,3},{3,2},{4,5},{5,4},{6,7},{7,6},{8,9},{9,8},{10,11... | collective-permute-start | bytes 393224 | tf_op jit(solution)/shard_map/ppermute | solution.py:746
  33.6 9.9 %collective-permute-start.11 = (f32[8,32,128]{2,1,0:T(8,128)S(1)}, f32[8,32,128]{2,1,0:T(8,128)S(1)}, u32[]{:S(2)}, u32[]{:S(2)}) collective-permute-start(f32[8,32,128]{2,1,0:T(8,128)S(1)} %get-tuple-element.84), channel_id=1, source_target_pairs={{0,2},{1,3},{2,0},{3,1},{4,6},{5,7},{6,4},{7,5},{8,10},{9,11},{10,... | collective-permute-start | bytes 393224 | tf_op jit(solution)/shard_map/ppermute | solution.py:746
  34.7 11.6 %collective-permute-start.12 = (f32[8,32,128]{2,1,0:T(8,128)S(1)}, f32[8,32,128]{2,1,0:T(8,128)S(1)}, u32[]{:S(2)}, u32[]{:S(2)}) collective-permute-start(f32[8,32,128]{2,1,0:T(8,128)S(1)} %get-tuple-element.85), channel_id=1, source_target_pairs={{0,3},{1,2},{2,1},{3,0},{4,7},{5,6},{6,5},{7,4},{8,11},{9,10},{10,... | collective-permute-start | bytes 393224 | tf_op jit(solution)/shard_map/ppermute | solution.py:746
  40.4 6.4 %collective-permute-start.9 = (f32[9,32,128]{2,1,0:T(8,128)S(1)}, f32[9,32,128]{2,1,0:T(8,128)S(1)}, u32[]{:S(2)}, u32[]{:S(2)}) collective-permute-start(f32[9,32,128]{2,1,0:T(8,128)S(1)} %get-tuple-element.82), channel_id=1, source_target_pairs={{0,24},{4,28},{8,16},{12,20},{16,8},{20,12},{24,0},{28,4},{32,56},... | collective-permute-start | bytes 442376 | tf_op jit(solution)/shard_map/ppermute | solution.py:742
  42.4 10.3 %collective-permute-start.18 = (f32[16,32,128]{2,1,0:T(8,128)S(1)}, f32[16,32,128]{2,1,0:T(8,128)S(1)}, u32[]{:S(2)}, u32[]{:S(2)}) collective-permute-start(f32[16,32,128]{2,1,0:T(8,128)S(1)} %get-tuple-element.95), channel_id=1, source_target_pairs={{0,1},{1,0},{2,3},{3,2},{4,5},{5,4},{6,7},{7,6},{8,9},{9,8},{10,11... | collective-permute-start | bytes 786440 | tf_op jit(solution)/shard_map/ppermute | solution.py:746
  42.4 12.2 %collective-permute-start.19 = (f32[16,32,128]{2,1,0:T(8,128)S(1)}, f32[16,32,128]{2,1,0:T(8,128)S(1)}, u32[]{:S(2)}, u32[]{:S(2)}) collective-permute-start(f32[16,32,128]{2,1,0:T(8,128)S(1)} %get-tuple-element.96), channel_id=1, source_target_pairs={{0,2},{1,3},{2,0},{3,1},{4,6},{5,7},{6,4},{7,5},{8,10},{9,11},{10,... | collective-permute-start | bytes 786440 | tf_op jit(solution)/shard_map/ppermute | solution.py:746
  43.5 13.6 %collective-permute-start.20 = (f32[16,32,128]{2,1,0:T(8,128)S(1)}, f32[16,32,128]{2,1,0:T(8,128)S(1)}, u32[]{:S(2)}, u32[]{:S(2)}) collective-permute-start(f32[16,32,128]{2,1,0:T(8,128)S(1)} %get-tuple-element.97), channel_id=1, source_target_pairs={{0,3},{1,2},{2,1},{3,0},{4,7},{5,6},{6,5},{7,4},{8,11},{9,10},{10,... | collective-permute-start | bytes 786440 | tf_op jit(solution)/shard_map/ppermute | solution.py:746
  49.3 9.4 %collective-permute-start.17 = (f32[8,32,128]{2,1,0:T(8,128)S(1)}, f32[8,32,128]{2,1,0:T(8,128)S(1)}, u32[]{:S(2)}, u32[]{:S(2)}) collective-permute-start(f32[8,32,128]{2,1,0:T(8,128)S(1)} %get-tuple-element.93), channel_id=1, source_target_pairs={{0,32},{4,36},{8,40},{12,44},{16,48},{20,52},{24,56},{28,60},{32,0... | collective-permute-start | bytes 393224 | tf_op jit(solution)/shard_map/ppermute | solution.py:742
  60.0 12.1 %collective-permute-start.21 = (f32[16,32,128]{2,1,0:T(8,128)}, f32[16,32,128]{2,1,0:T(8,128)S(1)}, u32[]{:S(2)}, u32[]{:S(2)}) collective-permute-start(f32[16,32,128]{2,1,0:T(8,128)} %get-tuple-element.98.refs_0_), channel_id=1, source_target_pairs={{0,4},{4,0},{8,12},{12,8},{16,20},{20,16},{24,28},{28,24},{32,36},... | collective-permute-start | bytes 786440 | tf_op jit(solution)/shard_map/ppermute | solution.py:742
  64.7 6.3 %collective-permute-start.24 = (f32[8,32,128]{2,1,0:T(8,128)S(1)}, f32[8,32,128]{2,1,0:T(8,128)S(1)}, u32[]{:S(2)}, u32[]{:S(2)}) collective-permute-start(f32[8,32,128]{2,1,0:T(8,128)S(1)} %get-tuple-element.93), channel_id=1, source_target_pairs={{0,96},{4,100},{8,104},{12,108},{16,112},{20,116},{24,120},{28,124... | collective-permute-start | bytes 393224 | tf_op jit(solution)/shard_map/ppermute | solution.py:742
  67.0 14.0 %collective-permute-start.22 = (f32[16,32,128]{2,1,0:T(8,128)}, f32[16,32,128]{2,1,0:T(8,128)}, u32[]{:S(2)}, u32[]{:S(2)}) collective-permute-start(f32[16,32,128]{2,1,0:T(8,128)} %get-tuple-element.98.refs_0_), channel_id=1, source_target_pairs={{0,96},{4,100},{8,104},{12,108},{16,112},{20,116},{24,120},{28,124... | collective-permute-start | bytes 786440 | tf_op jit(solution)/shard_map/ppermute | solution.py:742
  71.1 16.7 %collective-permute-start.25 = (f32[8,32,128]{2,1,0:T(8,128)S(1)}, f32[8,32,128]{2,1,0:T(8,128)S(1)}, u32[]{:S(2)}, u32[]{:S(2)}) collective-permute-start(f32[8,32,128]{2,1,0:T(8,128)S(1)} %collective-permute-done.24.refs_2_), channel_id=1, source_target_pairs={{0,4},{4,0},{8,12},{12,8},{16,20},{20,16},{24,28},{28,24},{32,36},... | collective-permute-start | bytes 393224 | tf_op jit(solution)/shard_map/ppermute | solution.py:742
  75.7 17.9 %all-to-all-start = ((f32[16,2,32,128]{3,2,1,0:T(8,128)}), f32[16,2,32,128]{3,2,1,0:T(8,128)S(1)}, u32[]{:S(2)}, u32[]{:S(2)}) async-start(f32[16,2,32,128]{3,2,1,0:T(8,128)} %get-tuple-element.102), calls=%async_computation | async-start | bytes 1048576 | tf_op jit(solution)/shard_map/all_to_all | solution.py:751
  81.0 6.7 %collective-permute-start.23 = (f32[16,32,128]{2,1,0:T(8,128)}, f32[16,32,128]{2,1,0:T(8,128)S(1)}, u32[]{:S(2)}, u32[]{:S(2)}) collective-permute-start(f32[16,32,128]{2,1,0:T(8,128)} %collective-permute-done.22.refs_0_), channel_id=1, source_target_pairs={{0,4},{4,0},{8,12},{12,8},{16,20},{20,16},{24,28},{28,24},{32,36},... | collective-permute-start | bytes 786440 | tf_op jit(solution)/shard_map/ppermute | solution.py:742
  102.5 17.1 %all-to-all-start.1 = ((f32[16,2,32,128]{3,2,1,0:T(8,128)}), f32[16,2,32,128]{3,2,1,0:T(8,128)S(1)}, u32[]{:S(2)}, u32[]{:S(2)}) async-start(f32[16,2,32,128]{3,2,1,0:T(8,128)} %level4_operand.1), calls=%async_computation.1 | async-start | bytes 1048576 | tf_op jit(solution)/shard_map/all_to_all | solution.py:751
  131.0 20.2 %all-to-all-start.2 = ((f32[16,4,32,128]{3,2,1,0:T(8,128)}), f32[16,4,32,128]{3,2,1,0:T(8,128)S(1)}, u32[]{:S(2)}, u32[]{:S(2)}) async-start(f32[16,4,32,128]{3,2,1,0:T(8,128)} %level3_operand.1), calls=%async_computation.2 | async-start | bytes 2097152 | tf_op jit(solution)/shard_map/all_to_all | solution.py:751
  134.6 20.8 %collective-permute-start.35 = (f32[16,32,128]{2,1,0:T(8,128)}, f32[16,32,128]{2,1,0:T(8,128)}, u32[]{:S(2)}, u32[]{:S(2)}) collective-permute-start(f32[16,32,128]{2,1,0:T(8,128)} %copy-done.9), channel_id=1, source_target_pairs={{0,3},{1,2},{2,1},{3,0},{4,7},{5,6},{6,5},{7,4},{8,11},{9,10},{10,... | collective-permute-start | bytes 786440 | tf_op jit(solution)/shard_map/ppermute | solution.py:746
  135.0 20.4 %collective-permute-start.34 = (f32[16,32,128]{2,1,0:T(8,128)}, f32[16,32,128]{2,1,0:T(8,128)}, u32[]{:S(2)}, u32[]{:S(2)}) collective-permute-start(f32[16,32,128]{2,1,0:T(8,128)} %copy-done.9), channel_id=1, source_target_pairs={{0,2},{1,3},{2,0},{3,1},{4,6},{5,7},{6,4},{7,5},{8,10},{9,11},{10,... | collective-permute-start | bytes 786440 | tf_op jit(solution)/shard_map/ppermute | solution.py:746
  135.0 20.4 %collective-permute-start.33 = (f32[16,32,128]{2,1,0:T(8,128)}, f32[16,32,128]{2,1,0:T(8,128)}, u32[]{:S(2)}, u32[]{:S(2)}) collective-permute-start(f32[16,32,128]{2,1,0:T(8,128)} %copy-done.9), channel_id=1, source_target_pairs={{0,1},{1,0},{2,3},{3,2},{4,5},{5,4},{6,7},{7,6},{8,9},{9,8},{10,11... | collective-permute-start | bytes 786440 | tf_op jit(solution)/shard_map/ppermute | solution.py:746
  157.1 9.0 %collective-permute-start.31 = (f32[8,32,128]{2,1,0:T(8,128)S(1)}, f32[8,32,128]{2,1,0:T(8,128)S(1)}, u32[]{:S(2)}, u32[]{:S(2)}) collective-permute-start(f32[8,32,128]{2,1,0:T(8,128)S(1)} %get-tuple-element.117.refs_0_), channel_id=1, source_target_pairs={{0,3},{1,2},{2,1},{3,0},{4,7},{5,6},{6,5},{7,4},{8,11},{9,10},{10,... | collective-permute-start | bytes 393224 | tf_op jit(solution)/shard_map/ppermute | solution.py:746
  157.4 8.7 %collective-permute-start.30 = (f32[8,32,128]{2,1,0:T(8,128)S(1)}, f32[8,32,128]{2,1,0:T(8,128)S(1)}, u32[]{:S(2)}, u32[]{:S(2)}) collective-permute-start(f32[8,32,128]{2,1,0:T(8,128)S(1)} %get-tuple-element.117.refs_0_), channel_id=1, source_target_pairs={{0,2},{1,3},{2,0},{3,1},{4,6},{5,7},{6,4},{7,5},{8,10},{9,11},{10,... | collective-permute-start | bytes 393224 | tf_op jit(solution)/shard_map/ppermute | solution.py:746
  157.4 8.7 %collective-permute-start.29 = (f32[8,32,128]{2,1,0:T(8,128)S(1)}, f32[8,32,128]{2,1,0:T(8,128)S(1)}, u32[]{:S(2)}, u32[]{:S(2)}) collective-permute-start(f32[8,32,128]{2,1,0:T(8,128)S(1)} %get-tuple-element.117.refs_0_), channel_id=1, source_target_pairs={{0,1},{1,0},{2,3},{3,2},{4,5},{5,4},{6,7},{7,6},{8,9},{9,8},{10,11... | collective-permute-start | bytes 393224 | tf_op jit(solution)/shard_map/ppermute | solution.py:746
  164.3 10.9 %collective-permute-start.36 = (f32[4,16,32,128]{3,2,1,0:T(8,128)S(1)}, f32[4,16,32,128]{3,2,1,0:T(8,128)S(1)}, u32[]{:S(2)}, u32[]{:S(2)}) collective-permute-start(f32[4,16,32,128]{3,2,1,0:T(8,128)S(1)} %pack.3.x5m), channel_id=1, source_target_pairs={{0,4},{4,0},{8,12},{12,8},{16,20},{20,16},{24,28},{28,24},{32,36},... | collective-permute-start | bytes 3145736 | tf_op jit(solution)/shard_map/ppermute | solution.py:742
  171.8 13.2 %collective-permute-start.43 = (f32[14,32,128]{2,1,0:T(8,128)S(1)}, f32[14,32,128]{2,1,0:T(8,128)S(1)}, u32[]{:S(2)}, u32[]{:S(2)}) collective-permute-start(f32[14,32,128]{2,1,0:T(8,128)S(1)} %get-tuple-element.125.low0), channel_id=1, source_target_pairs={{0,3},{1,2},{2,1},{3,0},{4,7},{5,6},{6,5},{7,4},{8,11},{9,10},{10,... | collective-permute-start | bytes 688136 | tf_op jit(solution)/shard_map/ppermute | solution.py:746
  172.1 12.9 %collective-permute-start.42 = (f32[14,32,128]{2,1,0:T(8,128)S(1)}, f32[14,32,128]{2,1,0:T(8,128)S(1)}, u32[]{:S(2)}, u32[]{:S(2)}) collective-permute-start(f32[14,32,128]{2,1,0:T(8,128)S(1)} %get-tuple-element.125.low0), channel_id=1, source_target_pairs={{0,2},{1,3},{2,0},{3,1},{4,6},{5,7},{6,4},{7,5},{8,10},{9,11},{10,... | collective-permute-start | bytes 688136 | tf_op jit(solution)/shard_map/ppermute | solution.py:746
  172.3 12.8 %collective-permute-start.41 = (f32[14,32,128]{2,1,0:T(8,128)S(1)}, f32[14,32,128]{2,1,0:T(8,128)S(1)}, u32[]{:S(2)}, u32[]{:S(2)}) collective-permute-start(f32[14,32,128]{2,1,0:T(8,128)S(1)} %get-tuple-element.125.low0), channel_id=1, source_target_pairs={{0,1},{1,0},{2,3},{3,2},{4,5},{5,4},{6,7},{7,6},{8,9},{9,8},{10,11... | collective-permute-start | bytes 688136 | tf_op jit(solution)/shard_map/ppermute | solution.py:746
  (44 other events, 280.7 us)

commit v5 on v4

--- a/solution.py
+++ b/solution.py
@@ -76,7 +76,7 @@
 
 def cost(us):
     return pl.CostEstimate(
-        flops=int(us * 1e9), bytes_accessed=int(us * 3e6), transcendentals=0
+        flops=int(us * 3e8), bytes_accessed=int(us * 1e6), transcendentals=0
     )
 
 
@@ -593,7 +593,7 @@
 
 
 LOW = 14
-AT_ONCE = 4
+AT_ONCE = 8
 
 
 def pack_kernel(coords, part0, part1, part2, part3, out):

time: 190 us -> 189 us (level)
  waiting for transfers between devices: 44.4 us -> 51.3 us
  local copies, waits for them, and re-layouts: 16.6 us -> 12.1 us
  Pallas kernels: 57.7 us -> 54.2 us
    unnamed x59 -> x57, local copies, waits for them, and re-layouts: 16.6 us -> 12.1 us
    ppermute x26, waiting for transfers between devices: 17.3 us -> 20.7 us  [across(): return lax.ppermute(value, 'leaf', [(i, i ^ mask) for i in range(32)])]
    pallas_call x25, Pallas kernels: 42.1 us -> 38.7 us  [call(): pl.pallas_call(kernel, name=name, out_shape=[jax.ShapeDtypeStruct(shape,...]
    all_to_all x3, starting transfers between devices: 15.9 us -> 13 us  [swap16(): return lax.all_to_all(value, 'leaf', 0, 0, axis_index_groups=groups)]
    ppermute x26, starting transfers between devices: 30.3 us -> 33.2 us  [across(): return lax.ppermute(value, 'leaf', [(i, i ^ mask) for i in range(32)])]
    ppermute x18, waiting for transfers between devices: 11.1 us -> 13.3 us  [across_front(): return lax.ppermute(value, 'front', [(i, i ^ mask) for i in range(4)])]
where the time goes in v5:
time: 189 us; the launch traced here: 188 us
  starting transfers between devices  68.9 us (36%)
  Pallas kernels  54.2 us (29%)
  waiting for transfers between devices  51.3 us (27%)
  local copies, waits for them, and re-layouts  12.1 us (6%)
    pallas_call x25, Pallas kernels, call(): pl.pallas_call(kernel, name=name, out_shape=[jax.ShapeDtypeStruct(shape,...  38.7 us
    ppermute x26, starting transfers between devices, across(): return lax.ppermute(value, 'leaf', [(i, i ^ mask) for i in range(32)])  33.2 us
    ppermute x18, starting transfers between devices, across_front(): return lax.ppermute(value, 'front', [(i, i ^ mask) for i in range(4)])  22.7 us
    ppermute x26, waiting for transfers between devices, across(): return lax.ppermute(value, 'leaf', [(i, i ^ mask) for i in range(32)])  20.7 us
    all_to_all x3, waiting for transfers between devices, swap16(): return lax.all_to_all(value, 'leaf', 0, 0, axis_index_groups=groups)  17.3 us
    ppermute x18, waiting for transfers between devices, across_front(): return lax.ppermute(value, 'front', [(i, i ^ mask) for i in range(4)])  13.3 us
    all_to_all x3, starting transfers between devices, swap16(): return lax.all_to_all(value, 'leaf', 0, 0, axis_index_groups=groups)  13 us
    unnamed x57, local copies, waits for them, and re-layouts  12.1 us
  transfers between devices with their start and end apart: 47, of which 20 were waited for; matrix products, arithmetic and copies ran while one was open for 0% of the time, Pallas kernels for 20%

profile of v5, /device:TPU:1, one launch (start us, length us, event | category | flops | bytes accessed | tf_op | source)
XLA Modules:
  0.0 188.0 jit_solution(16328583356424816502)
XLA Ops:
  4.6 5.4 %leaf_forward.1 = (f32[10,128,128]{2,1,0:T(8,128)S(1)}, f32[10,128,128]{2,1,0:T(8,128)S(1)}, f32[24,128,128]{2,1,0:T(8,128)S(1)}, f32[24,128,128]{2,1,0:T(8,128)S(1)}) custom-call(s32[4]{0:T(128)S(1)} %pad_add_fusion.coords.coords_ref, s32[12,8]{1,0:T(8,128)S(1)} %copy.14.pattern, f32[128,1536]{1,0:T(8,128)S(1)} %copy-done.3, f32[12,128,128]{2,1,0:T(8,128)S(1)} %copy-done, ...), custom_call_target="tpu_custom_call" | custom-call | flops 1800000000 | bytes 6000000 | tf_op jit(solution)/shard_map/leaf_forward/pallas_call | solution.py:209
  17.6 3.3 %collective-permute-start.2 = (f32[10,32,128]{2,1,0:T(8,128)S(1)}, f32[10,32,128]{2,1,0:T(8,128)S(1)}, u32[]{:S(2)}, u32[]{:S(2)}) collective-permute-start(f32[10,32,128]{2,1,0:T(8,128)S(1)} %get-tuple-element.71), channel_id=1, source_target_pairs={{0,2},{1,3},{2,0},{3,1},{4,6},{5,7},{6,4},{7,5},{8,10},{9,11},{10,... | collective-permute-start | bytes 491528 | tf_op jit(solution)/shard_map/ppermute | solution.py:746
  23.1 2.9 %preload.1 = (f32[5,128,128]{2,1,0:T(8,128)S(1)}, f32[16,128,128]{2,1,0:T(8,128)S(1)}, f32[48,128,128]{2,1,0:T(8,128)S(1)}) custom-call(s32[4]{0:T(128)S(1)} %pad_add_fusion.coords.coords_ref, f32[5,128,128]{2,1,0:T(8,128)S(1)} %copy-done.9, f32[196,128,128]{2,1,0:T(8,128)} %refs_1_.3, f32[196,128,128]{2,1,0:T(8,128)} %refs_1_.3, ...), custom_call_target="tpu_custom_call" | custom-call | flops 600000000 | bytes 2000000 | tf_op jit(solution)/shard_map/preload/pallas_call | solution.py:100
  26.0 2.4 %collective-permute-done.2.refs_2_ = f32[10,32,128]{2,1,0:T(8,128)S(1)} collective-permute-done((f32[10,32,128]{2,1,0:T(8,128)S(1)}, f32[10,32,128]{2,1,0:T(8,128)S(1)}, u32[]{:S(2)}, u32[]{:S(2)}) %collective-permute-start.2) | collective-permute-done | bytes 163872 | tf_op jit(solution)/shard_map/ppermute | solution.py:746
  28.4 2.7 %collective-permute-done.3.refs_3_ = f32[10,32,128]{2,1,0:T(8,128)S(1)} collective-permute-done((f32[10,32,128]{2,1,0:T(8,128)S(1)}, f32[10,32,128]{2,1,0:T(8,128)S(1)}, u32[]{:S(2)}, u32[]{:S(2)}) %collective-permute-start.3) | collective-permute-done | bytes 163872 | tf_op jit(solution)/shard_map/ppermute | solution.py:746
  34.0 3.0 %collective-permute-start.12 = (f32[8,32,128]{2,1,0:T(8,128)S(1)}, f32[8,32,128]{2,1,0:T(8,128)S(1)}, u32[]{:S(2)}, u32[]{:S(2)}) collective-permute-start(f32[8,32,128]{2,1,0:T(8,128)S(1)} %get-tuple-element.85), channel_id=1, source_target_pairs={{0,3},{1,2},{2,1},{3,0},{4,7},{5,6},{6,5},{7,4},{8,11},{9,10},{10,... | collective-permute-start | bytes 393224 | tf_op jit(solution)/shard_map/ppermute | solution.py:746
  43.0 2.8 %collective-permute-start.20 = (f32[16,32,128]{2,1,0:T(8,128)S(1)}, f32[16,32,128]{2,1,0:T(8,128)S(1)}, u32[]{:S(2)}, u32[]{:S(2)}) collective-permute-start(f32[16,32,128]{2,1,0:T(8,128)S(1)} %get-tuple-element.97), channel_id=1, source_target_pairs={{0,3},{1,2},{2,1},{3,0},{4,7},{5,6},{6,5},{7,4},{8,11},{9,10},{10,... | collective-permute-start | bytes 786440 | tf_op jit(solution)/shard_map/ppermute | solution.py:746
  49.1 2.1 %collective-permute-done.13.refs_2_ = f32[5,32,128]{2,1,0:T(8,128)S(1)} collective-permute-done((f32[5,32,128]{2,1,0:T(8,128)S(1)}, f32[5,32,128]{2,1,0:T(8,128)S(1)}, u32[]{:S(2)}, u32[]{:S(2)}) %collective-permute-start.13) | collective-permute-done | bytes 81952 | tf_op jit(solution)/shard_map/ppermute | solution.py:742
  58.8 4.8 %collective-permute-start.21 = (f32[16,32,128]{2,1,0:T(8,128)S(1)}, f32[16,32,128]{2,1,0:T(8,128)S(1)}, u32[]{:S(2)}, u32[]{:S(2)}) collective-permute-start(f32[16,32,128]{2,1,0:T(8,128)S(1)} %get-tuple-element.98.refs_0_), channel_id=1, source_target_pairs={{0,4},{4,0},{8,12},{12,8},{16,20},{20,16},{24,28},{28,24},{32,36},... | collective-permute-start | bytes 786440 | tf_op jit(solution)/shard_map/ppermute | solution.py:742
  63.6 2.3 %collective-permute-start.22 = (f32[16,32,128]{2,1,0:T(8,128)S(1)}, f32[16,32,128]{2,1,0:T(8,128)S(1)}, u32[]{:S(2)}, u32[]{:S(2)}) collective-permute-start(f32[16,32,128]{2,1,0:T(8,128)S(1)} %get-tuple-element.98.refs_0_), channel_id=1, source_target_pairs={{0,96},{4,100},{8,104},{12,108},{16,112},{20,116},{24,120},{28,124... | collective-permute-start | bytes 786440 | tf_op jit(solution)/shard_map/ppermute | solution.py:742
  65.9 2.6 %level4.1 = (f32[32,128]{1,0:T(8,128)S(1)}, f32[16,2,32,128]{3,2,1,0:T(8,128)}) custom-call(s32[4]{0:T(128)S(1)} %pad_add_fusion.coords.coords_ref, f32[16,32,128]{2,1,0:T(8,128)S(1)} %get-tuple-element.98.refs_0_, f32[16,32,128]{2,1,0:T(8,128)S(1)} %collective-permute-done.21.refs_1_, f32[16,32,128]{2,1,0:T(8,128)S(1)} %get-tuple-element.99.refs_2_, ...), custom_call_target="tpu_custom_call" | custom-call | flops 900000000 | bytes 3000000 | tf_op jit(solution)/shard_map/level4/pallas_call | solution.py:100
  68.5 4.3 %all-to-all-start = ((f32[16,2,32,128]{3,2,1,0:T(8,128)}), f32[16,2,32,128]{3,2,1,0:T(8,128)S(1)}, u32[]{:S(2)}, u32[]{:S(2)}) async-start(f32[16,2,32,128]{3,2,1,0:T(8,128)} %get-tuple-element.102), calls=%async_computation | async-start | bytes 1048576 | tf_op jit(solution)/shard_map/all_to_all | solution.py:751
  72.9 2.6 %collective-permute-start.24 = (f32[8,32,128]{2,1,0:T(8,128)S(1)}, f32[8,32,128]{2,1,0:T(8,128)S(1)}, u32[]{:S(2)}, u32[]{:S(2)}) collective-permute-start(f32[8,32,128]{2,1,0:T(8,128)S(1)} %get-tuple-element.93), channel_id=1, source_target_pairs={{0,96},{4,100},{8,104},{12,108},{16,112},{20,116},{24,120},{28,124... | collective-permute-start | bytes 393224 | tf_op jit(solution)/shard_map/ppermute | solution.py:742
  76.7 7.5 %collective-permute-done.24.refs_2_ = f32[8,32,128]{2,1,0:T(8,128)S(1)} collective-permute-done((f32[8,32,128]{2,1,0:T(8,128)S(1)}, f32[8,32,128]{2,1,0:T(8,128)S(1)}, u32[]{:S(2)}, u32[]{:S(2)}) %collective-permute-start.24) | collective-permute-done | bytes 131104 | tf_op jit(solution)/shard_map/ppermute | solution.py:742
  85.7 3.5 %level5_own.1.refs_4_ = f32[64,256]{1,0:T(8,128)S(1)} custom-call(s32[4]{0:T(128)S(1)} %pad_add_fusion.coords.coords_ref, f32[16,32,128]{2,1,0:T(8,128)S(1)} %get-tuple-element.98.refs_0_, f32[16,32,128]{2,1,0:T(8,128)S(1)} %collective-permute-done.21.refs_1_, f32[16,32,128]{2,1,0:T(8,128)S(1)} %get-tuple-element.99.refs_2_, f32[196,128,128]{2,1,0:T(8,128)} %refs_1_.3), custom_call_target="tpu_custom_call" | custom-call | flops 1200000000 | bytes 4000000 | tf_op jit(solution)/shard_map/level5_own/pallas_call | solution.py:100
  89.2 3.5 %level5_far.1 = (f32[64,256]{1,0:T(8,128)S(1)}, f32[32,128,128]{2,1,0:T(8,128)S(1)}) custom-call(s32[4]{0:T(128)S(1)} %pad_add_fusion.coords.coords_ref, f32[16,32,128]{2,1,0:T(8,128)S(1)} %collective-permute-done.22.refs_0_, f32[16,32,128]{2,1,0:T(8,128)S(1)} %collective-permute-done.23.refs_1_, f32[8,32,128]{2,1,0:T(8,128)S(1)} %collective-permute-done.24.refs_2_, ...), custom_call_target="tpu_custom_call" | custom-call | flops 1200000000 | bytes 4000000 | tf_op jit(solution)/shard_map/level5_far/pallas_call | solution.py:100
  97.6 2.5 %level5.1 = (f32[32,128]{1,0:T(8,128)S(1)}, f32[16,32,128]{2,1,0:T(8,128)S(1)}, f32[16,32,128]{2,1,0:T(8,128)S(1)}) custom-call(s32[4]{0:T(128)S(1)} %pad_add_fusion.coords.coords_ref, f32[64,256]{1,0:T(8,128)S(1)} %get-tuple-element.105.refs_0_, f32[16,2,32,128]{3,2,1,0:T(8,128)S(1)} %all-to-all-done.refs_1_, ...), custom_call_target="tpu_custom_call" | custom-call | flops 1200000000 | bytes 4000000 | tf_op jit(solution)/shard_map/level5/pallas_call | solution.py:100
  103.0 4.4 %all-to-all-start.1 = ((f32[16,2,32,128]{3,2,1,0:T(8,128)}), f32[16,2,32,128]{3,2,1,0:T(8,128)S(1)}, u32[]{:S(2)}, u32[]{:S(2)}) async-start(f32[16,2,32,128]{3,2,1,0:T(8,128)} %level4_operand.1), calls=%async_computation.1 | async-start | bytes 1048576 | tf_op jit(solution)/shard_map/all_to_all | solution.py:751
  107.4 4.5 %level5_back.1 = (f32[96,32,128]{2,1,0:T(8,128)S(1)}, f32[48,128,128]{2,1,0:T(8,128)S(1)}) custom-call(s32[4]{0:T(128)S(1)} %pad_add_fusion.coords.coords_ref, f32[32,128]{1,0:T(8,128)S(1)} %get-tuple-element.108.refs_0_, f32[196,128,128]{2,1,0:T(8,128)} %refs_1_.3), custom_call_target="tpu_custom_call" | custom-call | flops 1800000000 | bytes 6000000 | tf_op jit(solution)/shard_map/level5_back/pallas_call | solution.py:100
  113.5 4.1 %all-to-all-done.1.refs_0_ = f32[16,2,32,128]{3,2,1,0:T(8,128)S(1)} async-done(((f32[16,2,32,128]{3,2,1,0:T(8,128)}), f32[16,2,32,128]{3,2,1,0:T(8,128)S(1)}, u32[]{:S(2)}, u32[]{:S(2)}) %all-to-all-start.1) | async-done | bytes 524320 | tf_op jit(solution)/shard_map/all_to_all | solution.py:751
  121.7 2.3 %collective-permute-start.28 = (f32[16,3,32,128]{3,2,1,0:T(8,128)S(1)}, f32[16,3,32,128]{3,2,1,0:T(8,128)S(1)}, u32[]{:S(2)}, u32[]{:S(2)}) collective-permute-start(f32[16,3,32,128]{3,2,1,0:T(8,128)S(1)} %get-tuple-element.116), channel_id=1, source_target_pairs={{0,4},{4,0},{8,12},{12,8},{16,20},{20,16},{24,28},{28,24},{32,36},... | collective-permute-start | bytes 2359304 | tf_op jit(solution)/shard_map/ppermute | solution.py:742
  127.5 4.3 %all-to-all-start.2 = ((f32[16,4,32,128]{3,2,1,0:T(8,128)}), f32[16,4,32,128]{3,2,1,0:T(8,128)}, u32[]{:S(2)}, u32[]{:S(2)}) async-start(f32[16,4,32,128]{3,2,1,0:T(8,128)} %copy-done.2), calls=%async_computation.2 | async-start | bytes 2097152 | tf_op jit(solution)/shard_map/all_to_all | solution.py:751
  132.5 2.8 %collective-permute-start.33 = (f32[16,32,128]{2,1,0:T(8,128)}, f32[16,32,128]{2,1,0:T(8,128)}, u32[]{:S(2)}, u32[]{:S(2)}) collective-permute-start(f32[16,32,128]{2,1,0:T(8,128)} %copy-done.12), channel_id=1, source_target_pairs={{0,1},{1,0},{2,3},{3,2},{4,5},{5,4},{6,7},{7,6},{8,9},{9,8},{10,11... | collective-permute-start | bytes 786440 | tf_op jit(solution)/shard_map/ppermute | solution.py:746
  135.2 13.2 %all-to-all-done.2.refs_0_ = f32[16,4,32,128]{3,2,1,0:T(8,128)} async-done(((f32[16,4,32,128]{3,2,1,0:T(8,128)}), f32[16,4,32,128]{3,2,1,0:T(8,128)}, u32[]{:S(2)}, u32[]{:S(2)}) %all-to-all-start.2) | async-done | bytes 1048608 | tf_op jit(solution)/shard_map/all_to_all | solution.py:751
  148.5 2.2 %level3_back.1 = (f32[32,128]{1,0:T(8,128)S(1)}, f32[8,32,128]{2,1,0:T(8,128)S(1)}, f32[8,32,128]{2,1,0:T(8,128)S(1)}, f32[8,32,128]{2,1,0:T(8,128)S(1)}) custom-call(s32[4]{0:T(128)S(1)} %pad_add_fusion.coords.coords_ref, f32[16,4,32,128]{3,2,1,0:T(8,128)} %all-to-all-done.2.refs_0_, f32[32,128]{1,0:T(8,128)S(1)} %get-tuple-element.87.refs_0_.refs_1_, ...), custom_call_target="tpu_custom_call" | custom-call | flops 450000000 | bytes 1500000 | tf_op jit(solution)/shard_map/level3_back/pallas_call | solution.py:100
  150.7 2.3 %collective-permute-start.37 = (f32[8,32,128]{2,1,0:T(8,128)S(1)}, f32[8,32,128]{2,1,0:T(8,128)S(1)}, u32[]{:S(2)}, u32[]{:S(2)}) collective-permute-start(f32[8,32,128]{2,1,0:T(8,128)S(1)} %get-tuple-element.121), channel_id=1, source_target_pairs={{0,4},{4,0},{8,12},{12,8},{16,20},{20,16},{24,28},{28,24},{32,36},... | collective-permute-start | bytes 393224 | tf_op jit(solution)/shard_map/ppermute | solution.py:742
  156.4 2.8 %collective-permute-start.29 = (f32[8,32,128]{2,1,0:T(8,128)S(1)}, f32[8,32,128]{2,1,0:T(8,128)S(1)}, u32[]{:S(2)}, u32[]{:S(2)}) collective-permute-start(f32[8,32,128]{2,1,0:T(8,128)S(1)} %get-tuple-element.117.refs_0_), channel_id=1, source_target_pairs={{0,1},{1,0},{2,3},{3,2},{4,5},{5,4},{6,7},{7,6},{8,9},{9,8},{10,11... | collective-permute-start | bytes 393224 | tf_op jit(solution)/shard_map/ppermute | solution.py:746
  161.6 3.2 %collective-permute-done.31.refs_3_.refs_4_ = f32[8,32,128]{2,1,0:T(8,128)S(1)} collective-permute-done((f32[8,32,128]{2,1,0:T(8,128)S(1)}, f32[8,32,128]{2,1,0:T(8,128)S(1)}, u32[]{:S(2)}, u32[]{:S(2)}) %collective-permute-start.31) | collective-permute-done | bytes 131104 | tf_op jit(solution)/shard_map/ppermute | solution.py:746
  171.2 2.8 %collective-permute-start.41 = (f32[14,32,128]{2,1,0:T(8,128)S(1)}, f32[14,32,128]{2,1,0:T(8,128)S(1)}, u32[]{:S(2)}, u32[]{:S(2)}) collective-permute-start(f32[14,32,128]{2,1,0:T(8,128)S(1)} %get-tuple-element.125.low0), channel_id=1, source_target_pairs={{0,1},{1,0},{2,3},{3,2},{4,5},{5,4},{6,7},{7,6},{8,9},{9,8},{10,11... | collective-permute-start | bytes 688136 | tf_op jit(solution)/shard_map/ppermute | solution.py:746
  174.1 6.1 %leaf_high.1 = (f32[12,128,128]{2,1,0:T(8,128)S(1)}, f32[12,8,128,128]{3,2,1,0:T(8,128)S(1)}, s32[98]{0:T(128)S(1)}) custom-call(s32[4]{0:T(128)S(1)} %pad_add_fusion.coords.coords_ref, s32[12,8]{1,0:T(8,128)S(1)} %copy.14.pattern, f32[128,1536]{1,0:T(8,128)S(1)} %copy-done.4, f32[12,128,128]{2,1,0:T(8,128)S(1)} %copy-done.1, ...), custom_call_target="tpu_custom_call" | custom-call | flops 2400000000 | bytes 8000000 | tf_op jit(solution)/shard_map/leaf_high/pallas_call | solution.py:659
  180.2 3.4 %collective-permute-done.43.low3 = f32[14,32,128]{2,1,0:T(8,128)S(1)} collective-permute-done((f32[14,32,128]{2,1,0:T(8,128)S(1)}, f32[14,32,128]{2,1,0:T(8,128)S(1)}, u32[]{:S(2)}, u32[]{:S(2)}) %collective-permute-start.43) | collective-permute-done | bytes 229408 | tf_op jit(solution)/shard_map/ppermute | solution.py:746
  183.9 3.9 %leaf_low.1 = f32[128,1536]{1,0:T(8,128)} custom-call(s32[4]{0:T(128)S(1)} %pad_add_fusion.coords.coords_ref, s32[12,8]{1,0:T(8,128)S(1)} %copy.14.pattern, s32[98]{0:T(128)S(1)} %get-tuple-element.119.items, f32[14,32,128]{2,1,0:T(8,128)S(1)} %get-tuple-element.125.low0, f32[14,32,128]{2,1,0:T(8,128)S(1)} %collective-permute-done.41.low1, ...), custom_call_target="tpu_custom_call" | custom-call | flops 1200000000 | bytes 4000000 | tf_op jit(solution)/shard_map/leaf_low/pallas_call | solution.py:720
  (155 shorter events, 66.3 us)
Async XLA Ops:
  14.2 6.8 %collective-permute-start.4 = (f32[24,128,128]{2,1,0:T(8,128)S(1)}, f32[24,128,128]{2,1,0:T(8,128)S(1)}, u32[]{:S(2)}, u32[]{:S(2)}) collective-permute-start(f32[24,128,128]{2,1,0:T(8,128)S(1)} %get-tuple-element.74), channel_id=1, source_target_pairs={{0,4},{4,0},{8,12},{12,8},{16,20},{20,16},{24,28},{28,24},{32,36},... | collective-permute-start | bytes 4718600 | tf_op jit(solution)/shard_map/ppermute | solution.py:742
  14.6 16.5 %collective-permute-start.5 = (f32[6,128,128]{2,1,0:T(8,128)S(1)}, f32[6,128,128]{2,1,0:T(8,128)S(1)}, u32[]{:S(2)}, u32[]{:S(2)}) collective-permute-start(f32[6,128,128]{2,1,0:T(8,128)S(1)} %get-tuple-element.77.refs_2_.refs_3_), channel_id=1, source_target_pairs={{0,8},{4,12},{8,0},{12,4},{16,24},{20,28},{24,16},{28,20},{32,40},... | collective-permute-start | bytes 1179656 | tf_op jit(solution)/shard_map/ppermute | solution.py:742
  16.0 10.0 %collective-permute-start.1 = (f32[10,32,128]{2,1,0:T(8,128)S(1)}, f32[10,32,128]{2,1,0:T(8,128)S(1)}, u32[]{:S(2)}, u32[]{:S(2)}) collective-permute-start(f32[10,32,128]{2,1,0:T(8,128)S(1)} %get-tuple-element.70), channel_id=1, source_target_pairs={{0,1},{1,0},{2,3},{3,2},{4,5},{5,4},{6,7},{7,6},{8,9},{9,8},{10,11... | collective-permute-start | bytes 491528 | tf_op jit(solution)/shard_map/ppermute | solution.py:746
  17.6 10.7 %collective-permute-start.2 = (f32[10,32,128]{2,1,0:T(8,128)S(1)}, f32[10,32,128]{2,1,0:T(8,128)S(1)}, u32[]{:S(2)}, u32[]{:S(2)}) collective-permute-start(f32[10,32,128]{2,1,0:T(8,128)S(1)} %get-tuple-element.71), channel_id=1, source_target_pairs={{0,2},{1,3},{2,0},{3,1},{4,6},{5,7},{6,4},{7,5},{8,10},{9,11},{10,... | collective-permute-start | bytes 491528 | tf_op jit(solution)/shard_map/ppermute | solution.py:746
  20.9 10.1 %collective-permute-start.3 = (f32[10,32,128]{2,1,0:T(8,128)S(1)}, f32[10,32,128]{2,1,0:T(8,128)S(1)}, u32[]{:S(2)}, u32[]{:S(2)}) collective-permute-start(f32[10,32,128]{2,1,0:T(8,128)S(1)} %get-tuple-element.72), channel_id=1, source_target_pairs={{0,3},{1,2},{2,1},{3,0},{4,7},{5,6},{6,5},{7,4},{8,11},{9,10},{10,... | collective-permute-start | bytes 491528 | tf_op jit(solution)/shard_map/ppermute | solution.py:746
  21.0 13.1 %collective-permute-start.7 = (f32[6,128,128]{2,1,0:T(8,128)S(1)}, f32[6,128,128]{2,1,0:T(8,128)S(1)}, u32[]{:S(2)}, u32[]{:S(2)}) collective-permute-start(f32[6,128,128]{2,1,0:T(8,128)S(1)} %get-tuple-element.77.refs_2_.refs_3_), channel_id=1, source_target_pairs={{0,4},{4,0},{8,12},{12,8},{16,20},{20,16},{24,28},{28,24},{32,36},... | collective-permute-start | bytes 1179656 | tf_op jit(solution)/shard_map/ppermute | solution.py:742
  31.7 6.3 %collective-permute-start.8 = (f32[6,128,128]{2,1,0:T(8,128)S(1)}, f32[6,128,128]{2,1,0:T(8,128)S(1)}, u32[]{:S(2)}, u32[]{:S(2)}) collective-permute-start(f32[6,128,128]{2,1,0:T(8,128)S(1)} %get-tuple-element.80.refs_4_.refs_5_), channel_id=1, source_target_pairs={{0,4},{4,0},{8,12},{12,8},{16,20},{20,16},{24,28},{28,24},{32,36},... | collective-permute-start | bytes 1179656 | tf_op jit(solution)/shard_map/ppermute | solution.py:742
  33.1 8.8 %collective-permute-start.10 = (f32[8,32,128]{2,1,0:T(8,128)S(1)}, f32[8,32,128]{2,1,0:T(8,128)S(1)}, u32[]{:S(2)}, u32[]{:S(2)}) collective-permute-start(f32[8,32,128]{2,1,0:T(8,128)S(1)} %get-tuple-element.83), channel_id=1, source_target_pairs={{0,1},{1,0},{2,3},{3,2},{4,5},{5,4},{6,7},{7,6},{8,9},{9,8},{10,11... | collective-permute-start | bytes 393224 | tf_op jit(solution)/shard_map/ppermute | solution.py:746
  33.1 9.8 %collective-permute-start.11 = (f32[8,32,128]{2,1,0:T(8,128)S(1)}, f32[8,32,128]{2,1,0:T(8,128)S(1)}, u32[]{:S(2)}, u32[]{:S(2)}) collective-permute-start(f32[8,32,128]{2,1,0:T(8,128)S(1)} %get-tuple-element.84), channel_id=1, source_target_pairs={{0,2},{1,3},{2,0},{3,1},{4,6},{5,7},{6,4},{7,5},{8,10},{9,11},{10,... | collective-permute-start | bytes 393224 | tf_op jit(solution)/shard_map/ppermute | solution.py:746
  34.0 11.8 %collective-permute-start.12 = (f32[8,32,128]{2,1,0:T(8,128)S(1)}, f32[8,32,128]{2,1,0:T(8,128)S(1)}, u32[]{:S(2)}, u32[]{:S(2)}) collective-permute-start(f32[8,32,128]{2,1,0:T(8,128)S(1)} %get-tuple-element.85), channel_id=1, source_target_pairs={{0,3},{1,2},{2,1},{3,0},{4,7},{5,6},{6,5},{7,4},{8,11},{9,10},{10,... | collective-permute-start | bytes 393224 | tf_op jit(solution)/shard_map/ppermute | solution.py:746
  39.9 6.4 %collective-permute-start.9 = (f32[9,32,128]{2,1,0:T(8,128)S(1)}, f32[9,32,128]{2,1,0:T(8,128)S(1)}, u32[]{:S(2)}, u32[]{:S(2)}) collective-permute-start(f32[9,32,128]{2,1,0:T(8,128)S(1)} %get-tuple-element.82), channel_id=1, source_target_pairs={{0,24},{4,28},{8,16},{12,20},{16,8},{20,12},{24,0},{28,4},{32,56},... | collective-permute-start | bytes 442376 | tf_op jit(solution)/shard_map/ppermute | solution.py:742
  41.9 10.3 %collective-permute-start.18 = (f32[16,32,128]{2,1,0:T(8,128)S(1)}, f32[16,32,128]{2,1,0:T(8,128)S(1)}, u32[]{:S(2)}, u32[]{:S(2)}) collective-permute-start(f32[16,32,128]{2,1,0:T(8,128)S(1)} %get-tuple-element.95), channel_id=1, source_target_pairs={{0,1},{1,0},{2,3},{3,2},{4,5},{5,4},{6,7},{7,6},{8,9},{9,8},{10,11... | collective-permute-start | bytes 786440 | tf_op jit(solution)/shard_map/ppermute | solution.py:746
  41.9 12.2 %collective-permute-start.19 = (f32[16,32,128]{2,1,0:T(8,128)S(1)}, f32[16,32,128]{2,1,0:T(8,128)S(1)}, u32[]{:S(2)}, u32[]{:S(2)}) collective-permute-start(f32[16,32,128]{2,1,0:T(8,128)S(1)} %get-tuple-element.96), channel_id=1, source_target_pairs={{0,2},{1,3},{2,0},{3,1},{4,6},{5,7},{6,4},{7,5},{8,10},{9,11},{10,... | collective-permute-start | bytes 786440 | tf_op jit(solution)/shard_map/ppermute | solution.py:746
  43.0 13.6 %collective-permute-start.20 = (f32[16,32,128]{2,1,0:T(8,128)S(1)}, f32[16,32,128]{2,1,0:T(8,128)S(1)}, u32[]{:S(2)}, u32[]{:S(2)}) collective-permute-start(f32[16,32,128]{2,1,0:T(8,128)S(1)} %get-tuple-element.97), channel_id=1, source_target_pairs={{0,3},{1,2},{2,1},{3,0},{4,7},{5,6},{6,5},{7,4},{8,11},{9,10},{10,... | collective-permute-start | bytes 786440 | tf_op jit(solution)/shard_map/ppermute | solution.py:746
  48.8 9.4 %collective-permute-start.17 = (f32[8,32,128]{2,1,0:T(8,128)S(1)}, f32[8,32,128]{2,1,0:T(8,128)S(1)}, u32[]{:S(2)}, u32[]{:S(2)}) collective-permute-start(f32[8,32,128]{2,1,0:T(8,128)S(1)} %get-tuple-element.93), channel_id=1, source_target_pairs={{0,32},{4,36},{8,40},{12,44},{16,48},{20,52},{24,56},{28,60},{32,0... | collective-permute-start | bytes 393224 | tf_op jit(solution)/shard_map/ppermute | solution.py:742
  58.8 7.1 %collective-permute-start.21 = (f32[16,32,128]{2,1,0:T(8,128)S(1)}, f32[16,32,128]{2,1,0:T(8,128)S(1)}, u32[]{:S(2)}, u32[]{:S(2)}) collective-permute-start(f32[16,32,128]{2,1,0:T(8,128)S(1)} %get-tuple-element.98.refs_0_), channel_id=1, source_target_pairs={{0,4},{4,0},{8,12},{12,8},{16,20},{20,16},{24,28},{28,24},{32,36},... | collective-permute-start | bytes 786440 | tf_op jit(solution)/shard_map/ppermute | solution.py:742
  63.6 11.8 %collective-permute-start.22 = (f32[16,32,128]{2,1,0:T(8,128)S(1)}, f32[16,32,128]{2,1,0:T(8,128)S(1)}, u32[]{:S(2)}, u32[]{:S(2)}) collective-permute-start(f32[16,32,128]{2,1,0:T(8,128)S(1)} %get-tuple-element.98.refs_0_), channel_id=1, source_target_pairs={{0,96},{4,100},{8,104},{12,108},{16,112},{20,116},{24,120},{28,124... | collective-permute-start | bytes 786440 | tf_op jit(solution)/shard_map/ppermute | solution.py:742
  68.5 25.5 %all-to-all-start = ((f32[16,2,32,128]{3,2,1,0:T(8,128)}), f32[16,2,32,128]{3,2,1,0:T(8,128)S(1)}, u32[]{:S(2)}, u32[]{:S(2)}) async-start(f32[16,2,32,128]{3,2,1,0:T(8,128)} %get-tuple-element.102), calls=%async_computation | async-start | bytes 1048576 | tf_op jit(solution)/shard_map/all_to_all | solution.py:751
  72.9 11.3 %collective-permute-start.24 = (f32[8,32,128]{2,1,0:T(8,128)S(1)}, f32[8,32,128]{2,1,0:T(8,128)S(1)}, u32[]{:S(2)}, u32[]{:S(2)}) collective-permute-start(f32[8,32,128]{2,1,0:T(8,128)S(1)} %get-tuple-element.93), channel_id=1, source_target_pairs={{0,96},{4,100},{8,104},{12,108},{16,112},{20,116},{24,120},{28,124... | collective-permute-start | bytes 393224 | tf_op jit(solution)/shard_map/ppermute | solution.py:742
  75.4 13.8 %collective-permute-start.23 = (f32[16,32,128]{2,1,0:T(8,128)S(1)}, f32[16,32,128]{2,1,0:T(8,128)S(1)}, u32[]{:S(2)}, u32[]{:S(2)}) collective-permute-start(f32[16,32,128]{2,1,0:T(8,128)S(1)} %collective-permute-done.22.refs_0_), channel_id=1, source_target_pairs={{0,4},{4,0},{8,12},{12,8},{16,20},{20,16},{24,28},{28,24},{32,36},... | collective-permute-start | bytes 786440 | tf_op jit(solution)/shard_map/ppermute | solution.py:742
  103.0 14.5 %all-to-all-start.1 = ((f32[16,2,32,128]{3,2,1,0:T(8,128)}), f32[16,2,32,128]{3,2,1,0:T(8,128)S(1)}, u32[]{:S(2)}, u32[]{:S(2)}) async-start(f32[16,2,32,128]{3,2,1,0:T(8,128)} %level4_operand.1), calls=%async_computation.1 | async-start | bytes 1048576 | tf_op jit(solution)/shard_map/all_to_all | solution.py:751
  127.5 20.9 %all-to-all-start.2 = ((f32[16,4,32,128]{3,2,1,0:T(8,128)}), f32[16,4,32,128]{3,2,1,0:T(8,128)}, u32[]{:S(2)}, u32[]{:S(2)}) async-start(f32[16,4,32,128]{3,2,1,0:T(8,128)} %copy-done.2), calls=%async_computation.2 | async-start | bytes 2097152 | tf_op jit(solution)/shard_map/all_to_all | solution.py:751
  131.9 21.1 %collective-permute-start.35 = (f32[16,32,128]{2,1,0:T(8,128)}, f32[16,32,128]{2,1,0:T(8,128)}, u32[]{:S(2)}, u32[]{:S(2)}) collective-permute-start(f32[16,32,128]{2,1,0:T(8,128)} %copy-done.12), channel_id=1, source_target_pairs={{0,3},{1,2},{2,1},{3,0},{4,7},{5,6},{6,5},{7,4},{8,11},{9,10},{10,... | collective-permute-start | bytes 786440 | tf_op jit(solution)/shard_map/ppermute | solution.py:746
  132.5 20.5 %collective-permute-start.34 = (f32[16,32,128]{2,1,0:T(8,128)}, f32[16,32,128]{2,1,0:T(8,128)}, u32[]{:S(2)}, u32[]{:S(2)}) collective-permute-start(f32[16,32,128]{2,1,0:T(8,128)} %copy-done.12), channel_id=1, source_target_pairs={{0,2},{1,3},{2,0},{3,1},{4,6},{5,7},{6,4},{7,5},{8,10},{9,11},{10,... | collective-permute-start | bytes 786440 | tf_op jit(solution)/shard_map/ppermute | solution.py:746
  132.5 20.5 %collective-permute-start.33 = (f32[16,32,128]{2,1,0:T(8,128)}, f32[16,32,128]{2,1,0:T(8,128)}, u32[]{:S(2)}, u32[]{:S(2)}) collective-permute-start(f32[16,32,128]{2,1,0:T(8,128)} %copy-done.12), channel_id=1, source_target_pairs={{0,1},{1,0},{2,3},{3,2},{4,5},{5,4},{6,7},{7,6},{8,9},{9,8},{10,11... | collective-permute-start | bytes 786440 | tf_op jit(solution)/shard_map/ppermute | solution.py:746
  154.7 19.3 %collective-permute-start.36 = (f32[4,16,32,128]{3,2,1,0:T(8,128)S(1)}, f32[4,16,32,128]{3,2,1,0:T(8,128)S(1)}, u32[]{:S(2)}, u32[]{:S(2)}) collective-permute-start(f32[4,16,32,128]{3,2,1,0:T(8,128)S(1)} %pack.3.x5m), channel_id=1, source_target_pairs={{0,4},{4,0},{8,12},{12,8},{16,20},{20,16},{24,28},{28,24},{32,36},... | collective-permute-start | bytes 3145736 | tf_op jit(solution)/shard_map/ppermute | solution.py:742
  155.8 9.0 %collective-permute-start.31 = (f32[8,32,128]{2,1,0:T(8,128)S(1)}, f32[8,32,128]{2,1,0:T(8,128)S(1)}, u32[]{:S(2)}, u32[]{:S(2)}) collective-permute-start(f32[8,32,128]{2,1,0:T(8,128)S(1)} %get-tuple-element.117.refs_0_), channel_id=1, source_target_pairs={{0,3},{1,2},{2,1},{3,0},{4,7},{5,6},{6,5},{7,4},{8,11},{9,10},{10,... | collective-permute-start | bytes 393224 | tf_op jit(solution)/shard_map/ppermute | solution.py:746
  156.4 8.4 %collective-permute-start.30 = (f32[8,32,128]{2,1,0:T(8,128)S(1)}, f32[8,32,128]{2,1,0:T(8,128)S(1)}, u32[]{:S(2)}, u32[]{:S(2)}) collective-permute-start(f32[8,32,128]{2,1,0:T(8,128)S(1)} %get-tuple-element.117.refs_0_), channel_id=1, source_target_pairs={{0,2},{1,3},{2,0},{3,1},{4,6},{5,7},{6,4},{7,5},{8,10},{9,11},{10,... | collective-permute-start | bytes 393224 | tf_op jit(solution)/shard_map/ppermute | solution.py:746
  156.4 8.7 %collective-permute-start.29 = (f32[8,32,128]{2,1,0:T(8,128)S(1)}, f32[8,32,128]{2,1,0:T(8,128)S(1)}, u32[]{:S(2)}, u32[]{:S(2)}) collective-permute-start(f32[8,32,128]{2,1,0:T(8,128)S(1)} %get-tuple-element.117.refs_0_), channel_id=1, source_target_pairs={{0,1},{1,0},{2,3},{3,2},{4,5},{5,4},{6,7},{7,6},{8,9},{9,8},{10,11... | collective-permute-start | bytes 393224 | tf_op jit(solution)/shard_map/ppermute | solution.py:746
  170.6 13.0 %collective-permute-start.43 = (f32[14,32,128]{2,1,0:T(8,128)S(1)}, f32[14,32,128]{2,1,0:T(8,128)S(1)}, u32[]{:S(2)}, u32[]{:S(2)}) collective-permute-start(f32[14,32,128]{2,1,0:T(8,128)S(1)} %get-tuple-element.125.low0), channel_id=1, source_target_pairs={{0,3},{1,2},{2,1},{3,0},{4,7},{5,6},{6,5},{7,4},{8,11},{9,10},{10,... | collective-permute-start | bytes 688136 | tf_op jit(solution)/shard_map/ppermute | solution.py:746
  171.2 12.4 %collective-permute-start.42 = (f32[14,32,128]{2,1,0:T(8,128)S(1)}, f32[14,32,128]{2,1,0:T(8,128)S(1)}, u32[]{:S(2)}, u32[]{:S(2)}) collective-permute-start(f32[14,32,128]{2,1,0:T(8,128)S(1)} %get-tuple-element.125.low0), channel_id=1, source_target_pairs={{0,2},{1,3},{2,0},{3,1},{4,6},{5,7},{6,4},{7,5},{8,10},{9,11},{10,... | collective-permute-start | bytes 688136 | tf_op jit(solution)/shard_map/ppermute | solution.py:746
  171.2 12.7 %collective-permute-start.41 = (f32[14,32,128]{2,1,0:T(8,128)S(1)}, f32[14,32,128]{2,1,0:T(8,128)S(1)}, u32[]{:S(2)}, u32[]{:S(2)}) collective-permute-start(f32[14,32,128]{2,1,0:T(8,128)S(1)} %get-tuple-element.125.low0), channel_id=1, source_target_pairs={{0,1},{1,0},{2,3},{3,2},{4,5},{5,4},{6,7},{7,6},{8,9},{9,8},{10,11... | collective-permute-start | bytes 688136 | tf_op jit(solution)/shard_map/ppermute | solution.py:746
  (43 other events, 345.4 us)
